TPU v7x, 32 devices: a whole 2x2x4 slice. The times are simulated.
32 devices in a mesh: dp: 4 (over y, x), fsdp: 8 (over z, core).
Axes of the slice: x: 2, y: 2, z: 4, core: 2. Of those that a mesh axis runs over, the one named last changes fastest.
Arguments:
- states: float32 [32768, 256], P(('dp', 'fsdp')), may hold values from -6 to 6
- inject: float32 [32768, 256], P(('dp', 'fsdp')), may hold values from -4 to 4
- ln1_gain: bfloat16 [256], P('fsdp'), may hold values from 0.099609375 to 1.8984375
- w_qkv: bfloat16 [256, 768], P('fsdp'), may hold values from -0.375 to 0.375
- w_out: bfloat16 [256, 256], P('fsdp'), may hold values from -1.5 to 1.5
- ln2_gain: bfloat16 [256], P('fsdp'), may hold values from 0.099609375 to 1.8984375
- w_up: bfloat16 [256, 1024], P('fsdp'), may hold values from -0.375 to 0.375
- w_down: bfloat16 [1024, 256], P('fsdp'), may hold values from -0.1875 to 0.1875
- prompt_lengths: int32 [32, 16], P(('dp', 'fsdp')), may hold values from 1 to 101, 1024 in all within a row
- loop_counts: int32 [32, 16], P(('dp', 'fsdp')), may hold values from 12 to 30
- cotangent: float32 [32768, 256], P(('dp', 'fsdp')), may hold values from -6 to 6
Outputs:
- final_states: float32 [32768, 256], P(('dp', 'fsdp'))
- states_grad: float32 [32768, 256], P(('dp', 'fsdp'))
- inject_grad: float32 [32768, 256], P(('dp', 'fsdp'))
- ln1_gain_grad: float32 [256], P('fsdp')
- w_qkv_grad: float32 [256, 768], P('fsdp')
- w_out_grad: float32 [256, 256], P('fsdp')
- ln2_gain_grad: float32 [256], P('fsdp')
- w_up_grad: float32 [256, 1024], P('fsdp')
- w_down_grad: float32 [1024, 256], P('fsdp')
Inputs may be any that keep to these rules, and one draw needn't show every extreme that they name: `prompt_lengths`: each row sums to 1024; its longest prompt has exactly 101 tokens.
All inputs are finite; a program needn't handle non-finite values.
Results may differ from a plain program's by a relative error of at most 0.02.
Values may be sent and summed in bfloat16 or wider, within the bound.
No kernel may reach another device: no remote copies, remote signals or barrier semaphores. Data moves between devices by JAX's collectives and lax.ppermute only.
A program may use at most 128 MiB of HBM per device.

v0:
```python
import jax
import jax.numpy as jnp
from jax import lax
from jax.sharding import PartitionSpec as P

HEADS = 8
ITERS = 2


def norm_rows(values, gain_row):
    center = values - jnp.mean(values, axis=-1, keepdims=True)
    spread = jnp.mean(center * center, axis=-1, keepdims=True)
    return center * lax.rsqrt(spread + 1e-05) * gain_row


def gelu_tanh(values):
    return (
        0.5
        * values
        * (1.0 + jnp.tanh(0.7978845608028654 * (values + 0.044715 * values * values * values)))
    )


def dot_rows(left, right):
    return jnp.dot(left, right, preferred_element_type=jnp.float32)


def dot_left(left, right):
    return lax.dot_general(
        left, right, (((0,), (0,)), ((), ())), preferred_element_type=jnp.float32
    )


def dot_right(left, right):
    return lax.dot_general(
        left, right, (((1,), (1,)), ((), ())), preferred_element_type=jnp.float32
    )


def split_packed(packed, head_count):
    token_count = packed.shape[0]
    model_width = packed.shape[1] // 3
    head_dim = model_width // head_count
    query_all = packed[:, :model_width].reshape(token_count, head_count, head_dim)
    key_all = packed[:, model_width : 2 * model_width].reshape(token_count, head_count, head_dim)
    value_all = packed[:, 2 * model_width :].reshape(token_count, head_count, head_dim)
    return (query_all, key_all, value_all)


def block_scores(query_all, key_all, segment, offset, row_block):
    token_count = key_all.shape[0]
    scaling = key_all.shape[2] ** (-0.5)
    query_rows = lax.dynamic_slice_in_dim(query_all, offset, row_block, 0)
    row_segment = lax.dynamic_slice_in_dim(segment, offset, row_block, 0)
    row_position = offset + jnp.arange(row_block, dtype=jnp.int32)
    position = jnp.arange(token_count, dtype=jnp.int32)
    allowed = (row_segment[:, None] == segment[None, :]) & (
        position[None, :] <= row_position[:, None]
    )
    scores = (
        jnp.einsum("rhd,thd->hrt", query_rows, key_all, preferred_element_type=jnp.float32)
        * scaling
    )
    return (query_rows, jnp.where(allowed[None], scores, -1e30))


def attention_forward(packed, segment, head_count):
    token_count = packed.shape[0]
    model_width = packed.shape[1] // 3
    row_block = min(512, token_count)
    query_all, key_all, value_all = split_packed(packed, head_count)
    offsets = jnp.arange(token_count // row_block, dtype=jnp.int32) * row_block

    def one_block(offset):
        query_rows, scores = block_scores(query_all, key_all, segment, offset, row_block)
        row_max = jnp.max(scores, axis=-1, keepdims=True)
        summed = jnp.sum(jnp.exp(scores - row_max), axis=-1, keepdims=True)
        logsum = row_max + jnp.log(summed)
        attn_probs = jnp.exp(scores - logsum).astype(jnp.bfloat16)
        output = jnp.einsum(
            "hrt,thd->rhd", attn_probs, value_all, preferred_element_type=jnp.float32
        )
        return (output.reshape(row_block, model_width), logsum[..., 0])

    outputs, logsums = lax.map(one_block, offsets)
    return (outputs.reshape(token_count, model_width), logsums)


def attention_backward(packed, segment, head_count, logsums, grad_heads):
    token_count = packed.shape[0]
    model_width = packed.shape[1] // 3
    row_block = min(512, token_count)
    scaling = (model_width // head_count) ** (-0.5)
    query_all, key_all, value_all = split_packed(packed, head_count)
    grad_all = grad_heads.reshape(query_all.shape)
    offsets = jnp.arange(token_count // row_block, dtype=jnp.int32) * row_block

    def one_block(state_carry, inputs):
        key_grad, value_grad = state_carry
        offset, logsum = inputs
        query_rows, scores = block_scores(query_all, key_all, segment, offset, row_block)
        grad_rows = lax.dynamic_slice_in_dim(grad_all, offset, row_block, 0)
        attn_probs = jnp.exp(scores - logsum[..., None])
        probs_low = attn_probs.astype(jnp.bfloat16)
        value_grad = value_grad + jnp.einsum(
            "hrt,rhd->thd", probs_low, grad_rows, preferred_element_type=jnp.float32
        )
        prob_grad = jnp.einsum(
            "rhd,thd->hrt", grad_rows, value_all, preferred_element_type=jnp.float32
        )
        score_grad = attn_probs * (
            prob_grad - jnp.sum(attn_probs * prob_grad, axis=-1, keepdims=True)
        )
        score_low = score_grad.astype(jnp.bfloat16)
        query_grad = (
            jnp.einsum("hrt,thd->rhd", score_low, key_all, preferred_element_type=jnp.float32)
            * scaling
        )
        key_grad = (
            key_grad
            + jnp.einsum("hrt,rhd->thd", score_low, query_rows, preferred_element_type=jnp.float32)
            * scaling
        )
        return ((key_grad, value_grad), query_grad.reshape(row_block, model_width))

    zero_grads = jnp.zeros(query_all.shape, jnp.float32)
    (key_grad, value_grad), query_grads = lax.scan(
        one_block, (zero_grads, zero_grads), (offsets, logsums)
    )
    return jnp.concatenate(
        [
            query_grads.reshape(token_count, model_width),
            key_grad.reshape(token_count, model_width),
            value_grad.reshape(token_count, model_width),
        ],
        axis=1,
    )


def on_device(
    states,
    inject,
    ln1_gain,
    w_qkv,
    w_out,
    ln2_gain,
    w_up,
    w_down,
    prompt_lengths,
    loop_counts,
    cotangent,
):
    gain_one, weight_qkv, weight_out, gain_two, weight_up, weight_down = (
        lax.all_gather(ln1_gain, "fsdp", axis=0, tiled=True),
        lax.all_gather(w_qkv, "fsdp", axis=0, tiled=True),
        lax.all_gather(w_out, "fsdp", axis=0, tiled=True),
        lax.all_gather(ln2_gain, "fsdp", axis=0, tiled=True),
        lax.all_gather(w_up, "fsdp", axis=0, tiled=True),
        lax.all_gather(w_down, "fsdp", axis=0, tiled=True),
    )
    gain_first = gain_one.astype(jnp.float32)
    gain_second = gain_two.astype(jnp.float32)
    token_count = states.shape[0]
    prompt_ends = jnp.cumsum(prompt_lengths[0])
    position = jnp.arange(token_count, dtype=jnp.int32)
    segment = jnp.sum((position[:, None] >= prompt_ends[None, :]).astype(jnp.int32), axis=1)
    prompt_ids = jnp.arange(prompt_ends.shape[0], dtype=jnp.int32)
    member_mask = (segment[:, None] == prompt_ids[None, :]).astype(jnp.float32)
    rates = 12.0 / loop_counts[0].astype(jnp.float32)
    row_weight = jnp.sum(member_mask * rates[None, :], axis=1)
    state = states
    stored = []
    for repeat in range(ITERS):
        entered = state + inject
        normed_one = norm_rows(entered, gain_first).astype(jnp.bfloat16)
        packed = dot_rows(normed_one, weight_qkv).astype(jnp.bfloat16)
        heads_out, logsums = attention_forward(packed, segment, HEADS)
        heads_low = heads_out.astype(jnp.bfloat16)
        middle = entered + dot_rows(heads_low, weight_out)
        normed_two = norm_rows(middle, gain_second).astype(jnp.bfloat16)
        hidden = dot_rows(normed_two, weight_up)
        active = gelu_tanh(hidden).astype(jnp.bfloat16)
        state = middle + dot_rows(active, weight_down)
        stored.append(
            (entered, normed_one, packed, logsums, heads_low, middle, normed_two, hidden, active)
        )
    grad_state = cotangent * row_weight[:, None]
    grad_inject = jnp.zeros_like(inject)
    grad_gain_one = jnp.zeros(gain_first.shape, jnp.float32)
    grad_gain_two = jnp.zeros(gain_second.shape, jnp.float32)
    grad_qkv = jnp.zeros(weight_qkv.shape, jnp.float32)
    grad_attn_out = jnp.zeros(weight_out.shape, jnp.float32)
    grad_up_proj = jnp.zeros(weight_up.shape, jnp.float32)
    grad_down_proj = jnp.zeros(weight_down.shape, jnp.float32)
    for repeat in reversed(range(ITERS)):
        entered, normed_one, packed, logsums, heads_low, middle, normed_two, hidden, active = (
            stored[repeat]
        )
        grad_low = grad_state.astype(jnp.bfloat16)
        grad_down_proj = grad_down_proj + dot_left(active, grad_low)
        grad_active = dot_right(grad_low, weight_down)
        unused_gelu, gelu_pull = jax.vjp(gelu_tanh, hidden)
        grad_hidden = gelu_pull(grad_active)[0].astype(jnp.bfloat16)
        grad_up_proj = grad_up_proj + dot_left(normed_two, grad_hidden)
        grad_normed = dot_right(grad_hidden, weight_up)
        unused_norm, norm_pull = jax.vjp(norm_rows, middle, gain_second)
        grad_middle, grad_gain = norm_pull(grad_normed)
        grad_gain_two = grad_gain_two + grad_gain
        grad_state = grad_state + grad_middle
        grad_low = grad_state.astype(jnp.bfloat16)
        grad_attn_out = grad_attn_out + dot_left(heads_low, grad_low)
        grad_heads = dot_right(grad_low, weight_out).astype(jnp.bfloat16)
        grad_packed = attention_backward(packed, segment, HEADS, logsums, grad_heads).astype(
            jnp.bfloat16
        )
        grad_qkv = grad_qkv + dot_left(normed_one, grad_packed)
        grad_normed = dot_right(grad_packed, weight_qkv)
        unused_norm, norm_pull = jax.vjp(norm_rows, entered, gain_first)
        grad_entered, grad_gain = norm_pull(grad_normed)
        grad_gain_one = grad_gain_one + grad_gain
        grad_state = grad_state + grad_entered
        grad_inject = grad_inject + grad_state
    partials = (grad_gain_one, grad_qkv, grad_attn_out, grad_gain_two, grad_up_proj, grad_down_proj)
    shares = (
        lax.psum_scatter(
            partials[0].astype(jnp.bfloat16), "fsdp", scatter_dimension=0, tiled=True
        ).astype(jnp.float32),
        lax.psum_scatter(
            partials[1].astype(jnp.bfloat16), "fsdp", scatter_dimension=0, tiled=True
        ).astype(jnp.float32),
        lax.psum_scatter(
            partials[2].astype(jnp.bfloat16), "fsdp", scatter_dimension=0, tiled=True
        ).astype(jnp.float32),
        lax.psum_scatter(
            partials[3].astype(jnp.bfloat16), "fsdp", scatter_dimension=0, tiled=True
        ).astype(jnp.float32),
        lax.psum_scatter(
            partials[4].astype(jnp.bfloat16), "fsdp", scatter_dimension=0, tiled=True
        ).astype(jnp.float32),
        lax.psum_scatter(
            partials[5].astype(jnp.bfloat16), "fsdp", scatter_dimension=0, tiled=True
        ).astype(jnp.float32),
    )
    totals = (
        lax.psum(shares[0].astype(jnp.bfloat16), "dp").astype(jnp.float32),
        lax.psum(shares[1].astype(jnp.bfloat16), "dp").astype(jnp.float32),
        lax.psum(shares[2].astype(jnp.bfloat16), "dp").astype(jnp.float32),
        lax.psum(shares[3].astype(jnp.bfloat16), "dp").astype(jnp.float32),
        lax.psum(shares[4].astype(jnp.bfloat16), "dp").astype(jnp.float32),
        lax.psum(shares[5].astype(jnp.bfloat16), "dp").astype(jnp.float32),
    )
    return (
        state,
        grad_state,
        grad_inject,
        totals[0],
        totals[1],
        totals[2],
        totals[3],
        totals[4],
        totals[5],
    )


def solution(mesh):
    return jax.shard_map(
        on_device,
        mesh=mesh,
        in_specs=(
            P(("dp", "fsdp"), None),
            P(("dp", "fsdp"), None),
            P("fsdp"),
            P("fsdp", None),
            P("fsdp", None),
            P("fsdp"),
            P("fsdp", None),
            P("fsdp", None),
            P(("dp", "fsdp"), None),
            P(("dp", "fsdp"), None),
            P(("dp", "fsdp"), None),
        ),
        out_specs=(
            P(("dp", "fsdp"), None),
            P(("dp", "fsdp"), None),
            P(("dp", "fsdp"), None),
            P("fsdp"),
            P("fsdp", None),
            P("fsdp", None),
            P("fsdp"),
            P("fsdp", None),
            P("fsdp", None),
        ),
        check_vma=False,
    )
```

profile of v0, /device:TPU:0, one launch (start us, length us, event | category | flops | bytes accessed | tf_op | source)
XLA Modules:
  0.0 605.8 jit_solution(5549381173510764974)
XLA Ops:
  12.2 18.1 %all-reduce.5 = (bf16[256]{0:T(256)(128)(2,1)S(1)}, bf16[256]{0:T(256)(128)(2,1)S(1)}) all-reduce(bf16[256]{0:T(256)(128)(2,1)S(1)} %dynamic-update-slice, bf16[256]{0:T(256)(128)(2,1)S(1)} %dynamic-update-slice.1), channel_id=1, replica_groups=mesh['dp'=4,'fsdp'=8] {'fsdp'}, use_global_device_ids=true, to_apply=%add | all-reduce | flops 512 | bytes 2048
  31.2 15.3 %all_gather.20 = bf16[256,256]{1,0:T(8,128)(2,1)} all-gather(bf16[32,256]{1,0:T(8,128)(2,1)} %param.23), channel_id=1, replica_groups=mesh['dp'=4,'fsdp'=8] {'fsdp'}, dimensions={0}, use_global_device_ids=true | all-gather | bytes 147456 | tf_op jit(solution)/shard_map/all_gather | solution.py:156
  46.5 14.7 %all_gather.19 = bf16[256,768]{1,0:T(8,128)(2,1)S(1)} all-gather(bf16[32,768]{1,0:T(8,128)(2,1)} %param.22), channel_id=1, replica_groups=mesh['dp'=4,'fsdp'=8] {'fsdp'}, dimensions={0}, use_global_device_ids=true | all-gather | bytes 442368 | tf_op jit(solution)/shard_map/all_gather | solution.py:155
  61.2 16.0 %all_gather.22 = bf16[256,1024]{1,0:T(8,128)(2,1)} all-gather(bf16[32,1024]{1,0:T(8,128)(2,1)} %param.25), channel_id=1, replica_groups=mesh['dp'=4,'fsdp'=8] {'fsdp'}, dimensions={0}, use_global_device_ids=true | all-gather | bytes 589824 | tf_op jit(solution)/shard_map/all_gather | solution.py:158
  77.2 16.0 %all_gather.23 = bf16[1024,256]{1,0:T(8,128)(2,1)} all-gather(bf16[128,256]{1,0:T(8,128)(2,1)} %param.26), channel_id=1, replica_groups=mesh['dp'=4,'fsdp'=8] {'fsdp'}, dimensions={0}, use_global_device_ids=true | all-gather | bytes 589824 | tf_op jit(solution)/shard_map/all_gather | solution.py:159
  104.9 38.1 %while.54 = (s32[]{:T(128)}, bf16[2,512,256]{2,1,0:T(8,128)(2,1)}, f32[2,8,512]{2,1,0:T(8,128)}, s32[2]{0:T(128)}, s32[1024]{0:T(1024)S(1)}, /*index=5*/bf16[102...) while((s32[]{:T(128)}, bf16[2,512,256]{2,1,0:T(8,128)(2,1)}, ...), condition=%wide.region_7.8_spmd, body=%wide.region_4.0_spmd.sunk | while | flops 584577536 | bytes 55195832 | solution.py:85
  152.8 37.7 %while.55 = (s32[]{:T(128)}, bf16[2,512,256]{2,1,0:T(8,128)(2,1)S(1)}, f32[2,8,512]{2,1,0:T(8,128)S(1)}, s32[2]{0:T(128)}, s32[1024]{0:T(1024)S(1)}, /*index=5*/...) while((s32[]{:T(128)}, ...), condition=%wide.region_15.16_spmd, body=%wide.region_12.15_spmd.sunk | while | flops 584577536 | bytes 55195832 | solution.py:85
  202.0 91.7 %while.56 = (s32[]{:T(128)}, f32[1024,8,32]{0,2,1:T(8,128)}, f32[1024,8,32]{0,2,1:T(8,128)}, bf16[2,512,256]{2,1,0:T(8,128)(2,1)}, s32[2]{0:T(128)}, /*index=5*/...) while((s32[]{:T(128)}, f32[1024,8,32]{0,2,1:T(8,128)}, ...), condition=%wide.region_23.24_spmd.clone, body=%wide.region_21.23_spmd.clone.sunk | while | flops 1383068160 | bytes 183597536 | solution.py:127
  211.0 11.7 %multiply_reduce_fusion.16 = (f32[8,512]{1,0:T(8,128)}, f32[8,512,1024]{2,1,0:T(8,128)}) fusion(f32[8,512,1024]{2,1,0:T(8,128)S(1)} %fusion.204, f32[8,512]{1,0:T(8,128)} %dynamic-slice_bitcast_fusion.4, bf16[1024,8,32]{0,2,1:T(8,128)(2,1)S(1)} %get-tuple-element.833, bf16[1024,8,32]{0,2,1:T(8,128)(2,1)} %get-tuple-element.831, s32[]{:T(128)S(6)} %select_n.71, ...), kind=kOutput, calls=%fused_computation.35.clone.1 | convolution fusion | flops 289402880 | bytes 34897924 | tf_op jit(solution)/shard_map/while/body/eval_jaxpr/rhd,thd->hrt/dot_general | solution.py:61
  222.7 9.4 %multiply_convert_fusion.25 = bf16[8,512,1024]{2,1,0:T(8,128)(2,1)} fusion(f32[8,512,1024]{2,1,0:T(8,128)} %get-tuple-element.717, f32[8,512,1024]{2,1,0:T(8,128)S(1)} %fusion.204, f32[8,512]{1,0:T(8,128)} %get-tuple-element.718), kind=kLoop, calls=%fused_computation.34.clone.1 | loop fusion | flops 12582912 | bytes 41959424 | tf_op jit(solution)/shard_map/while/body/eval_jaxpr/convert_element_type | solution.py:114
  256.4 11.7 %multiply_reduce_fusion.16 = (f32[8,512]{1,0:T(8,128)}, f32[8,512,1024]{2,1,0:T(8,128)}) fusion(f32[8,512,1024]{2,1,0:T(8,128)S(1)} %fusion.204, f32[8,512]{1,0:T(8,128)} %dynamic-slice_bitcast_fusion.4, bf16[1024,8,32]{0,2,1:T(8,128)(2,1)S(1)} %get-tuple-element.833, bf16[1024,8,32]{0,2,1:T(8,128)(2,1)} %get-tuple-element.831, s32[]{:T(128)S(6)} %select_n.71, ...), kind=kOutput, calls=%fused_computation.35.clone.1 | convolution fusion | flops 289402880 | bytes 34897924 | tf_op jit(solution)/shard_map/while/body/eval_jaxpr/rhd,thd->hrt/dot_general | solution.py:61
  268.1 9.4 %multiply_convert_fusion.25 = bf16[8,512,1024]{2,1,0:T(8,128)(2,1)} fusion(f32[8,512,1024]{2,1,0:T(8,128)} %get-tuple-element.717, f32[8,512,1024]{2,1,0:T(8,128)S(1)} %fusion.204, f32[8,512]{1,0:T(8,128)} %get-tuple-element.718), kind=kLoop, calls=%fused_computation.34.clone.1 | loop fusion | flops 12582912 | bytes 41959424 | tf_op jit(solution)/shard_map/while/body/eval_jaxpr/convert_element_type | solution.py:114
  277.5 8.7 %fusion.207 = f32[1024,8,32]{0,2,1:T(8,128)} fusion(f32[8,512,1024]{2,1,0:T(8,128)} %get-tuple-element.717, f32[1024,8,32]{0,2,1:T(8,128)} %get-tuple-element.814, pred[]{:T(512)S(6)} %compare.6, bf16[1024,8,32]{0,2,1:T(8,128)(2,1)S(1)} %copy-done.21, s32[]{:T(128)S(6)} %select_n.71), kind=kOutput, calls=%fused_computation.45.clone.1 | convolution fusion | flops 273154048 | bytes 19136516 | tf_op jit(solution)/shard_map/while/body/eval_jaxpr/hrt,rhd->thd/dot_general | solution.py:105
  315.8 90.6 %while.57 = (s32[]{:T(128)}, f32[1024,8,32]{0,2,1:T(8,128)}, f32[1024,8,32]{0,2,1:T(8,128)}, bf16[2,512,256]{2,1,0:T(8,128)(2,1)}, s32[2]{0:T(128)}, /*index=5*/...) while((s32[]{:T(128)}, f32[1024,8,32]{0,2,1:T(8,128)}, ...), condition=%wide.region_30.31_spmd.clone, body=%wide.region_28.30_spmd.clone.sunk | while | flops 1383068160 | bytes 185432512 | solution.py:127
  325.4 11.7 %multiply_reduce_fusion.17 = (f32[8,512]{1,0:T(8,128)}, f32[8,512,1024]{2,1,0:T(8,128)}) fusion(f32[8,512,1024]{2,1,0:T(8,128)S(1)} %fusion.217, f32[8,512]{1,0:T(8,128)} %dynamic-slice_bitcast_fusion.5, bf16[1024,8,32]{0,2,1:T(8,128)(2,1)S(1)} %get-tuple-element.875, bf16[1024,8,32]{0,2,1:T(8,128)(2,1)} %get-tuple-element.873, s32[]{:T(128)S(6)} %select_n.72, ...), kind=kOutput, calls=%fused_computation.60.clone.1 | convolution fusion | flops 289402880 | bytes 34897924 | tf_op jit(solution)/shard_map/while/body/eval_jaxpr/rhd,thd->hrt/dot_general | solution.py:61
  337.1 9.4 %multiply_convert_fusion.26 = bf16[8,512,1024]{2,1,0:T(8,128)(2,1)} fusion(f32[8,512,1024]{2,1,0:T(8,128)} %get-tuple-element.730, f32[8,512,1024]{2,1,0:T(8,128)S(1)} %fusion.217, f32[8,512]{1,0:T(8,128)} %get-tuple-element.731), kind=kLoop, calls=%fused_computation.59.clone.1 | loop fusion | flops 12582912 | bytes 41959424 | tf_op jit(solution)/shard_map/while/body/eval_jaxpr/convert_element_type | solution.py:114
  370.6 11.7 %multiply_reduce_fusion.17 = (f32[8,512]{1,0:T(8,128)}, f32[8,512,1024]{2,1,0:T(8,128)}) fusion(f32[8,512,1024]{2,1,0:T(8,128)S(1)} %fusion.217, f32[8,512]{1,0:T(8,128)} %dynamic-slice_bitcast_fusion.5, bf16[1024,8,32]{0,2,1:T(8,128)(2,1)S(1)} %get-tuple-element.875, bf16[1024,8,32]{0,2,1:T(8,128)(2,1)} %get-tuple-element.873, s32[]{:T(128)S(6)} %select_n.72, ...), kind=kOutput, calls=%fused_computation.60.clone.1 | convolution fusion | flops 289402880 | bytes 34897924 | tf_op jit(solution)/shard_map/while/body/eval_jaxpr/rhd,thd->hrt/dot_general | solution.py:61
  382.2 9.4 %multiply_convert_fusion.26 = bf16[8,512,1024]{2,1,0:T(8,128)(2,1)} fusion(f32[8,512,1024]{2,1,0:T(8,128)} %get-tuple-element.730, f32[8,512,1024]{2,1,0:T(8,128)S(1)} %fusion.217, f32[8,512]{1,0:T(8,128)} %get-tuple-element.731), kind=kLoop, calls=%fused_computation.59.clone.1 | loop fusion | flops 12582912 | bytes 41959424 | tf_op jit(solution)/shard_map/while/body/eval_jaxpr/convert_element_type | solution.py:114
  391.6 8.7 %fusion.220 = f32[1024,8,32]{0,2,1:T(8,128)} fusion(f32[8,512,1024]{2,1,0:T(8,128)} %get-tuple-element.730, f32[1024,8,32]{0,2,1:T(8,128)} %get-tuple-element.856, pred[]{:T(512)S(6)} %compare.7, bf16[1024,8,32]{0,2,1:T(8,128)(2,1)S(1)} %copy-done.20, s32[]{:T(128)S(6)} %select_n.72), kind=kOutput, calls=%fused_computation.70.clone.1 | convolution fusion | flops 273154048 | bytes 19136516 | tf_op jit(solution)/shard_map/while/body/eval_jaxpr/hrt,rhd->thd/dot_general | solution.py:105
  431.5 14.3 %all-reduce.4 = (bf16[256]{0:T(256)(128)(2,1)S(1)}, bf16[256]{0:T(256)(128)(2,1)S(1)}) all-reduce(bf16[256]{0:T(256)(128)(2,1)S(1)} %get-tuple-element.475, bf16[256]{0:T(256)(128)(2,1)S(1)} %get-tuple-element.474), channel_id=2, replica_groups=mesh['dp'=4,'fsdp'=8] {'fsdp'}, use_global_device_ids=true, to_apply=%region_35.36.clone | all-reduce | flops 512 | bytes 2048
  452.0 22.9 %reduce-scatter.9.cloned.1.call-done = bf16[32,1024]{1,0:T(8,128)(2,1)} async-done(((bf16[256,1024]{1,0:T(8,128)(2,1)}), bf16[32,1024]{1,0:T(8,128)(2,1)}) %reduce-scatter.9.cloned.1.call-update) | async-done | bytes 65552 | tf_op jit(solution)/shard_map/reduce_scatter | solution.py:237
  474.9 31.3 %reduce-scatter.11.cloned.1.call-done = bf16[128,256]{1,0:T(8,128)(2,1)} async-done(((bf16[1024,256]{1,0:T(8,128)(2,1)}), bf16[128,256]{1,0:T(8,128)(2,1)}) %reduce-scatter.11.cloned.1.call-update) | async-done | bytes 65552 | tf_op jit(solution)/shard_map/reduce_scatter | solution.py:240
  516.0 32.9 %all-reduce.11.cloned.1.call-done = (bf16[32]{0:T(256)(128)(2,1)}, bf16[32,768]{1,0:T(8,128)(2,1)}, bf16[32,256]{1,0:T(8,128)(2,1)}, bf16[32]{0:T(256)(128)(2,1)}) async-done(((bf16[32]{0:T(256)(128)(2,1)}, bf16[32,768]{1,0:T(8,128)(2,1)}, bf16[32,256]{1,0:T(8,128)(2,1)}, bf16[32]{0:T(256)(128)(2,1)}), (bf16[32]{0:T(256)(128)(2,1)}, bf16[32,768]{1,0:T(8,128)(2,1)}, bf16[32,256]{1,0:T(8,128)(2,1)}, ...) | async-done | bytes 65680 | tf_op jit(solution)/shard_map/psum | solution.py:245
  554.0 41.7 %all-reduce.13.cloned.1.call-done = (bf16[32,1024]{1,0:T(8,128)(2,1)}, bf16[128,256]{1,0:T(8,128)(2,1)}) async-done(((bf16[32,1024]{1,0:T(8,128)(2,1)}, bf16[128,256]{1,0:T(8,128)(2,1)}), (bf16[32,1024]{1,0:T(8,128)(2,1)}, bf16[128,256]{1,0:T(8,128)(2,1)})) %all-reduce.13.cloned.1.call-update) | async-done | bytes 131088 | tf_op jit(solution)/shard_map/psum | solution.py:249
  (430 shorter events, 246.5 us)
Async XLA Ops:
  7.2 88.5 %copy-start.46 = (f32[1024,256]{1,0:T(8,128)S(1)}, f32[1024,256]{1,0:T(8,128)}, u32[]{:S(2)}) copy-start(f32[1024,256]{1,0:T(8,128)} %param.20) | copy-start | bytes 3145732
  7.2 444.7 %reduce-scatter.7.cloned.1.call-start = ((), (), s32[]{:S(2)}) async-start(), calls=%async_computation.5 | async-start | bytes 147456 | tf_op jit(solution)/shard_map/reduce_scatter | solution.py:231
  30.2 119.4 %copy-start.82 = (f32[256]{0:T(256)}, f32[256]{0:T(256)S(1)}, u32[]{:S(2)}) copy-start(f32[256]{0:T(256)S(1)} %convert_element_type.143) | copy-start | bytes 3076
  30.2 167.4 %copy-start.72 = (f32[256]{0:T(256)}, f32[256]{0:T(256)S(1)}, u32[]{:S(2)}) copy-start(f32[256]{0:T(256)S(1)} %convert_element_type.148) | copy-start | bytes 3076
  61.2 88.5 %copy-start.38 = (bf16[256,768]{1,0:T(8,128)(2,1)}, bf16[256,768]{1,0:T(8,128)(2,1)S(1)}, u32[]{:S(2)}) copy-start(bf16[256,768]{1,0:T(8,128)(2,1)S(1)} %all_gather.19) | copy-start | bytes 1179652
  100.4 42.6 %copy-start.11 = (f32[1024,256]{0,1:T(8,128)}, f32[1024,256]{0,1:T(8,128)S(1)}, u32[]{:S(2)}) copy-start(f32[1024,256]{0,1:T(8,128)S(1)} %get-tuple-element.445) | copy-start | bytes 3145732
  149.5 41.0 %copy-start.18 = (f32[1024,256]{0,1:T(8,128)}, f32[1024,256]{0,1:T(8,128)S(1)}, u32[]{:S(2)}) copy-start(f32[1024,256]{0,1:T(8,128)S(1)} %get-tuple-element.465) | copy-start | bytes 3145732
  152.8 37.7 %copy-start.41 = (bf16[256,256]{1,0:T(8,128)(2,1)S(1)}, bf16[256,256]{1,0:T(8,128)(2,1)}, u32[]{:S(2)}) copy-start(bf16[256,256]{1,0:T(8,128)(2,1)} %all_gather.20) | copy-start | bytes 393220
  222.7 9.4 %copy-start.21 = (bf16[1024,8,32]{0,2,1:T(8,128)(2,1)S(1)}, bf16[1024,8,32]{0,2,1:T(8,128)(2,1)}, u32[]{:S(2)}) copy-start(bf16[1024,8,32]{0,2,1:T(8,128)(2,1)} %get-tuple-element.835) | copy-start | bytes 1572868 | tf_op jit(solution)/shard_map/while
  232.1 8.5 %copy-start = (bf16[8,512,1024]{2,1,0:T(8,128)(2,1)S(1)}, bf16[8,512,1024]{2,1,0:T(8,128)(2,1)}, u32[]{:S(2)}) copy-start(bf16[8,512,1024]{2,1,0:T(8,128)(2,1)} %multiply_convert_fusion.25) | copy-start | bytes 25165828 | tf_op jit(solution)/shard_map/while
  268.1 9.4 %copy-start.21 = (bf16[1024,8,32]{0,2,1:T(8,128)(2,1)S(1)}, bf16[1024,8,32]{0,2,1:T(8,128)(2,1)}, u32[]{:S(2)}) copy-start(bf16[1024,8,32]{0,2,1:T(8,128)(2,1)} %get-tuple-element.835) | copy-start | bytes 1572868 | tf_op jit(solution)/shard_map/while
  277.5 8.7 %copy-start = (bf16[8,512,1024]{2,1,0:T(8,128)(2,1)S(1)}, bf16[8,512,1024]{2,1,0:T(8,128)(2,1)}, u32[]{:S(2)}) copy-start(bf16[8,512,1024]{2,1,0:T(8,128)(2,1)} %multiply_convert_fusion.25) | copy-start | bytes 25165828 | tf_op jit(solution)/shard_map/while
  311.0 140.9 %reduce-scatter.5.cloned.1.call-start = ((), (), s32[]{:S(2)}) async-start(), calls=%async_computation.4 | async-start | bytes 442368 | tf_op jit(solution)/shard_map/reduce_scatter | solution.py:228
  337.1 9.4 %copy-start.20 = (bf16[1024,8,32]{0,2,1:T(8,128)(2,1)S(1)}, bf16[1024,8,32]{0,2,1:T(8,128)(2,1)}, u32[]{:S(2)}) copy-start(bf16[1024,8,32]{0,2,1:T(8,128)(2,1)} %get-tuple-element.877) | copy-start | bytes 1572868 | tf_op jit(solution)/shard_map/while
  346.5 8.5 %copy-start.1 = (bf16[8,512,1024]{2,1,0:T(8,128)(2,1)S(1)}, bf16[8,512,1024]{2,1,0:T(8,128)(2,1)}, u32[]{:S(2)}) copy-start(bf16[8,512,1024]{2,1,0:T(8,128)(2,1)} %multiply_convert_fusion.26) | copy-start | bytes 25165828 | tf_op jit(solution)/shard_map/while
  382.2 9.4 %copy-start.20 = (bf16[1024,8,32]{0,2,1:T(8,128)(2,1)S(1)}, bf16[1024,8,32]{0,2,1:T(8,128)(2,1)}, u32[]{:S(2)}) copy-start(bf16[1024,8,32]{0,2,1:T(8,128)(2,1)} %get-tuple-element.877) | copy-start | bytes 1572868 | tf_op jit(solution)/shard_map/while
  391.6 8.8 %copy-start.1 = (bf16[8,512,1024]{2,1,0:T(8,128)(2,1)S(1)}, bf16[8,512,1024]{2,1,0:T(8,128)(2,1)}, u32[]{:S(2)}) copy-start(bf16[8,512,1024]{2,1,0:T(8,128)(2,1)} %multiply_convert_fusion.26) | copy-start | bytes 25165828 | tf_op jit(solution)/shard_map/while
  414.2 60.7 %reduce-scatter.9.cloned.1.call-start = ((), (), s32[]{:S(2)}) async-start(), calls=%async_computation.6 | async-start | bytes 589824 | tf_op jit(solution)/shard_map/reduce_scatter | solution.py:237
  419.0 87.2 %reduce-scatter.11.cloned.1.call-start = ((), (), s32[]{:S(2)}) async-start(), calls=%async_computation.7 | async-start | bytes 589824 | tf_op jit(solution)/shard_map/reduce_scatter | solution.py:240
  426.1 21.0 %copy-start.17 = (f32[1024,256]{0,1:T(8,128)S(1)}, f32[1024,256]{0,1:T(8,128)}, u32[]{:S(2)}) copy-start(f32[1024,256]{0,1:T(8,128)} %copy-done.16) | copy-start | bytes 3145732
  426.1 20.9 %copy-start.51 = (bf16[1024,256]{1,0:T(8,128)(2,1)S(1)}, bf16[1024,256]{1,0:T(8,128)(2,1)}, u32[]{:S(2)}) copy-start(bf16[1024,256]{1,0:T(8,128)(2,1)} %all_gather.23) | copy-start | bytes 1572868
  426.1 122.8 %all-reduce.11.cloned.1.call-start = ((), (), s32[]{:S(2)}) async-start(), calls=%async_computation.8 | async-start | bytes 133120 | tf_op jit(solution)/shard_map/psum | solution.py:245
  447.0 59.2 %copy-start.86 = (f32[1024]{0:T(1024)S(1)}, f32[1024]{0:T(1024)}, u32[]{:S(2)}) copy-start(f32[1024]{0:T(1024)} %copy-done.85) | copy-start | bytes 12292
  451.9 143.8 %all-reduce.13.cloned.1.call-start = ((), (), s32[]{:S(2)}) async-start(), calls=%async_computation.9 | async-start | bytes 262144 | tf_op jit(solution)/shard_map/psum | solution.py:249
  (98 other events, 328.5 us)
Sparse Core Ops, SparseCore 0:
  311.1 28.5 reduce-scatter.6
  414.3 29.1 reduce-scatter.4
  445.7 29.1 reduce-scatter.8
  477.1 29.0 reduce-scatter.10
  509.8 39.0 all-reduce.10
  551.9 43.8 all-reduce.12
where the time goes:
time: 612 us; the launch traced here: 606 us
  matrix products  200 us (33%)
  waiting for transfers between devices  129 us (21%)
  blocking collectives  94.3 us (15%)
  other arithmetic  91.4 us (15%)
  local copies, waits for them, and re-layouts  55.9 us (9%)
  loops' own time  17.5 us (3%)
  between operations  16.9 us (3%)
    dot_general x8, matrix products, block_scores(): jnp.einsum('rhd,thd->hrt', query_rows, key_all, preferred_element_type=jn...  63.8 us
    psum x1, waiting for transfers between devices, on_device(): lax.psum(shares[4].astype(jnp.bfloat16), 'dp').astype(jnp.float32)  41.7 us
    convert_element_type x4, other arithmetic, one_block(): score_low = score_grad.astype(jnp.bfloat16)  37.5 us
    dot_general x4, matrix products, one_block(): jnp.einsum('hrt,rhd->thd', probs_low, grad_rows, preferred_element_type=j...  34.5 us
    psum x1, waiting for transfers between devices, on_device(): lax.psum(shares[0].astype(jnp.bfloat16), 'dp').astype(jnp.float32)  32.9 us
    unnamed x2, blocking collectives  32.4 us
    reduce_scatter x1, waiting for transfers between devices, on_device(): lax.psum_scatter(partials[5].astype(jnp.bfloat16), 'fsdp', scatter_dimens...  31.3 us
    unnamed x185, local copies, waits for them, and re-layouts  23 us
  transfers between devices with their start and end apart: 6, of which 4 were waited for; matrix products, arithmetic and copies ran while one was open for 22% of the time, Pallas kernels for 0%

commit v1 on v0

v1 whole, which is shorter than its diff:
```python
import functools
import types

import jax
import jax.numpy as jnp
from jax import lax
from jax.experimental import pallas as pl
from jax.experimental.pallas import tpu as pltpu
from jax.sharding import PartitionSpec as P

BF = jnp.bfloat16
F32 = jnp.float32
HEADS = 8
ITERS = 2
BLK = 128
CHUNK = 256
NEG = -1e30
LOG2E = 1.4426950408889634
LN2 = 0.6931471805599453
GELU_A = 0.7978845608028654
GELU_B = GELU_A * 0.044715


def dot(a, b):
    return jnp.dot(a, b, preferred_element_type=F32)

def dot_tn(a, b):
    return lax.dot_general(a, b, (((0,), (0,)), ((), ())), preferred_element_type=F32)

def dot_nt(a, b):
    return lax.dot_general(a, b, (((1,), (1,)), ((), ())), preferred_element_type=F32)

def rows(start, size):
    return pl.ds(pl.multiple_of(start, size), size)

def ln_fwd(x):
    c = x - jnp.mean(x, axis=1, keepdims=True)
    r = lax.rsqrt(jnp.mean(c * c, axis=1, keepdims=True) + 1e-5)
    return c * r, r

def ln_bwd(y, n, r):
    return r * (y - jnp.mean(y, axis=1, keepdims=True) - n * jnp.mean(y * n, axis=1, keepdims=True))

def make_masks(len_ref, mask_ref, nb):
    pos = lax.broadcasted_iota(jnp.int32, (1, BLK), 1)
    ends = []
    total = jnp.int32(0)
    for p in range(len_ref.shape[1]):
        total = total + len_ref[0, p]
        ends.append(total)

    def block(i, _):
        q = pos + i * BLK
        start = jnp.zeros((1, BLK), jnp.int32)
        for e in ends:
            start = jnp.where(q >= e, e, start)
        k = lax.broadcasted_iota(jnp.int32, (2 * BLK, BLK), 0) + (i - 1) * BLK
        mask_ref[i] = jnp.where((k >= start) & (k <= q), 0.0, NEG).astype(F32)
        return 0

    lax.fori_loop(0, nb, block, 0)

def pad_zero(s):
    s.kp[0:BLK, :] = jnp.zeros((BLK, s.kp.shape[1]), BF)
    s.vp[0:BLK, :] = jnp.zeros((BLK, s.vp.shape[1]), BF)
    s.kt[0] = jnp.zeros(s.kt.shape[1:], BF)
    s.vt[0] = jnp.zeros(s.vt.shape[1:], BF)

def project(s, j, ent, wqkv):
    d = ent.shape[1]
    n, r = ln_fwd(ent)
    nb16 = n.astype(BF)
    s.n1[rows(j * CHUNK, CHUNK), :] = nb16
    s.r1[rows(j * CHUNK, CHUNK), :] = jnp.broadcast_to(r, (CHUNK, 128))
    scale = LOG2E * (d // HEADS) ** -0.5
    q = (dot(nb16, wqkv[:, 0:d]) * scale).astype(BF)
    k = dot(nb16, wqkv[:, d:2 * d]).astype(BF)
    v = dot(nb16, wqkv[:, 2 * d:3 * d]).astype(BF)
    s.qs[rows(j * CHUNK, CHUNK), :] = q
    s.kp[pl.ds(pl.multiple_of(j * CHUNK + BLK, BLK), CHUNK), :] = k
    s.vp[pl.ds(pl.multiple_of(j * CHUNK + BLK, BLK), CHUNK), :] = v
    qt, kt, vt = q.T, k.T, v.T
    for b in range(CHUNK // BLK):
        i = j * (CHUNK // BLK) + b
        s.qst[i] = qt[:, b * BLK:(b + 1) * BLK]
        s.kt[i + 1] = kt[:, b * BLK:(b + 1) * BLK]
        s.vt[i + 1] = vt[:, b * BLK:(b + 1) * BLK]

def split_heads(tile, a, hd):
    z = jnp.zeros_like(tile)
    row = lax.broadcasted_iota(jnp.int32, tile.shape, 0)
    left = jnp.where((row >= a) & (row < a + hd), tile, z)
    right = jnp.where((row >= a + hd) & (row < a + 2 * hd), tile, z)
    return jnp.concatenate([left, right], axis=1)

def stack_heads(tile, a, hd):
    z = jnp.zeros_like(tile)
    lane = lax.broadcasted_iota(jnp.int32, tile.shape, 1)
    top = jnp.where((lane >= a) & (lane < a + hd), tile, z)
    low = jnp.where((lane >= a + hd) & (lane < a + 2 * hd), tile, z)
    return jnp.concatenate([top, low], axis=0)

def attend(s, i, mask_ref):
    d = s.qs.shape[1]
    hd = d // HEADS
    mask = mask_ref[i]
    mask2 = jnp.concatenate([mask, mask], axis=1)
    ones = jnp.ones((16, 2 * BLK), BF)
    for t in range(d // 128):
        kw = s.kp[pl.ds(pl.multiple_of(i * BLK, BLK), 2 * BLK), t * 128:(t + 1) * 128]
        qt = s.qst[i, t * 128:(t + 1) * 128, :]
        for pp in range(128 // (2 * hd)):
            pair = t * (128 // (2 * hd)) + pp
            lo = pair * 2 * hd
            sc = dot(kw, split_heads(qt, pp * 2 * hd, hd)) + mask2
            m = jnp.max(sc, axis=0, keepdims=True)
            e = jnp.exp2(sc - m).astype(BF)
            s.e[i, pair] = e
            vt = jnp.concatenate([s.vt[i, lo:lo + 2 * hd, :], s.vt[i + 1, lo:lo + 2 * hd, :]], axis=1)
            o = dot(jnp.concatenate([vt, ones], axis=0), e)
            inv = 1.0 / o[2 * hd:2 * hd + 1, :]
            s.linv[i, 2 * pair:2 * pair + 1, :] = inv[:, :BLK]
            s.linv[i, 2 * pair + 1:2 * pair + 2, :] = inv[:, BLK:]
            s.ht[i, lo:lo + hd, :] = (o[0:hd, :BLK] * inv[:, :BLK]).astype(BF)
            s.ht[i, lo + hd:lo + 2 * hd, :] = (o[hd:2 * hd, BLK:] * inv[:, BLK:]).astype(BF)

def heads_chunk(s, j):
    return jnp.concatenate([s.ht[j * (CHUNK // BLK) + b] for b in range(CHUNK // BLK)], axis=1)

def mlp(s, j, ent, wout, wup, wdown):
    mid = ent + dot_tn(heads_chunk(s, j), wout[...])
    n, r = ln_fwd(mid)
    nb16 = n.astype(BF)
    at = rows(j * CHUNK, CHUNK)
    s.n2[at, :] = nb16
    s.r2[at, :] = jnp.broadcast_to(r, (CHUNK, 128))
    acc = mid
    for f in range(wup.shape[1] // 256):
        c = slice(f * 256, (f + 1) * 256)
        h = dot(nb16, wup[:, c])
        h2 = h * h
        th = jnp.tanh(h * (GELU_B * h2 + GELU_A))
        sg = 0.5 * th + 0.5
        a = h * sg
        act = a.astype(BF)
        s.act[at, c] = act
        s.gp[at, c] = (sg + a * (1.0 - th) * (3 * GELU_B * h2 + GELU_A)).astype(BF)
        acc = acc + dot(act, wdown[c, :])
    return acc

def mlp_back(s, j, g, wdown_t, wup_t):
    at = rows(j * CHUNK, CHUNK)
    gb = g.astype(BF)
    s.g2[at, :] = gb
    acc = None
    for f in range(wdown_t.shape[1] // 256):
        c = slice(f * 256, (f + 1) * 256)
        dh = (dot(gb, wdown_t[:, c]) * s.gp[at, c].astype(F32)).astype(BF)
        s.dh[at, c] = dh
        part = dot(dh, wup_t[c, :])
        acc = part if acc is None else acc + part
    g = g + ln_bwd(acc, s.n2[at, :].astype(F32), s.r2[at, 0:1])
    s.gm[at, :] = g.astype(BF)
    return g

def attend_back(s, i, wout, dk_ref, dv_ref):
    d = s.qs.shape[1]
    hd = d // HEADS
    at = rows(i * BLK, BLK)
    win = pl.ds(pl.multiple_of(i * BLK, BLK), 2 * BLK)
    dot_ = dot_nt(wout[...], s.gm[at, :])
    li = jnp.concatenate([jnp.broadcast_to(s.linv[i, h:h + 1, :], (hd, BLK)) for h in range(HEADS)], axis=0)
    dost = (dot_ * li).astype(BF)
    doh = (dost.astype(F32) * s.ht[i].astype(F32)).astype(BF)
    dos = dost.T
    minus = jnp.full((2 * BLK, 128), -1.0, BF)
    dqs = []
    for t in range(d // 128):
        tl = slice(t * 128, (t + 1) * 128)
        av = jnp.concatenate([s.vp[win, tl], minus], axis=1)
        qtok = s.qs[at, tl]
        dk = dv = None
        for pp in range(128 // (2 * hd)):
            pair = t * (128 // (2 * hd)) + pp
            lo = pair * 2 * hd
            a = pp * 2 * hd
            bd = jnp.concatenate([split_heads(dost[tl, :], a, hd), split_heads(doh[tl, :], a, hd)], axis=0)
            dp = dot(av, bd)
            e = s.e[i, pair]
            ds = (e.astype(F32) * dp).astype(BF)
            pv = dot(e, stack_heads(dos[:, tl], a, hd))
            pk = dot(ds, stack_heads(qtok, a, hd))
            dv = pv if dv is None else dv + pv
            dk = pk if dk is None else dk + pk
            kt = jnp.concatenate([s.kt[i, lo:lo + 2 * hd, :], s.kt[i + 1, lo:lo + 2 * hd, :]], axis=1)
            dq = dot(kt, ds)
            dqs.append(dq[0:hd, :BLK])
            dqs.append(dq[hd:2 * hd, BLK:])
        top, low = pl.ds(pl.multiple_of(i * BLK, BLK), BLK), pl.ds(pl.multiple_of(i * BLK + BLK, BLK), BLK)
        dk_ref[top, tl] += dk[:BLK]
        dv_ref[top, tl] += dv[:BLK]
        dk_ref[low, tl] = dk[BLK:]
        dv_ref[low, tl] = dv[BLK:]
    dq = jnp.concatenate(dqs, axis=0) * hd ** -0.5
    s.dpk[at, 0:d] = dq.astype(BF).T

def project_back(s, j, g, wqkv_t, dk_ref, dv_ref):
    d = g.shape[1]
    at = rows(j * CHUNK, CHUNK)
    pat = pl.ds(pl.multiple_of(j * CHUNK + BLK, BLK), CHUNK)
    dk = (dk_ref[pat, :] * LN2).astype(BF)
    dv = dv_ref[pat, :].astype(BF)
    s.dpk[at, d:2 * d] = dk
    s.dpk[at, 2 * d:3 * d] = dv
    y = dot(s.dpk[at, 0:d], wqkv_t[0:d, :]) + dot(dk, wqkv_t[d:2 * d, :]) + dot(dv, wqkv_t[2 * d:, :])
    return g + ln_bwd(y, s.n1[at, :].astype(F32), s.r1[at, 0:1])

def saved_shapes(t, d, ff):
    nb = t // BLK
    return dict(n1=((t, d), BF), r1=((t, 128), F32), qs=((t, d), BF), kp=((t + BLK, d), BF), vp=((t + BLK, d), BF),
                qst=((nb, d, BLK), BF), kt=((nb + 1, d, BLK), BF), vt=((nb + 1, d, BLK), BF), e=((nb, HEADS // 2, 2 * BLK, 2 * BLK), BF),
                ht=((nb, d, BLK), BF), linv=((nb, HEADS, BLK), F32))
def more_shapes(t, d, ff):
    return dict(n2=((t, d), BF), r2=((t, 128), F32), act=((t, ff), BF), gp=((t, ff), BF),
                g2=((t, d), BF), gm=((t, d), BF), dh=((t, ff), BF), dpk=((t, 3 * d), BF))

def loop(n, body):
    lax.fori_loop(0, n, lambda i, _: (body(i), 0)[1], 0)

def all_kernel(names, parts, me_ref, len_ref, cnt_ref, *refs):
    states, inject, cot = refs[:3]
    qkv_parts, rest_parts = refs[3:3 + parts], refs[3 + parts:3 + 2 * parts]
    refs = refs[3 + 2 * parts:]
    out, gout, ginj, keep, send = refs[:5]
    sc = dict(zip(names, refs[5:]))
    wqkv, wout, wup, wdown, mqkv, mout, mup, mdown_t, mdown = [sc[k] for k in ("wqkv", "wout", "wup", "wdown", "mqkv", "mout", "mup", "mdown_t", "mdown")]
    me = me_ref[0]
    place_qkv(me, qkv_parts, wqkv)
    place_rest(me, rest_parts, wout, wup, wdown)
    its = [types.SimpleNamespace(**{k[:-1]: v for k, v in sc.items() if k[-1] == str(i)}) for i in range(2)]
    mask, state, dkr, dvr, wqkv_t, wup_t, wdown_t, wout_t = [sc[k] for k in ("mask", "state", "dk", "dv", "wqkv_t", "wup_t", "wdown_t", "tr")]
    t, d = states.shape
    nb, nc = t // BLK, t // CHUNK
    make_masks(len_ref, mask, nb)
    wqkv_t[...] = wqkv[...].T
    wup_t[...] = wup[...].T
    wdown_t[...] = wdown[...].T
    for it, s in enumerate(its):
        src, dst = (states, state) if it == 0 else (state, out)
        pad_zero(s)
        loop(nc, lambda j: project(s, j, src[rows(j * CHUNK, CHUNK), :] + inject[rows(j * CHUNK, CHUNK), :], wqkv))
        loop(nb, lambda i: attend(s, i, mask))
        def m(j):
            at = rows(j * CHUNK, CHUNK)
            dst[at, :] = mlp(s, j, src[at, :] + inject[at, :], wout, wup, wdown)
        loop(nc, m)
    ends = []
    total = jnp.int32(0)
    for p in range(len_ref.shape[1]):
        ends.append(total)
        total = total + len_ref[0, p]
    def wgt(j):
        at = rows(j * CHUNK, CHUNK)
        pos = lax.broadcasted_iota(jnp.int32, (CHUNK, 128), 0) + j * CHUNK
        w = jnp.zeros((CHUNK, 128), F32)
        for p, e in enumerate(ends):
            w = jnp.where(pos >= e, 12.0 / cnt_ref[0, p].astype(F32), w)
        gout[at, :] = cot[at, :] * jnp.concatenate([w] * (d // 128), axis=1)
    loop(nc, wgt)
    for it in (1, 0):
        s = its[it]
        def mb(j):
            at = rows(j * CHUNK, CHUNK)
            gout[at, :] = mlp_back(s, j, gout[at, :], wdown_t, wup_t)
        loop(nc, mb)
        dkr[0:BLK, :] = jnp.zeros((BLK, d), F32)
        dvr[0:BLK, :] = jnp.zeros((BLK, d), F32)
        loop(nb, lambda i: attend_back(s, i, wout, dkr, dvr))
        def pb(j):
            at = rows(j * CHUNK, CHUNK)
            g = project_back(s, j, gout[at, :], wqkv_t, dkr, dvr)
            gout[at, :] = g
            ginj[at, :] = g if it == 1 else ginj[at, :] + g
        loop(nc, pb)
    def wg(lhs, rhs, dst, transpose):
        for it in range(2):
            if transpose: wout_t[it] = lhs[it][...].T
        def tile(c):
            cc = pl.ds(pl.multiple_of(c * 256, 256), 256)
            dst[:, cc] = (dot(wout_t[0], rhs[0][:, cc]) + dot(wout_t[1], rhs[1][:, cc])).astype(BF)
        loop(dst.shape[1] // 256, tile)
    wg([s.g2 for s in its], [s.act for s in its], mdown_t, True)
    wg([s.n2 for s in its], [s.dh for s in its], mup, True)
    wg([s.n1 for s in its], [s.dpk for s in its], mqkv, True)
    for it in range(2):
        for b in range(nb):
            wout_t[it, :, b * BLK:(b + 1) * BLK] = its[it].ht[b]
    wg(None, [s.gm for s in its], mout, False)
    mdown[...] = mdown_t[...].T
    for x in range(parts):
        dst = send if x % 2 else keep
        owner = me ^ x
        r, k = d // parts, x // 2
        lo = 0
        for m in (mqkv, mout, mup):
            for c in range(m.shape[1] // 256):
                dst[k, lo:lo + r, :] = m[rows(owner * r, r), c * 256:(c + 1) * 256]
                lo += r
        r = mdown.shape[0] // parts
        dst[k, lo:lo + r, :] = mdown[rows(owner * r, r), :]

def place_qkv(me, parts, wqkv):
    r = wqkv.shape[0] // len(parts)
    for x, p in enumerate(parts):
        wqkv[rows((me ^ x) * r, r), :] = p[...]

def place_rest(me, parts, wout, wup, wdown):
    r, rd = wout.shape[0] // len(parts), wdown.shape[0] // len(parts)
    for x, p in enumerate(parts):
        at = rows((me ^ x) * r, r)
        wout[at, :] = p[0:r, :]
        for c in range(wup.shape[1] // 256):
            wup[at, c * 256:(c + 1) * 256] = p[(c + 1) * r:(c + 2) * r, :]
        lo = r * (1 + wup.shape[1] // 256)
        wdown[rows((me ^ x) * rd, rd), :] = p[lo:lo + rd, :]

def compute_all(me, states, inject, qkv_parts, rest_parts, lengths, counts, cot, ff):
    t, d = states.shape
    nb = t // BLK
    parts = len(qkv_parts)
    sh = {}
    for i in range(2):
        for k, v in {**saved_shapes(t, d, ff), **more_shapes(t, d, ff)}.items(): sh[k + str(i)] = v
    sh.update(mask=((nb, 2 * BLK, BLK), F32), state=((t, d), F32), dk=((t + BLK, d), F32), dv=((t + BLK, d), F32),
              wqkv_t=((3 * d, d), BF), wup_t=((ff, d), BF), wdown_t=((d, ff), BF), tr=((2, d, t), BF),
              wqkv=((d, 3 * d), BF), wout=((d, d), BF), wup=((d, ff), BF), wdown=((ff, d), BF),
              mqkv=((d, 3 * d), BF), mout=((d, d), BF), mup=((d, ff), BF), mdown_t=((d, ff), BF), mdown=((ff, d), BF))
    S = jax.ShapeDtypeStruct
    vm = pl.BlockSpec(memory_space=pltpu.VMEM)
    sm = pl.BlockSpec(memory_space=pltpu.SMEM)
    piece = (4 * d + 2 * ff) // parts
    half = S((max(parts // 2, 1), piece, d), BF)
    outs = (S((t, d), F32),) * 3 + (half, half)
    return pl.pallas_call(
        functools.partial(all_kernel, list(sh), parts), out_shape=outs, in_specs=[sm, sm, sm] + [vm] * (3 + 2 * parts), out_specs=(vm,) * 5,
        scratch_shapes=[pltpu.VMEM(*v) for v in sh.values()],
        compiler_params=pltpu.CompilerParams(vmem_limit_bytes=63 << 20), name="compute")(
        me, lengths, counts, states, inject, cot, *qkv_parts, *rest_parts)


def exchange(x, axis, size, step):
    return lax.ppermute(x, axis, [(i, i ^ step) for i in range(size)])

def gather_parts(x, size):
    far = [x] + [exchange(x, "fsdp", size, 2 * k) for k in range(1, size // 2)]
    near = [exchange(v, "fsdp", size, 1) for v in far]
    return [v for pair in zip(far, near) for v in pair]

def add_parts(first, others):
    total = first.astype(F32)
    for v in others:
        total = total + v.astype(F32)
    return total

def reduce_parts(keep, send, n_fsdp, n_dp):
    near = exchange(send, "fsdp", n_fsdp, 1)
    summed = [add_parts(keep[k], [near[k]]) for k in range(n_fsdp // 2)]
    far = [exchange(summed[k].astype(BF), "fsdp", n_fsdp, 2 * k) for k in range(1, n_fsdp // 2)]
    share = add_parts(summed[0], far).astype(BF)
    return add_parts(share, [exchange(share, "dp", n_dp, k) for k in range(1, n_dp)])

def on_device(n_dp, n_fsdp, states, inject, ln1_gain, w_qkv, w_out, ln2_gain, w_up, w_down, prompt_lengths, loop_counts, cotangent):
    d = states.shape[1]
    r, ff = w_up.shape
    wide = lambda v: [v[:, c:c + d] for c in range(0, v.shape[1], d)]
    gain_one, gain_two = ln1_gain.astype(F32)[:, None], ln2_gain.astype(F32)[:, None]
    qkv = (w_qkv.astype(F32) * gain_one).astype(BF)
    up = (w_up.astype(F32) * gain_two).astype(BF)
    rest = jnp.concatenate([w_out] + wide(up) + [w_down], axis=0)
    direct = r % 16 == 0
    if direct:
        me = lax.axis_index("fsdp").astype(jnp.int32).reshape(1)
        qkv_parts, rest_parts = gather_parts(qkv, n_fsdp), gather_parts(rest, n_fsdp)
    else:
        me = jnp.zeros((1,), jnp.int32)
        full = lambda v: lax.all_gather(v, "fsdp", axis=0, tiled=True)
        qkv_parts = [full(qkv)]
        rest_parts = [jnp.concatenate([full(w_out)] + wide(full(up)) + [full(w_down)], axis=0)]
    final, grad_states, grad_inject, keep, send = compute_all(
        me, states, inject, qkv_parts, rest_parts, prompt_lengths, loop_counts, cotangent, ff)
    if direct:
        total = reduce_parts(keep, send, n_fsdp, n_dp)
    else:
        whole = keep[0].astype(F32)
        share = lambda v: lax.psum(lax.psum_scatter(v.astype(BF), "fsdp", scatter_dimension=0, tiled=True), "dp").astype(F32)
        pieces = [share(whole[c * d:(c + 1) * d]) for c in range(4 + ff // d)] + [share(whole[4 * d + ff:])]
        total = jnp.concatenate(pieces, axis=0)
    join = lambda lo, n: jnp.concatenate([total[lo + c * r:lo + (c + 1) * r] for c in range(n)], axis=1)
    m_qkv, m_out, m_up = join(0, 3), join(3 * r, 1), join(4 * r, ff // d)
    m_down = total[(4 + ff // d) * r:]
    return (final, grad_states, grad_inject,
            jnp.sum(m_qkv * w_qkv.astype(F32), axis=1), m_qkv * gain_one, m_out,
            jnp.sum(m_up * w_up.astype(F32), axis=1), m_up * gain_two, m_down)

def solution(mesh):
    tok, vec, mat = P(("dp", "fsdp"), None), P("fsdp"), P("fsdp", None)
    return jax.shard_map(
        functools.partial(on_device, mesh.shape["dp"], mesh.shape["fsdp"]), mesh=mesh,
        in_specs=(tok, tok, vec, mat, mat, vec, mat, mat, tok, tok, tok),
        out_specs=(tok, tok, tok, vec, mat, mat, vec, mat, mat), check_vma=False)
```

time: 612 us -> 149 us (0.24)
  matrix products: 200 us -> 0 us
  blocking collectives: 94.3 us -> 0 us
  waiting for transfers between devices: 129 us -> 38.2 us
  other arithmetic: 91.4 us -> 6.76 us
  Pallas kernels: 0 us -> 72.7 us
  local copies, waits for them, and re-layouts: 55.9 us -> 5.94 us
  starting transfers between devices: 0.45 us -> 24.5 us
  loops' own time: 17.5 us -> 0 us
  between operations: 16.9 us -> 0.86 us
    dot_general x52 -> x0, matrix products: 200 us -> none  [the longest x8 63.8 us: block_scores(): jnp.einsum('rhd,thd->hrt', query_rows, key_all, preferred_element_type=jn...]
    psum x2 -> x0, waiting for transfers between devices: 74.6 us -> none  [the longest x1 41.7 us: on_device(): lax.psum(shares[4].astype(jnp.bfloat16), 'dp').astype(jnp.float32)]
    pallas_call x0 -> x1, Pallas kernels: none -> 72.7 us  [compute_all(): pl.pallas_call(functools.partial(all_kernel, list(sh), parts), out_shape=...]
    all_gather x4 -> x0, blocking collectives: 61.9 us -> none  [the longest x1 16 us: on_device(): lax.all_gather(w_up, 'fsdp', axis=0, tiled=True)]
    reduce_scatter x4 -> x0, waiting for transfers between devices: 54.2 us -> none  [the longest x1 31.3 us: on_device(): lax.psum_scatter(partials[5].astype(jnp.bfloat16), 'fsdp', scatter_dimens...]
    convert_element_type x15 -> x6, other arithmetic: 46.1 us -> 3.97 us  [the longest x1 1.25 us: reduce_parts(): summed[k].astype(BF)]
    ppermute x0 -> x21, waiting for transfers between devices: none -> 38.2 us  [exchange(): return lax.ppermute(x, axis, [(i, i ^ step) for i in range(size)])]
    unnamed x2 -> x0, blocking collectives: 32.4 us -> none
  transfers between devices with their start and end apart: 6 -> 21, of which waited for: 4 -> 13; matrix products, arithmetic and copies ran while one was open for 22% -> 0% of each run, Pallas kernels for 0% -> 0%
where the time goes in v1:
time: 149 us
  Pallas kernels  72.7 us (49%)
  waiting for transfers between devices  38.2 us (26%)
  starting transfers between devices  24.5 us (16%)
  other arithmetic  6.76 us (5%)
  local copies, waits for them, and re-layouts  5.94 us (4%)
    pallas_call x1, Pallas kernels, compute_all(): pl.pallas_call(functools.partial(all_kernel, list(sh), parts), out_shape=...  72.7 us
    ppermute x21, waiting for transfers between devices, exchange(): return lax.ppermute(x, axis, [(i, i ^ step) for i in range(size)])  38.2 us
    ppermute x21, starting transfers between devices, exchange(): return lax.ppermute(x, axis, [(i, i ^ step) for i in range(size)])  24.5 us
    unnamed x53, local copies, waits for them, and re-layouts  4.63 us
  transfers between devices with their start and end apart: 21, of which 13 were waited for; matrix products, arithmetic and copies ran while one was open for 0% of the time, Pallas kernels for 0%

profile of v1, /device:TPU:0, one launch (start us, length us, event | category | flops | bytes accessed | tf_op | source)
XLA Modules:
  0.0 148.9 jit_solution(16712055996088906767)
XLA Ops:
  1.3 0.7 constant_dynamic-update-slice_fusion.1
  2.0 0.9 fusion.6
  3.0 0.8 copy-done.11
  3.8 5.1 %collective-permute-start.12 = (bf16[288,256]{1,0:T(8,128)(2,1)S(1)}, bf16[288,256]{1,0:T(8,128)(2,1)S(1)}, u32[]{:S(2)}, u32[]{:S(2)}) collective-permute-start(bf16[288,256]{1,0:T(8,128)(2,1)S(1)} %constant_dynamic-update-slice_fusion.refs_11_), channel_id=1, source_target_pairs={{0,6},{1,7},{2,4},{3,5},{4,2},{5,3},{6,0},{7,1},{8,14},{9,15},{10,... | collective-permute-start | bytes 442376 | tf_op jit(solution)/shard_map/ppermute | solution.py:352
  10.1 3.7 %collective-permute-start.5 = (bf16[32,768]{1,0:T(8,128)(2,1)S(1)}, bf16[32,768]{1,0:T(8,128)(2,1)S(1)}, u32[]{:S(2)}, u32[]{:S(2)}) collective-permute-start(bf16[32,768]{1,0:T(8,128)(2,1)S(1)} %fusion.8.refs_3_), channel_id=1, source_target_pairs={{0,6},{1,7},{2,4},{3,5},{4,2},{5,3},{6,0},{7,1},{8,14},{9,15},{10,... | collective-permute-start | bytes 147464 | tf_op jit(solution)/shard_map/ppermute | solution.py:352
  13.8 7.0 %collective-permute-done.5.refs_9_ = bf16[32,768]{1,0:T(8,128)(2,1)S(1)} collective-permute-done((bf16[32,768]{1,0:T(8,128)(2,1)S(1)}, bf16[32,768]{1,0:T(8,128)(2,1)S(1)}, u32[]{:S(2)}, u32[]{:S(2)}) %collective-permute-start.5) | collective-permute-done | bytes 49184 | tf_op jit(solution)/shard_map/ppermute | solution.py:352
  20.8 4.8 %collective-permute-start.1 = (bf16[32,768]{1,0:T(8,128)(2,1)S(1)}, bf16[32,768]{1,0:T(8,128)(2,1)S(1)}, u32[]{:S(2)}, u32[]{:S(2)}) collective-permute-start(bf16[32,768]{1,0:T(8,128)(2,1)S(1)} %fusion.8.refs_3_), channel_id=1, source_target_pairs={{0,2},{1,3},{2,0},{3,1},{4,6},{5,7},{6,4},{7,5},{8,10},{9,11},{10,... | collective-permute-start | bytes 147464 | tf_op jit(solution)/shard_map/ppermute | solution.py:352
  25.7 2.0 %collective-permute-done.1.refs_5_ = bf16[32,768]{1,0:T(8,128)(2,1)S(1)} collective-permute-done((bf16[32,768]{1,0:T(8,128)(2,1)S(1)}, bf16[32,768]{1,0:T(8,128)(2,1)S(1)}, u32[]{:S(2)}, u32[]{:S(2)}) %collective-permute-start.1) | collective-permute-done | bytes 49184 | tf_op jit(solution)/shard_map/ppermute | solution.py:352
  29.5 0.9 collective-permute-done.4.refs_8_
  30.7 0.9 collective-permute-done.2.refs_6_
  33.1 72.7 %compute.1 = (f32[1024,256]{1,0:T(8,128)}, f32[1024,256]{1,0:T(8,128)}, f32[1024,256]{1,0:T(8,128)}, bf16[4,384,256]{2,1,0:T(8,128)(2,1)}, bf16[4,384,256]{2,1,0:T(8,128)(2,1)}) custom-call(s32[1]{0:T(128)} %bitcast.me_ref, s32[1,16]{1,0:T(1,128)} %len_ref.1, s32[1,16]{1,0:T(1,128)} %cnt_ref.1, f32[1024,256]{1,0:T(8,128)} %refs_0_.1, f32[1024,256]{1,0:T(8,128)} %refs_1_.1, ...), custom_call_target="tpu_custom_call" | custom-call | tf_op jit(solution)/shard_map/compute/pallas_call | solution.py:344
  106.1 2.2 %collective-permute-done.14 = bf16[4,384,256]{2,1,0:T(8,128)(2,1)S(1)} collective-permute-done((bf16[4,384,256]{2,1,0:T(8,128)(2,1)}, bf16[4,384,256]{2,1,0:T(8,128)(2,1)S(1)}, u32[]{:S(2)}, u32[]{:S(2)}) %collective-permute-start.14) | collective-permute-done | bytes 786464 | tf_op jit(solution)/shard_map/ppermute | solution.py:352
  108.3 1.3 fusion.3
  109.5 2.1 %collective-permute-start.15 = (bf16[384,256]{1,0:T(8,128)(2,1)S(1)}, bf16[384,256]{1,0:T(8,128)(2,1)S(1)}, u32[]{:S(2)}, u32[]{:S(2)}) collective-permute-start(bf16[384,256]{1,0:T(8,128)(2,1)S(1)} %get-tuple-element.19), channel_id=1, source_target_pairs={{0,2},{1,3},{2,0},{3,1},{4,6},{5,7},{6,4},{7,5},{8,10},{9,11},{10,... | collective-permute-start | bytes 589832 | tf_op jit(solution)/shard_map/ppermute | solution.py:352
  111.6 2.5 %collective-permute-start.17 = (bf16[384,256]{1,0:T(8,128)(2,1)S(1)}, bf16[384,256]{1,0:T(8,128)(2,1)S(1)}, u32[]{:S(2)}, u32[]{:S(2)}) collective-permute-start(bf16[384,256]{1,0:T(8,128)(2,1)S(1)} %get-tuple-element.20), channel_id=1, source_target_pairs={{0,6},{1,7},{2,4},{3,5},{4,2},{5,3},{6,0},{7,1},{8,14},{9,15},{10,... | collective-permute-start | bytes 589832 | tf_op jit(solution)/shard_map/ppermute | solution.py:352
  114.1 2.9 %collective-permute-done.15 = bf16[384,256]{1,0:T(8,128)(2,1)S(1)} collective-permute-done((bf16[384,256]{1,0:T(8,128)(2,1)S(1)}, bf16[384,256]{1,0:T(8,128)(2,1)S(1)}, u32[]{:S(2)}, u32[]{:S(2)}) %collective-permute-start.15) | collective-permute-done | bytes 196640 | tf_op jit(solution)/shard_map/ppermute | solution.py:352
  117.0 7.2 %collective-permute-done.17 = bf16[384,256]{1,0:T(8,128)(2,1)S(1)} collective-permute-done((bf16[384,256]{1,0:T(8,128)(2,1)S(1)}, bf16[384,256]{1,0:T(8,128)(2,1)S(1)}, u32[]{:S(2)}, u32[]{:S(2)}) %collective-permute-start.17) | collective-permute-done | bytes 196640 | tf_op jit(solution)/shard_map/ppermute | solution.py:352
  124.1 6.7 %collective-permute-done.16 = bf16[384,256]{1,0:T(8,128)(2,1)S(1)} collective-permute-done((bf16[384,256]{1,0:T(8,128)(2,1)S(1)}, bf16[384,256]{1,0:T(8,128)(2,1)S(1)}, u32[]{:S(2)}, u32[]{:S(2)}) %collective-permute-start.16) | collective-permute-done | bytes 196640 | tf_op jit(solution)/shard_map/ppermute | solution.py:352
  130.9 1.1 fusion.2
  131.9 2.5 %collective-permute-start.20 = (bf16[384,256]{1,0:T(8,128)(2,1)S(1)}, bf16[384,256]{1,0:T(8,128)(2,1)S(1)}, u32[]{:S(2)}, u32[]{:S(2)}) collective-permute-start(bf16[384,256]{1,0:T(8,128)(2,1)S(1)} %fusion.2), channel_id=1, source_target_pairs={{0,24},{8,16},{16,8},{24,0},{1,25},{9,17},{17,9},{25,1},{2,26},{10... | collective-permute-start | bytes 589832 | tf_op jit(solution)/shard_map/ppermute | solution.py:352
  135.5 5.2 %collective-permute-done.20 = bf16[384,256]{1,0:T(8,128)(2,1)S(1)} collective-permute-done((bf16[384,256]{1,0:T(8,128)(2,1)S(1)}, bf16[384,256]{1,0:T(8,128)(2,1)S(1)}, u32[]{:S(2)}, u32[]{:S(2)}) %collective-permute-start.20) | collective-permute-done | bytes 196640 | tf_op jit(solution)/shard_map/ppermute | solution.py:352
  140.7 2.7 %collective-permute-done.19 = bf16[384,256]{1,0:T(8,128)(2,1)S(1)} collective-permute-done((bf16[384,256]{1,0:T(8,128)(2,1)S(1)}, bf16[384,256]{1,0:T(8,128)(2,1)S(1)}, u32[]{:S(2)}, u32[]{:S(2)}) %collective-permute-start.19) | collective-permute-done | bytes 196640 | tf_op jit(solution)/shard_map/ppermute | solution.py:352
  145.6 1.3 fusion.11
  147.6 1.4 fusion.10
  (84 shorter events, 9.5 us)
Async XLA Ops:
  3.8 29.3 %copy-start.3 = (bf16[288,256]{1,0:T(8,128)(2,1)}, bf16[288,256]{1,0:T(8,128)(2,1)S(1)}, u32[]{:S(2)}) copy-start(bf16[288,256]{1,0:T(8,128)(2,1)S(1)} %constant_dynamic-update-slice_fusion.refs_11_) | copy-start | bytes 442372
  3.8 24.4 %collective-permute-start.12 = (bf16[288,256]{1,0:T(8,128)(2,1)S(1)}, bf16[288,256]{1,0:T(8,128)(2,1)S(1)}, u32[]{:S(2)}, u32[]{:S(2)}) collective-permute-start(bf16[288,256]{1,0:T(8,128)(2,1)S(1)} %constant_dynamic-update-slice_fusion.refs_11_), channel_id=1, source_target_pairs={{0,6},{1,7},{2,4},{3,5},{4,2},{5,3},{6,0},{7,1},{8,14},{9,15},{10,... | collective-permute-start | bytes 442376 | tf_op jit(solution)/shard_map/ppermute | solution.py:352
  8.9 19.4 %collective-permute-start.10 = (bf16[288,256]{1,0:T(8,128)(2,1)S(1)}, bf16[288,256]{1,0:T(8,128)(2,1)S(1)}, u32[]{:S(2)}, u32[]{:S(2)}) collective-permute-start(bf16[288,256]{1,0:T(8,128)(2,1)S(1)} %constant_dynamic-update-slice_fusion.refs_11_), channel_id=1, source_target_pairs={{0,4},{1,5},{2,6},{3,7},{4,0},{5,1},{6,2},{7,3},{8,12},{9,13},{10,... | collective-permute-start | bytes 442376 | tf_op jit(solution)/shard_map/ppermute | solution.py:352
  8.9 19.8 %collective-permute-start.8 = (bf16[288,256]{1,0:T(8,128)(2,1)S(1)}, bf16[288,256]{1,0:T(8,128)(2,1)S(1)}, u32[]{:S(2)}, u32[]{:S(2)}) collective-permute-start(bf16[288,256]{1,0:T(8,128)(2,1)S(1)} %constant_dynamic-update-slice_fusion.refs_11_), channel_id=1, source_target_pairs={{0,2},{1,3},{2,0},{3,1},{4,6},{5,7},{6,4},{7,5},{8,10},{9,11},{10,... | collective-permute-start | bytes 442376 | tf_op jit(solution)/shard_map/ppermute | solution.py:352
  10.1 23.0 %copy-start.1 = (bf16[32,768]{1,0:T(8,128)(2,1)}, bf16[32,768]{1,0:T(8,128)(2,1)S(1)}, u32[]{:S(2)}) copy-start(bf16[32,768]{1,0:T(8,128)(2,1)S(1)} %fusion.8.refs_3_) | copy-start | bytes 147460
  10.1 10.7 %collective-permute-start.5 = (bf16[32,768]{1,0:T(8,128)(2,1)S(1)}, bf16[32,768]{1,0:T(8,128)(2,1)S(1)}, u32[]{:S(2)}, u32[]{:S(2)}) collective-permute-start(bf16[32,768]{1,0:T(8,128)(2,1)S(1)} %fusion.8.refs_3_), channel_id=1, source_target_pairs={{0,6},{1,7},{2,4},{3,5},{4,2},{5,3},{6,0},{7,1},{8,14},{9,15},{10,... | collective-permute-start | bytes 147464 | tf_op jit(solution)/shard_map/ppermute | solution.py:352
  13.8 11.9 %collective-permute-start.3 = (bf16[32,768]{1,0:T(8,128)(2,1)S(1)}, bf16[32,768]{1,0:T(8,128)(2,1)S(1)}, u32[]{:S(2)}, u32[]{:S(2)}) collective-permute-start(bf16[32,768]{1,0:T(8,128)(2,1)S(1)} %fusion.8.refs_3_), channel_id=1, source_target_pairs={{0,4},{1,5},{2,6},{3,7},{4,0},{5,1},{6,2},{7,3},{8,12},{9,13},{10,... | collective-permute-start | bytes 147464 | tf_op jit(solution)/shard_map/ppermute | solution.py:352
  20.8 10.9 %copy-start.12 = (bf16[32,768]{1,0:T(8,128)(2,1)}, bf16[32,768]{1,0:T(8,128)(2,1)S(1)}, u32[]{:S(2)}) copy-start(bf16[32,768]{1,0:T(8,128)(2,1)S(1)} %collective-permute-done.5.refs_9_) | copy-start | bytes 147460
  20.8 6.9 %collective-permute-start.1 = (bf16[32,768]{1,0:T(8,128)(2,1)S(1)}, bf16[32,768]{1,0:T(8,128)(2,1)S(1)}, u32[]{:S(2)}, u32[]{:S(2)}) collective-permute-start(bf16[32,768]{1,0:T(8,128)(2,1)S(1)} %fusion.8.refs_3_), channel_id=1, source_target_pairs={{0,2},{1,3},{2,0},{3,1},{4,6},{5,7},{6,4},{7,5},{8,10},{9,11},{10,... | collective-permute-start | bytes 147464 | tf_op jit(solution)/shard_map/ppermute | solution.py:352
  25.7 2.0 %collective-permute-start = (bf16[32,768]{1,0:T(8,128)(2,1)S(1)}, bf16[32,768]{1,0:T(8,128)(2,1)S(1)}, u32[]{:S(2)}, u32[]{:S(2)}) collective-permute-start(bf16[32,768]{1,0:T(8,128)(2,1)S(1)} %fusion.8.refs_3_), channel_id=1, source_target_pairs={{0,1},{1,0},{2,3},{3,2},{4,5},{5,4},{6,7},{7,6},{8,9},{9,8},{10,11... | collective-permute-start | bytes 147464 | tf_op jit(solution)/shard_map/ppermute | solution.py:352
  27.7 3.9 %collective-permute-start.7 = (bf16[288,256]{1,0:T(8,128)(2,1)S(1)}, bf16[288,256]{1,0:T(8,128)(2,1)S(1)}, u32[]{:S(2)}, u32[]{:S(2)}) collective-permute-start(bf16[288,256]{1,0:T(8,128)(2,1)S(1)} %constant_dynamic-update-slice_fusion.refs_11_), channel_id=1, source_target_pairs={{0,1},{1,0},{2,3},{3,2},{4,5},{5,4},{6,7},{7,6},{8,9},{9,8},{10,11... | collective-permute-start | bytes 442376 | tf_op jit(solution)/shard_map/ppermute | solution.py:352
  27.7 1.4 collective-permute-start.6
  28.2 3.4 %collective-permute-start.13 = (bf16[288,256]{1,0:T(8,128)(2,1)S(1)}, bf16[288,256]{1,0:T(8,128)(2,1)S(1)}, u32[]{:S(2)}, u32[]{:S(2)}) collective-permute-start(bf16[288,256]{1,0:T(8,128)(2,1)S(1)} %collective-permute-done.12.refs_17_), channel_id=1, source_target_pairs={{0,1},{1,0},{2,3},{3,2},{4,5},{5,4},{6,7},{7,6},{8,9},{9,8},{10,11... | collective-permute-start | bytes 442376 | tf_op jit(solution)/shard_map/ppermute | solution.py:352
  28.3 3.3 %collective-permute-start.11 = (bf16[288,256]{1,0:T(8,128)(2,1)S(1)}, bf16[288,256]{1,0:T(8,128)(2,1)S(1)}, u32[]{:S(2)}, u32[]{:S(2)}) collective-permute-start(bf16[288,256]{1,0:T(8,128)(2,1)S(1)} %collective-permute-done.10.refs_15_), channel_id=1, source_target_pairs={{0,1},{1,0},{2,3},{3,2},{4,5},{5,4},{6,7},{7,6},{8,9},{9,8},{10,11... | collective-permute-start | bytes 442376 | tf_op jit(solution)/shard_map/ppermute | solution.py:352
  28.8 2.9 %collective-permute-start.9 = (bf16[288,256]{1,0:T(8,128)(2,1)S(1)}, bf16[288,256]{1,0:T(8,128)(2,1)S(1)}, u32[]{:S(2)}, u32[]{:S(2)}) collective-permute-start(bf16[288,256]{1,0:T(8,128)(2,1)S(1)} %collective-permute-done.8.refs_13_), channel_id=1, source_target_pairs={{0,1},{1,0},{2,3},{3,2},{4,5},{5,4},{6,7},{7,6},{8,9},{9,8},{10,11... | collective-permute-start | bytes 442376 | tf_op jit(solution)/shard_map/ppermute | solution.py:352
  29.2 1.2 collective-permute-start.4
  30.4 1.2 collective-permute-start.2
  105.8 2.5 %collective-permute-start.14 = (bf16[4,384,256]{2,1,0:T(8,128)(2,1)}, bf16[4,384,256]{2,1,0:T(8,128)(2,1)S(1)}, u32[]{:S(2)}, u32[]{:S(2)}) collective-permute-start(bf16[4,384,256]{2,1,0:T(8,128)(2,1)} %get-tuple-element.18), channel_id=1, source_target_pairs={{0,1},{1,0},{2,3},{3,2},{4,5},{5,4},{6,7},{7,6},{8,9},{9,8},{10,11... | collective-permute-start | bytes 2359304 | tf_op jit(solution)/shard_map/ppermute | solution.py:352
  109.5 7.5 %collective-permute-start.15 = (bf16[384,256]{1,0:T(8,128)(2,1)S(1)}, bf16[384,256]{1,0:T(8,128)(2,1)S(1)}, u32[]{:S(2)}, u32[]{:S(2)}) collective-permute-start(bf16[384,256]{1,0:T(8,128)(2,1)S(1)} %get-tuple-element.19), channel_id=1, source_target_pairs={{0,2},{1,3},{2,0},{3,1},{4,6},{5,7},{6,4},{7,5},{8,10},{9,11},{10,... | collective-permute-start | bytes 589832 | tf_op jit(solution)/shard_map/ppermute | solution.py:352
  111.6 12.5 %collective-permute-start.17 = (bf16[384,256]{1,0:T(8,128)(2,1)S(1)}, bf16[384,256]{1,0:T(8,128)(2,1)S(1)}, u32[]{:S(2)}, u32[]{:S(2)}) collective-permute-start(bf16[384,256]{1,0:T(8,128)(2,1)S(1)} %get-tuple-element.20), channel_id=1, source_target_pairs={{0,6},{1,7},{2,4},{3,5},{4,2},{5,3},{6,0},{7,1},{8,14},{9,15},{10,... | collective-permute-start | bytes 589832 | tf_op jit(solution)/shard_map/ppermute | solution.py:352
  114.1 16.8 %collective-permute-start.16 = (bf16[384,256]{1,0:T(8,128)(2,1)S(1)}, bf16[384,256]{1,0:T(8,128)(2,1)S(1)}, u32[]{:S(2)}, u32[]{:S(2)}) collective-permute-start(bf16[384,256]{1,0:T(8,128)(2,1)S(1)} %get-tuple-element.21), channel_id=1, source_target_pairs={{0,4},{1,5},{2,6},{3,7},{4,0},{5,1},{6,2},{7,3},{8,12},{9,13},{10,... | collective-permute-start | bytes 589832 | tf_op jit(solution)/shard_map/ppermute | solution.py:352
  131.9 8.8 %collective-permute-start.20 = (bf16[384,256]{1,0:T(8,128)(2,1)S(1)}, bf16[384,256]{1,0:T(8,128)(2,1)S(1)}, u32[]{:S(2)}, u32[]{:S(2)}) collective-permute-start(bf16[384,256]{1,0:T(8,128)(2,1)S(1)} %fusion.2), channel_id=1, source_target_pairs={{0,24},{8,16},{16,8},{24,0},{1,25},{9,17},{17,9},{25,1},{2,26},{10... | collective-permute-start | bytes 589832 | tf_op jit(solution)/shard_map/ppermute | solution.py:352
  134.4 9.0 %collective-permute-start.19 = (bf16[384,256]{1,0:T(8,128)(2,1)S(1)}, bf16[384,256]{1,0:T(8,128)(2,1)S(1)}, u32[]{:S(2)}, u32[]{:S(2)}) collective-permute-start(bf16[384,256]{1,0:T(8,128)(2,1)S(1)} %fusion.2), channel_id=1, source_target_pairs={{0,16},{8,24},{16,0},{24,8},{1,17},{9,25},{17,1},{25,9},{2,18},{10... | collective-permute-start | bytes 589832 | tf_op jit(solution)/shard_map/ppermute | solution.py:352
  135.0 8.6 %collective-permute-start.18 = (bf16[384,256]{1,0:T(8,128)(2,1)S(1)}, bf16[384,256]{1,0:T(8,128)(2,1)S(1)}, u32[]{:S(2)}, u32[]{:S(2)}) collective-permute-start(bf16[384,256]{1,0:T(8,128)(2,1)S(1)} %fusion.2), channel_id=1, source_target_pairs={{0,8},{8,0},{16,24},{24,16},{1,9},{9,1},{17,25},{25,17},{2,10},{10... | collective-permute-start | bytes 589832 | tf_op jit(solution)/shard_map/ppermute | solution.py:352
  (21 other events, 52.9 us)

commit v2 on v1

v2 whole, which is shorter than its diff:
```python
import functools
import types

import jax
import jax.numpy as jnp
from jax import lax
from jax.experimental import pallas as pl
from jax.experimental.pallas import tpu as pltpu
from jax.sharding import PartitionSpec as P

BF = jnp.bfloat16
F32 = jnp.float32
HEADS = 8
ITERS = 2
BLK = 128
CHUNK = 512
NEG = -1e30
LOG2E = 1.4426950408889634
LN2 = 0.6931471805599453
GELU_A = 0.7978845608028654
GELU_B = GELU_A * 0.044715
FLOPS_FIRST = 10 ** 9
FLOPS_LAST = 10 ** 10


def dot(a, b):
    return jnp.dot(a, b, preferred_element_type=F32)

def dot_tn(a, b):
    return lax.dot_general(a, b, (((0,), (0,)), ((), ())), preferred_element_type=F32)

def dot_nt(a, b):
    return lax.dot_general(a, b, (((1,), (1,)), ((), ())), preferred_element_type=F32)

def rows(start, size):
    return pl.ds(pl.multiple_of(start, size), size)

def ln_fwd(x):
    c = x - jnp.mean(x, axis=1, keepdims=True)
    r = lax.rsqrt(jnp.mean(c * c, axis=1, keepdims=True) + 1e-5)
    return c * r, r

def ln_bwd(y, n, r):
    return r * (y - jnp.mean(y, axis=1, keepdims=True) - n * jnp.mean(y * n, axis=1, keepdims=True))

def loop(n, body):
    lax.fori_loop(0, n, lambda i, _: (body(i), 0)[1], 0)

def make_masks(len_ref, mask_ref, nb):
    pos = lax.broadcasted_iota(jnp.int32, (1, BLK), 1)
    ends = []
    total = jnp.int32(0)
    for p in range(len_ref.shape[1]):
        total = total + len_ref[0, p]
        ends.append(total)

    def block(i, _):
        q = pos + i * BLK
        start = jnp.zeros((1, BLK), jnp.int32)
        for e in ends:
            start = jnp.where(q >= e, e, start)
        k = lax.broadcasted_iota(jnp.int32, (2 * BLK, BLK), 0) + (i - 1) * BLK
        mask_ref[i] = jnp.where((k >= start) & (k <= q), 0.0, NEG).astype(F32)
        return 0

    lax.fori_loop(0, nb, block, 0)

def pad_zero(s):
    s.kp[0:BLK, :] = jnp.zeros((BLK, s.kp.shape[1]), BF)
    s.vp[0:BLK, :] = jnp.zeros((BLK, s.vp.shape[1]), BF)
    s.kt[0] = jnp.zeros(s.kt.shape[1:], BF)
    s.vt[0] = jnp.zeros(s.vt.shape[1:], BF)

def project(s, j, ent, wqkv):
    d = ent.shape[1]
    n, r = ln_fwd(ent)
    nb16 = n.astype(BF)
    s.n1[rows(j * CHUNK, CHUNK), :] = nb16
    s.r1[rows(j * CHUNK, CHUNK), :] = jnp.broadcast_to(r, (CHUNK, 128))
    scale = LOG2E * (d // HEADS) ** -0.5
    q = (dot(nb16, wqkv[:, 0:d]) * scale).astype(BF)
    k = dot(nb16, wqkv[:, d:2 * d]).astype(BF)
    v = dot(nb16, wqkv[:, 2 * d:3 * d]).astype(BF)
    s.qs[rows(j * CHUNK, CHUNK), :] = q
    s.kp[pl.ds(pl.multiple_of(j * CHUNK + BLK, BLK), CHUNK), :] = k
    s.vp[pl.ds(pl.multiple_of(j * CHUNK + BLK, BLK), CHUNK), :] = v
    qt, kt, vt = q.T, k.T, v.T
    for b in range(CHUNK // BLK):
        i = j * (CHUNK // BLK) + b
        s.qst[i] = qt[:, b * BLK:(b + 1) * BLK]
        s.kt[i + 1] = kt[:, b * BLK:(b + 1) * BLK]
        s.vt[i + 1] = vt[:, b * BLK:(b + 1) * BLK]

def split_heads(tile, a, hd):
    def alone(lo):
        parts = [jnp.zeros((n, tile.shape[1]), tile.dtype) for n in (lo, tile.shape[0] - lo - hd)]
        parts = [parts[0], tile[lo:lo + hd], parts[1]]
        return jnp.concatenate([p for p in parts if p.shape[0]], axis=0)
    return jnp.concatenate([alone(a), alone(a + hd)], axis=1)

def stack_heads(tile, a, hd):
    z = jnp.zeros_like(tile)
    lane = lax.broadcasted_iota(jnp.int32, tile.shape, 1)
    top = jnp.where((lane >= a) & (lane < a + hd), tile, z)
    low = jnp.where((lane >= a + hd) & (lane < a + 2 * hd), tile, z)
    return jnp.concatenate([top, low], axis=0)

def pairs_of(d):
    hd = d // HEADS
    per = 128 // (2 * hd)
    return [(p, slice(p // per * 128, p // per * 128 + 128), p % per * 2 * hd, p * 2 * hd) for p in range(HEADS // 2)]

def window(ref, i, lo, n):
    return jnp.concatenate([ref[i, lo:lo + n, :], ref[i + 1, lo:lo + n, :]], axis=1)

def attend(s, blocks, mask_ref):
    d = s.qs.shape[1]
    hd = d // HEADS
    ones = jnp.ones((16, 2 * BLK), BF)
    def scores(i):
        win = pl.ds(pl.multiple_of(i * BLK, BLK), 2 * BLK)
        return [dot(s.kp[win, tile], split_heads(s.qst[i, tile, :], a, hd)) for _, tile, a, _ in pairs_of(d)]
    def soft(i, all_scores):
        mask = mask_ref[i]
        mask = jnp.concatenate([mask, mask], axis=1)
        out = []
        for sc in all_scores:
            sc = sc + mask
            out.append(jnp.exp2(sc - jnp.max(sc, axis=0, keepdims=True)).astype(BF))
        return out
    def values(i, es):
        return [dot(jnp.concatenate([window(s.vt, i, lo, 2 * hd), ones], axis=0), es[p]) for p, _, _, lo in pairs_of(d)]
    es = []
    ready = scores(blocks[0])
    for n, i in enumerate(blocks):
        ahead = scores(blocks[n + 1]) if n + 1 < len(blocks) else None
        es.append(soft(i, ready))
        ready = ahead
    os = [values(i, e) for i, e in zip(blocks, es)]
    for i, e, o in zip(blocks, es, os):
        for p, _, _, lo in pairs_of(d):
            s.e[i, p] = e[p]
            inv = 1.0 / o[p][2 * hd:2 * hd + 1, :]
            s.linv[i, 2 * p:2 * p + 1, :] = inv[:, :BLK]
            s.linv[i, 2 * p + 1:2 * p + 2, :] = inv[:, BLK:]
            s.ht[i, lo:lo + hd, :] = (o[p][0:hd, :BLK] * inv[:, :BLK]).astype(BF)
            s.ht[i, lo + hd:lo + 2 * hd, :] = (o[p][hd:2 * hd, BLK:] * inv[:, BLK:]).astype(BF)

def heads_chunk(s, j):
    return jnp.concatenate([s.ht[j * (CHUNK // BLK) + b] for b in range(CHUNK // BLK)], axis=1)

def mlp(s, j, ent, wout, wup, wdown):
    mid = ent + dot_tn(heads_chunk(s, j), wout[...])
    n, r = ln_fwd(mid)
    nb16 = n.astype(BF)
    at = rows(j * CHUNK, CHUNK)
    s.n2[at, :] = nb16
    s.r2[at, :] = jnp.broadcast_to(r, (CHUNK, 128))
    acc = mid
    for f in range(wup.shape[1] // 256):
        c = slice(f * 256, (f + 1) * 256)
        h = dot(nb16, wup[:, c])
        h2 = h * h
        th = jnp.tanh(h * (GELU_B * h2 + GELU_A))
        sg = 0.5 * th + 0.5
        a = h * sg
        act = a.astype(BF)
        s.act[at, c] = act
        s.gp[at, c] = (sg + a * (1.0 - th) * (3 * GELU_B * h2 + GELU_A)).astype(BF)
        acc = acc + dot(act, wdown[c, :])
    return acc

def mlp_back(s, j, g, wdown_t, wup_t):
    at = rows(j * CHUNK, CHUNK)
    gb = g.astype(BF)
    s.g2[at, :] = gb
    acc = None
    for f in range(wdown_t.shape[1] // 256):
        c = slice(f * 256, (f + 1) * 256)
        dh = (dot(gb, wdown_t[:, c]) * s.gp[at, c].astype(F32)).astype(BF)
        s.dh[at, c] = dh
        part = dot(dh, wup_t[c, :])
        acc = part if acc is None else acc + part
    g = g + ln_bwd(acc, s.n2[at, :].astype(F32), s.r2[at, 0:1])
    s.gm[at, :] = g.astype(BF)
    return g

def attend_back(s, blocks, wout, dk_ref, dv_ref):
    d = s.qs.shape[1]
    hd = d // HEADS
    minus = jnp.full((2 * BLK, 128), -1.0, BF)
    def head_grads(i):
        raw = dot_nt(wout[...], s.gm[rows(i * BLK, BLK), :])
        inv = jnp.concatenate([jnp.broadcast_to(s.linv[i, h:h + 1, :], (hd, BLK)) for h in range(HEADS)], axis=0)
        dost = (raw * inv).astype(BF)
        return dost, (dost.astype(F32) * s.ht[i].astype(F32)).astype(BF), dost.T
    def prob_grads(i, dost, doh):
        win = pl.ds(pl.multiple_of(i * BLK, BLK), 2 * BLK)
        return [dot(jnp.concatenate([s.vp[win, tile], minus], axis=1),
                    jnp.concatenate([split_heads(dost[tile, :], a, hd), split_heads(doh[tile, :], a, hd)], axis=0))
                for _, tile, a, _ in pairs_of(d)]
    def by_keys(lhs, tokens):
        return [dot(lhs[p], stack_heads(tokens[:, tile], a, hd)) for p, tile, a, _ in pairs_of(d)]
    def by_queries(i, dss):
        out = []
        for p, _, _, lo in pairs_of(d):
            dq = dot(window(s.kt, i, lo, 2 * hd), dss[p])
            out += [dq[0:hd, :BLK], dq[hd:2 * hd, BLK:]]
        return (jnp.concatenate(out, axis=0) * hd ** -0.5).astype(BF)
    heads = [head_grads(i) for i in blocks]
    dps = [prob_grads(i, h[0], h[1]) for i, h in zip(blocks, heads)]
    es = [[s.e[i, p] for p in range(HEADS // 2)] for i in blocks]
    dvs = [by_keys(e, h[2]) for e, h in zip(es, heads)]
    dss = [[(x.astype(F32) * y).astype(BF) for x, y in zip(e, dp)] for e, dp in zip(es, dps)]
    dks = [by_keys(ds, s.qs[rows(i * BLK, BLK), :]) for i, ds in zip(blocks, dss)]
    dqs = [by_queries(i, ds) for i, ds in zip(blocks, dss)]
    per = HEADS // 2 // (d // 128)
    for n, i in enumerate(blocks):
        top, low = pl.ds(pl.multiple_of(i * BLK, BLK), BLK), pl.ds(pl.multiple_of(i * BLK + BLK, BLK), BLK)
        for ref, parts in ((dk_ref, dks[n]), (dv_ref, dvs[n])):
            for t in range(d // 128):
                tile = slice(t * 128, (t + 1) * 128)
                total = sum(parts[t * per + 1:(t + 1) * per], parts[t * per])
                ref[top, tile] += total[:BLK]
                ref[low, tile] = total[BLK:]
        s.dpk[rows(i * BLK, BLK), 0:d] = dqs[n].T

def finish_packed(s, j, dk_ref, dv_ref):
    d = s.n1.shape[1]
    at = rows(j * CHUNK, CHUNK)
    pat = pl.ds(pl.multiple_of(j * CHUNK + BLK, BLK), CHUNK)
    s.dpk[at, d:2 * d] = (dk_ref[pat, :] * LN2).astype(BF)
    s.dpk[at, 2 * d:3 * d] = dv_ref[pat, :].astype(BF)

def project_back(s, j, g, wqkv_t):
    at = rows(j * CHUNK, CHUNK)
    return g + ln_bwd(dot(s.dpk[at, :], wqkv_t[...]), s.n1[at, :].astype(F32), s.r1[at, 0:1])

def weigh(cnt_ref, len_ref, j, cot):
    pos = lax.broadcasted_iota(jnp.int32, (CHUNK, 128), 0) + j * CHUNK
    w = jnp.zeros((CHUNK, 128), F32)
    begin = jnp.int32(0)
    for p in range(len_ref.shape[1]):
        w = jnp.where(pos >= begin, 12.0 / cnt_ref[0, p].astype(F32), w)
        begin = begin + len_ref[0, p]
    return cot * jnp.concatenate([w] * (cot.shape[1] // 128), axis=1)

def saved_shapes(t, d, ff):
    nb = t // BLK
    return dict(n1=((t, d), BF), r1=((t, 128), F32), qs=((t, d), BF), kp=((t + BLK, d), BF), vp=((t + BLK, d), BF),
                qst=((nb, d, BLK), BF), kt=((nb + 1, d, BLK), BF), vt=((nb + 1, d, BLK), BF), e=((nb, HEADS // 2, 2 * BLK, 2 * BLK), BF),
                ht=((nb, d, BLK), BF), linv=((nb, HEADS, BLK), F32))
def more_shapes(t, d, ff):
    return dict(n2=((t, d), BF), r2=((t, 128), F32), act=((t, ff), BF), gp=((t, ff), BF),
                g2=((t, d), BF), gm=((t, d), BF), dh=((t, ff), BF), dpk=((t, 3 * d), BF))

class Memory:
    def __init__(self, ins, outs, load_sems, store_sems, hbm_in, hbm_out, parts):
        self.ins, self.outs = ins, outs
        self.load_sems, self.store_sems, self.hbm_in, self.hbm_out, self.parts = load_sems, store_sems, hbm_in, hbm_out, parts
        self.used, self.started = 0, []

    def _load(self, n, c):
        size = self.ins[n].shape[0] // self.parts[n][0]
        where = pl.ds(c * size, size)
        return pltpu.make_async_copy(self.hbm_in[n].at[where], self.ins[n].at[where], self.load_sems.at[self.parts[n][1] + c])

    def start(self, *which):
        for n in which or sorted(self.parts):
            for c in range(self.parts[n][0]):
                self._load(n, c).start()

    def wait(self, *which, part=None):
        for n in which:
            for c in range(self.parts[n][0]) if part is None else (part,):
                self._load(n, c).wait()

    def put(self, n, entry=None):
        src, dst = self.outs[n], self.hbm_out[n]
        if entry is not None:
            src, dst = src.at[entry], dst.at[entry]
        copy = pltpu.make_async_copy(src, dst, self.store_sems.at[self.used])
        copy.start()
        self.started.append(copy)
        self.used += 1

def call(kernel, outs, args, scratch, name, flops, puts=0):
    spec = dict(vmem=pl.BlockSpec(memory_space=pltpu.VMEM), smem=pl.BlockSpec(memory_space=pltpu.SMEM), any=pl.BlockSpec(memory_space=pl.ANY))
    spec["load"] = spec["store"] = spec["any"]
    n_in, n_out, n_scratch = len(args), len(outs), len(scratch)
    parts, total = {}, 0
    for n, a in enumerate(args):
        if a[0] == "load":
            parts[n] = (a[2] if len(a) > 2 else 1, total)
            total += parts[n][0]
    stores = [n for n, o in enumerate(outs) if o[0] == "store"]
    puts = max(puts, len(stores))
    buffers = [pltpu.VMEM(args[n][1].shape, args[n][1].dtype) for n in parts] + [pltpu.VMEM(outs[n][1], outs[n][2]) for n in stores]
    sems = [pltpu.SemaphoreType.DMA((max(total, 1),)), pltpu.SemaphoreType.DMA((max(puts, 1),))]
    def run(*refs):
        ins, results, rest = list(refs[:n_in]), list(refs[n_in:n_in + n_out]), refs[n_in + n_out:]
        s = types.SimpleNamespace(**dict(zip(scratch, rest)))
        rest = rest[n_scratch:]
        hbm_in, hbm_out = dict(enumerate(ins)), dict(enumerate(results))
        for n, r in zip(parts, rest):
            ins[n] = r
        for n, r in zip(stores, rest[len(parts):]):
            results[n] = r
        memory = Memory(ins, results, rest[-2], rest[-1], hbm_in, hbm_out, parts)
        kernel(memory, s)
        for copy in memory.started:
            copy.wait()
    return pl.pallas_call(
        run, out_shape=tuple(jax.ShapeDtypeStruct(o[1], o[2]) for o in outs),
        in_specs=[spec[a[0]] for a in args], out_specs=tuple(spec[o[0]] for o in outs),
        scratch_shapes=[v if hasattr(v, "dtype") else pltpu.VMEM(*v) for v in scratch.values()] + buffers + sems,
        compiler_params=pltpu.CompilerParams(vmem_limit_bytes=62 << 20), name=name,
        cost_estimate=pl.CostEstimate(flops=flops, bytes_accessed=1 << 20, transcendentals=0))(*[a[1] for a in args])

def place_qkv(me, parts, wqkv):
    r = wqkv.shape[0] // len(parts)
    for x, p in enumerate(parts):
        wqkv[rows((me ^ x) * r, r), :] = p[...]

def place_rest(me, parts, wout, wup, wdown):
    r, rd = wout.shape[0] // len(parts), wdown.shape[0] // len(parts)
    for x, p in enumerate(parts):
        at = rows((me ^ x) * r, r)
        wout[at, :] = p[0:r, :]
        for c in range(wup.shape[1] // 256):
            wup[at, c * 256:(c + 1) * 256] = p[(c + 1) * r:(c + 2) * r, :]
        lo = r * (1 + wup.shape[1] // 256)
        wdown[rows((me ^ x) * rd, rd), :] = p[lo:lo + rd, :]

def hand_out(me, parts, mats, keep, send, wide):
    for x in range(parts):
        dst = send if x % 2 else keep
        lo = 0
        for m in mats:
            r = m.shape[0] // parts
            at = rows((me ^ x) * r, r)
            if wide:
                dst[x // 2] = m[at, :]
                continue
            for c in range(m.shape[1] // 256):
                dst[x // 2, lo:lo + r, :] = m[at, c * 256:(c + 1) * 256]
                lo += r

SAVED = ("e", "n1", "r1", "qs", "vp", "kt", "ht", "linv")

def first_attention(me, lengths, states, inject, qkv_parts, ff):
    t, d = states.shape
    nb, nc = t // BLK, t // CHUNK
    shapes = saved_shapes(t, d, ff)
    scratch = dict({k: v for k, v in shapes.items() if k not in SAVED}, mask=((nb, 2 * BLK, BLK), F32))
    def kernel(m, s):
        me_ref, len_ref, st, inj = m.ins[:4]
        m.start(*range(4, len(m.ins)))
        m.start(2, 3)
        vars(s).update(zip(SAVED, m.outs))
        wqkv = m.outs[-1]
        make_masks(len_ref, s.mask, nb)
        pad_zero(s)
        m.wait(*range(4, len(m.ins)))
        place_qkv(me_ref[0], m.ins[4:], wqkv)
        for j in range(nc):
            m.wait(2, 3, part=j)
            project(s, j, st[j * CHUNK:(j + 1) * CHUNK, :] + inj[j * CHUNK:(j + 1) * CHUNK, :], wqkv)
        for name in ("n1", "r1", "qs", "vp", "kt"):
            m.put(SAVED.index(name))
        m.put(len(SAVED))
        for i in range(0, nb, 2):
            attend(s, (i, i + 1), s.mask)
            m.put(SAVED.index("e"), i)
            m.put(SAVED.index("e"), i + 1)
        m.put(SAVED.index("ht"))
        m.put(SAVED.index("linv"))
    outs = [("store",) + shapes[k] for k in SAVED] + [("store", (d, 3 * d), BF)]
    args = [("smem", me), ("smem", lengths), ("load", states, nc), ("load", inject, nc)] + [("load", p) for p in qkv_parts]
    got = call(kernel, outs, args, scratch, "first_attention", FLOPS_FIRST, puts=len(SAVED) + nb)
    return dict(zip(SAVED, got)), got[-1]

def middle_part(me, lengths, counts, states, inject, cot, wqkv, ht, rest_parts, ff):
    t, d = states.shape
    nb, nc = t // BLK, t // CHUNK
    parts = len(rest_parts)
    sh = {"a_" + k: v for k, v in more_shapes(t, d, ff).items() if k != "dpk"}
    sh.update({"b_" + k: v for k, v in {**saved_shapes(t, d, ff), **more_shapes(t, d, ff)}.items()})
    sh.update(mask=((nb, 2 * BLK, BLK), F32), state=((t, d), F32), dk=((t + BLK, d), F32), dv=((t + BLK, d), F32),
              wqkv_t=((3 * d, d), BF), wup_t=((ff, d), BF), wdown_t=((d, ff), BF), tr=((2, d, t), BF),
              wup=((d, ff), BF), wdown=((ff, d), BF), mout=((d, d), BF), mup=((d, ff), BF), mdown_t=((d, ff), BF), mdown=((ff, d), BF))
    def kernel(m, x):
        me_ref, len_ref, cnt_ref, st, inj, ct, wqkv_ref, ht_ref = m.ins[:8]
        final, g, ginj, gm, wout, mqkv, keep, send = m.outs
        m.start(*range(8, len(m.ins)))
        m.start(7, 3, 4, 6, 5)
        its = [types.SimpleNamespace(**{k[2:]: v for k, v in vars(x).items() if k.startswith(p)}) for p in ("a_", "b_")]
        its[0].ht, its[0].gm = ht_ref, gm
        make_masks(len_ref, x.mask, nb)
        m.wait(*range(8, len(m.ins)))
        place_rest(me_ref[0], m.ins[8:], wout, x.wup, x.wdown)
        m.put(4)
        x.wup_t[...] = x.wup[...].T
        x.wdown_t[...] = x.wdown[...].T
        pad_zero(its[1])
        m.wait(3, 4, 6, 7)
        x.wqkv_t[...] = wqkv_ref[...].T
        def forward(s, src, dst):
            def chunk(j):
                at = rows(j * CHUNK, CHUNK)
                dst[at, :] = mlp(s, j, src[at, :] + inj[at, :], wout, x.wup, x.wdown)
            loop(nc, chunk)
        forward(its[0], st, x.state)
        loop(nc, lambda j: project(its[1], j, x.state[rows(j * CHUNK, CHUNK), :] + inj[rows(j * CHUNK, CHUNK), :], wqkv_ref))
        loop(nb // 2, lambda i: attend(its[1], (2 * i, 2 * i + 1), x.mask))
        forward(its[1], x.state, final)
        m.put(0)
        m.wait(5)
        def back_two(j):
            at = rows(j * CHUNK, CHUNK)
            g[at, :] = mlp_back(its[1], j, weigh(cnt_ref, len_ref, j, ct[at, :]), x.wdown_t, x.wup_t)
        loop(nc, back_two)
        x.dk[0:BLK, :] = jnp.zeros((BLK, d), F32)
        x.dv[0:BLK, :] = jnp.zeros((BLK, d), F32)
        loop(nb // 2, lambda i: attend_back(its[1], (2 * i, 2 * i + 1), wout, x.dk, x.dv))
        def back_one(j):
            at = rows(j * CHUNK, CHUNK)
            finish_packed(its[1], j, x.dk, x.dv)
            new = project_back(its[1], j, g[at, :], x.wqkv_t)
            ginj[at, :] = new
            g[at, :] = mlp_back(its[0], j, new, x.wdown_t, x.wup_t)
        loop(nc, back_one)
        for n in (1, 2, 3):
            m.put(n)
        def weight_grad(lefts, rights, dst):
            for n, left in enumerate(lefts):
                x.tr[n] = left[...].T
            def tile(c):
                cc = pl.ds(pl.multiple_of(c * 256, 256), 256)
                total = dot(x.tr[0], rights[0][:, cc])
                for n in range(1, len(rights)):
                    total = total + dot(x.tr[n], rights[n][:, cc])
                dst[:, cc] = total.astype(dst.dtype)
            loop(dst.shape[1] // 256, tile)
        weight_grad([s.g2 for s in its], [s.act for s in its], x.mdown_t)
        x.mdown[...] = x.mdown_t[...].T
        weight_grad([s.n2 for s in its], [s.dh for s in its], x.mup)
        weight_grad([its[1].n1], [its[1].dpk], mqkv)
        m.put(5)
        total = None
        for s in its:
            for b in range(nb):
                part = dot(s.ht[b], s.gm[b * BLK:(b + 1) * BLK, :])
                total = part if total is None else total + part
        x.mout[...] = total.astype(BF)
        hand_out(me_ref[0], parts, (x.mout, x.mup, x.mdown), keep, send, False)
        m.put(7)
        m.put(6)
    piece = ("store", (max(parts // 2, 1), (d + ff) // parts + ff // parts, d), BF)
    outs = [("store", (t, d), F32)] * 3 + [("store", (t, d), BF), ("store", (d, d), BF), ("store", (d, 3 * d), F32)] + [piece] * 2
    args = [("smem", me), ("smem", lengths), ("smem", counts)] + [("load", v) for v in (states, inject, cot, wqkv, ht, *rest_parts)]
    return call(kernel, outs, args, sh, "middle_part", 25 * 10 ** 9)

def last_part(me, saved, gm, wout, wqkv, mqkv, g, ginj, parts, ff, first):
    t, d = gm.shape
    nb, nc = t // BLK, t // CHUNK
    scratch = dict(dk=((t + BLK, d), F32), dv=((t + BLK, d), F32), tr=((d, t), BF), mat=((d, 3 * d), BF), wt=((3 * d, d), BF), dpk=((t, 3 * d), BF))
    def kernel(m, s):
        me_ref, s.gm, wout_ref, w_ref, m_ref, g_ref, gi_ref = m.ins[:7]
        vars(s).update(zip(SAVED, m.ins[7:]))
        keep, send, grad, grad_inject = m.outs
        at = {name: n + 7 for n, name in enumerate(SAVED)}
        head = [1, 2] + [at[k] for k in ("linv", "ht", "vp", "kt", "qs")]
        tail = [at["n1"], 3, 4, at["r1"], 5, 6]
        m.start(*head)
        m.start(at["e"])
        m.start(*tail)
        s.dk[0:BLK, :] = jnp.zeros((BLK, d), F32)
        s.dv[0:BLK, :] = jnp.zeros((BLK, d), F32)
        m.wait(*head)
        for i in range(0, nb, 2):
            m.wait(at["e"], part=i)
            m.wait(at["e"], part=i + 1)
            attend_back(s, (i, i + 1), wout_ref, s.dk, s.dv)
        m.wait(*tail)
        s.tr[...] = s.n1[...].T
        s.wt[...] = w_ref[...].T
        loop(nc, lambda j: finish_packed(s, j, s.dk, s.dv))
        def tile(c):
            cc = pl.ds(pl.multiple_of(c * 256, 256), 256)
            s.mat[:, cc] = (m_ref[:, cc] + dot(s.tr[...], s.dpk[:, cc])).astype(BF)
        loop(3, tile)
        hand_out(me_ref[0], parts, (s.mat,), keep, send, True)
        m.put(1)
        m.put(0)
        def chunk(j):
            at = rows(j * CHUNK, CHUNK)
            new = project_back(s, j, g_ref[at, :], s.wt)
            grad[at, :] = new
            grad_inject[at, :] = new + gi_ref[at, :]
        loop(nc, chunk)
        m.put(2)
        m.put(3)
    outs = [("store", (max(parts // 2, 1), d // parts, 3 * d), BF)] * 2 + [("store", (t, d), F32)] * 2
    args = [("smem", me)] + [("load", v) for v in (gm, wout, wqkv, mqkv, g, ginj)]
    args += [("load", saved[k], nb if k == "e" else 1) for k in SAVED] + [("any", v) for v in first]
    return call(kernel, outs, args, scratch, "last_part", FLOPS_LAST)

def to_column(row):
    n = row.shape[1]
    eye = lax.broadcasted_iota(jnp.int32, (n, n), 0) == lax.broadcasted_iota(jnp.int32, (n, n), 1)
    return jnp.sum(jnp.where(eye, jnp.broadcast_to(row, (n, n)), 0.0), axis=1, keepdims=True)

def to_row(column):
    n = column.shape[0]
    eye = lax.broadcasted_iota(jnp.int32, (n, n), 0) == lax.broadcasted_iota(jnp.int32, (n, n), 1)
    return jnp.sum(jnp.where(eye, jnp.broadcast_to(column, (n, n)), 0.0), axis=0, keepdims=True)

def pack_qkv(w_qkv, gain):
    def kernel(m, s):
        m.start()
        m.wait(0, 1)
        m.outs[0][...] = (m.ins[0][...].astype(F32) * to_column(m.ins[1][...].astype(F32))).astype(BF)
        m.put(0)
    return call(kernel, [("store", w_qkv.shape, BF)], [("load", w_qkv), ("load", gain.reshape(1, -1))], {}, "pack_qkv", 10 ** 6)[0]

def pack_rest(w_out, w_up, w_down, gain):
    r, d = w_out.shape
    n = w_up.shape[1] // d
    def kernel(m, s):
        out, up, down, g = m.ins[:4]
        m.start()
        m.wait(0, 1, 2, 3)
        m.outs[0][0:r, :] = out[...]
        col = to_column(g[...].astype(F32))
        for c in range(n):
            m.outs[0][(c + 1) * r:(c + 2) * r, :] = (up[:, c * d:(c + 1) * d].astype(F32) * col).astype(BF)
        m.outs[0][(n + 1) * r:, :] = down[...]
        m.put(0)
    args = [("load", v) for v in (w_out, w_up, w_down, gain.reshape(1, -1))]
    return call(kernel, [("store", ((n + 1) * r + w_down.shape[0], d), BF)], args, {}, "pack_rest", 10 ** 6)[0]

def sum_parts(parts, lo, size):
    acc = parts[0][lo:lo + size, :].astype(F32)
    for p in parts[1:]:
        acc = acc + p[lo:lo + size, :].astype(F32)
    return acc

def finished(shares, weight, gain, lead, tail):
    r, cols = weight.shape
    d = shares[0].shape[1]
    n = cols // d
    def kernel(m, s):
        m.start()
        m.wait(*range(len(m.ins)))
        w, g, parts = m.ins[0], to_column(m.ins[1][...].astype(F32)), m.ins[2:]
        along = jnp.zeros((r, 1), F32)
        for c in range(n):
            v = sum_parts(parts, lead + c * r, r)
            m.outs[0][:, c * d:(c + 1) * d] = v * g
            along = along + jnp.sum(v * w[:, c * d:(c + 1) * d].astype(F32), axis=1, keepdims=True)
        m.put(0)
        m.outs[1][...] = to_row(along)
        m.put(1)
        m.outs[2][...] = sum_parts(parts, 0, lead)
        m.outs[3][...] = sum_parts(parts, lead + n * r, tail)
        m.put(2)
        m.put(3)
    outs = [("store", (r, cols), F32), ("store", (1, r), F32), ("store", (lead, d), F32), ("store", (tail, d), F32)]
    got = call(kernel, outs, [("load", weight), ("load", gain.reshape(1, -1))] + [("load", v) for v in shares], {}, "finished", 10 ** 6)
    return [got[0], got[1].reshape(r)] + list(got[2:])

def after(values, *others):
    return lax.optimization_barrier((values, others))[0]

def exchange(x, axis, size, step):
    return lax.ppermute(x, axis, [(i, i ^ step) for i in range(size)])

def far_parts(x, size):
    return [x] + [exchange(x, "fsdp", size, 2 * k) for k in range(1, size // 2)]

def with_near(far, size):
    return [v for x in far for v in (x, exchange(x, "fsdp", size, 1))]

def sum_near(keep, near, then):
    total = keep.astype(F32) + near.astype(F32) + then
    return [total[k].astype(BF) for k in range(keep.shape[0])]

def send_far(summed, size):
    return [exchange(summed[k], "fsdp", size, 2 * k) for k in range(1, size // 2)]

def nothing(value):
    return jnp.minimum(jnp.abs(value[(0,) * value.ndim].astype(F32)), 0.0)

def along_dp(share, size):
    return [share] + [exchange(share, "dp", size, k) for k in range(1, size)]

def send_near(pieces, size):
    return [exchange(p, "fsdp", size, 1) for p in pieces[1::2]]

def send_far(summed, size):
    return [exchange(summed[k], "fsdp", size, 2 * k) for k in range(1, size // 2)]

def reduce_whole(whole, sizes):
    out, lo = [], 0
    for n in sizes:
        share = lax.psum_scatter(whole[lo:lo + n], "fsdp", scatter_dimension=0, tiled=True)
        out.append(lax.psum(share, "dp").astype(F32))
        lo += n
    return jnp.concatenate(out, axis=0)

def on_device(n_dp, n_fsdp, states, inject, ln1_gain, w_qkv, w_out, ln2_gain, w_up, w_down, prompt_lengths, loop_counts, cotangent):
    d = states.shape[1]
    r, ff = w_up.shape
    direct = r % 16 == 0
    if direct:
        me = lax.axis_index("fsdp").astype(jnp.int32).reshape(1)
        qkv_far = far_parts(pack_qkv(w_qkv, ln1_gain), n_fsdp)
        rest_far = far_parts(pack_rest(w_out, w_up, w_down, ln2_gain), n_fsdp)
        qkv_parts = with_near(qkv_far, n_fsdp)
    else:
        me = jnp.zeros((1,), jnp.int32)
        full = lambda v: lax.all_gather(v, "fsdp", axis=0, tiled=True)
        up = full((w_up.astype(F32) * ln2_gain.astype(F32)[:, None]).astype(BF))
        qkv_parts = [full((w_qkv.astype(F32) * ln1_gain.astype(F32)[:, None]).astype(BF))]
        rest_parts = [jnp.concatenate([full(w_out)] + [up[:, c:c + d] for c in range(0, ff, d)] + [full(w_down)], axis=0)]
    parts = len(qkv_parts)
    saved, wqkv = first_attention(me, prompt_lengths, states, inject, qkv_parts, ff)
    if direct:
        rest_parts = with_near(after(rest_far, wqkv), n_fsdp)
    final, g, ginj, gm, wout, mqkv, keep, send = middle_part(
        me, prompt_lengths, loop_counts, states, inject, cotangent, wqkv, saved["ht"], rest_parts, ff)
    summed = []
    if direct:
        summed = sum_near(keep, exchange(send, "fsdp", n_fsdp, 1), 0.0)
        far = send_far(summed, n_fsdp)
    else:
        shares = [reduce_whole(keep[0], [d] * (1 + ff // d) + [ff])]
    keep_qkv, send_qkv, grad_states, grad_inject = last_part(me, saved, gm, wout, wqkv, mqkv, g, ginj, parts, ff, summed)
    if direct:
        near = exchange(send_qkv, "fsdp", n_fsdp, 1)
        share = (sum_parts([summed[0], *far], 0, summed[0].shape[0]) + nothing(keep_qkv)).astype(BF)
        shares = along_dp(share, n_dp)
        summed = sum_near(keep_qkv, near, nothing(share))
        shares_qkv = along_dp(sum_parts([summed[0], *send_far(summed, n_fsdp)], 0, r).astype(BF), n_dp)
    else:
        shares_qkv = [reduce_whole(keep_qkv[0], [d])]
    d_up, d_gain_two, d_out, d_down = finished(shares, w_up, ln2_gain, r, w_down.shape[0])
    m_qkv = sum_parts(shares_qkv, 0, r)
    d_qkv = m_qkv * ln1_gain.astype(F32)[:, None]
    d_gain_one = jnp.sum(m_qkv * w_qkv.astype(F32), axis=1)
    return (final, grad_states, grad_inject, d_gain_one, d_qkv, d_out, d_gain_two, d_up, d_down)

def solution(mesh):
    tok, vec, mat = P(("dp", "fsdp"), None), P("fsdp"), P("fsdp", None)
    return jax.shard_map(
        functools.partial(on_device, mesh.shape["dp"], mesh.shape["fsdp"]), mesh=mesh,
        in_specs=(tok, tok, vec, mat, mat, vec, mat, mat, tok, tok, tok),
        out_specs=(tok, tok, tok, vec, mat, mat, vec, mat, mat), check_vma=False)
```

time: 149 us -> 106 us (0.71)
  waiting for transfers between devices: 38.2 us -> 7.16 us
  Pallas kernels: 72.7 us -> 57.2 us
  starting transfers between devices: 24.5 us -> 30.7 us
  other arithmetic: 6.76 us -> 3.65 us
    ppermute x21 -> x28, waiting for transfers between devices: 38.2 us -> 7.16 us  [exchange(): return lax.ppermute(x, axis, [(i, i ^ step) for i in range(size)])]
    pallas_call x1 -> x6, Pallas kernels: 72.7 us -> 57.2 us  [call(): pl.pallas_call(run, out_shape=tuple((jax.ShapeDtypeStruct(o[1], o[2]) for...]
    ppermute x21 -> x28, starting transfers between devices: 24.5 us -> 30.7 us  [exchange(): return lax.ppermute(x, axis, [(i, i ^ step) for i in range(size)])]
    convert_element_type x6 -> x3, other arithmetic: 3.97 us -> 0.12 us  [the longest x1 0.09 us: on_device(): (sum_parts([summed[0], *far], 0, summed[0].shape[0]) + nothing(keep_qkv))...]
    another operation x0 -> x2, other arithmetic: none -> 2.2 us
    unnamed x53 -> x48, local copies, waits for them, and re-layouts: 4.63 us -> 2.54 us
  transfers between devices with their start and end apart: 21 -> 28, of which waited for: 13 -> 10; matrix products, arithmetic and copies ran while one was open for 0% -> 2% of each run, Pallas kernels for 0% -> 21%
where the time goes in v2:
time: 106 us
  Pallas kernels  57.2 us (54%)
  starting transfers between devices  30.7 us (29%)
  waiting for transfers between devices  7.16 us (7%)
  local copies, waits for them, and re-layouts  4.95 us (5%)
  other arithmetic  3.65 us (3%)
  between operations  2.24 us (2%)
    pallas_call x6, Pallas kernels, call(): pl.pallas_call(run, out_shape=tuple((jax.ShapeDtypeStruct(o[1], o[2]) for...  57.2 us
    ppermute x28, starting transfers between devices, exchange(): return lax.ppermute(x, axis, [(i, i ^ step) for i in range(size)])  30.7 us
    ppermute x28, waiting for transfers between devices, exchange(): return lax.ppermute(x, axis, [(i, i ^ step) for i in range(size)])  7.16 us
    unnamed x48, local copies, waits for them, and re-layouts  2.54 us
    another operation x2, other arithmetic  2.2 us
  transfers between devices with their start and end apart: 28, of which 10 were waited for; matrix products, arithmetic and copies ran while one was open for 2% of the time, Pallas kernels for 21%

profile of v2, /device:TPU:0, one launch (start us, length us, event | category | flops | bytes accessed | tf_op | source)
XLA Modules:
  0.0 105.8 jit_solution(6370847390570031944)
XLA Ops:
  0.6 1.5 %pack_qkv.1.refs_4_ = bf16[32,768]{1,0:T(8,128)(2,1)} custom-call(bf16[32,768]{1,0:T(8,128)(2,1)} %refs_0_.3, bf16[1,32]{1,0:T(2,128)(2,1)} %bitcast.29), custom_call_target="tpu_custom_call" | custom-call | flops 1000000 | bytes 1048576 | tf_op jit(solution)/shard_map/pack_qkv/pallas_call | solution.py:313
  2.2 3.1 %collective-permute-start.1 = (bf16[32,768]{1,0:T(8,128)(2,1)}, bf16[32,768]{1,0:T(8,128)(2,1)S(1)}, u32[]{:S(2)}, u32[]{:S(2)}) collective-permute-start(bf16[32,768]{1,0:T(8,128)(2,1)} %pack_qkv.1.refs_4_), channel_id=1, source_target_pairs={{0,2},{1,3},{2,0},{3,1},{4,6},{5,7},{6,4},{7,5},{8,10},{9,11},{10,... | collective-permute-start | bytes 147464 | tf_op jit(solution)/shard_map/ppermute | solution.py:577
  5.3 2.6 %collective-permute-start.3 = (bf16[32,768]{1,0:T(8,128)(2,1)}, bf16[32,768]{1,0:T(8,128)(2,1)S(1)}, u32[]{:S(2)}, u32[]{:S(2)}) collective-permute-start(bf16[32,768]{1,0:T(8,128)(2,1)} %pack_qkv.1.refs_4_), channel_id=1, source_target_pairs={{0,4},{1,5},{2,6},{3,7},{4,0},{5,1},{6,2},{7,3},{8,12},{9,13},{10,... | collective-permute-start | bytes 147464 | tf_op jit(solution)/shard_map/ppermute | solution.py:577
  8.2 1.7 %pack_rest.1.refs_8_ = bf16[288,256]{1,0:T(8,128)(2,1)} custom-call(bf16[32,256]{1,0:T(8,128)(2,1)} %refs_0_.4, bf16[32,1024]{1,0:T(8,128)(2,1)} %refs_0_.5, bf16[128,256]{1,0:T(8,128)(2,1)} %refs_2_.4, bf16[1,32]{1,0:T(2,128)(2,1)} %bitcast.27), custom_call_target="tpu_custom_call" | custom-call | flops 1000000 | bytes 1048576 | tf_op jit(solution)/shard_map/pack_rest/pallas_call | solution.py:313
  9.8 1.5 %collective-permute-start.7 = (bf16[288,256]{1,0:T(8,128)(2,1)}, bf16[288,256]{1,0:T(8,128)(2,1)S(1)}, u32[]{:S(2)}, u32[]{:S(2)}) collective-permute-start(bf16[288,256]{1,0:T(8,128)(2,1)} %pack_rest.1.refs_8_), channel_id=1, source_target_pairs={{0,2},{1,3},{2,0},{3,1},{4,6},{5,7},{6,4},{7,5},{8,10},{9,11},{10,... | collective-permute-start | bytes 442376 | tf_op jit(solution)/shard_map/ppermute | solution.py:577
  11.3 2.7 %collective-permute-start.8 = (bf16[288,256]{1,0:T(8,128)(2,1)}, bf16[288,256]{1,0:T(8,128)(2,1)S(1)}, u32[]{:S(2)}, u32[]{:S(2)}) collective-permute-start(bf16[288,256]{1,0:T(8,128)(2,1)} %pack_rest.1.refs_8_), channel_id=1, source_target_pairs={{0,4},{1,5},{2,6},{3,7},{4,0},{5,1},{6,2},{7,3},{8,12},{9,13},{10,... | collective-permute-start | bytes 442376 | tf_op jit(solution)/shard_map/ppermute | solution.py:577
  14.0 1.5 %collective-permute-start.9 = (bf16[288,256]{1,0:T(8,128)(2,1)}, bf16[288,256]{1,0:T(8,128)(2,1)S(1)}, u32[]{:S(2)}, u32[]{:S(2)}) collective-permute-start(bf16[288,256]{1,0:T(8,128)(2,1)} %pack_rest.1.refs_8_), channel_id=1, source_target_pairs={{0,6},{1,7},{2,4},{3,5},{4,2},{5,3},{6,0},{7,1},{8,14},{9,15},{10,... | collective-permute-start | bytes 442376 | tf_op jit(solution)/shard_map/ppermute | solution.py:577
  17.5 7.4 %first_attention.1 = (bf16[8,4,256,256]{3,2,1,0:T(8,128)(2,1)}, bf16[1024,256]{1,0:T(8,128)(2,1)}, f32[1024,128]{1,0:T(8,128)}, bf16[1024,256]{1,0:T(8,128)(2,1)...) custom-call(s32[1]{0:T(128)} %bitcast.refs_0_, ...), custom_call_target="tpu_custom_call" | custom-call | flops 1000000000 | bytes 1048576 | tf_op jit(solution)/shard_map/first_attention/pallas_call | solution.py:313
  28.3 33.2 %middle_part.1 = (f32[1024,256]{1,0:T(8,128)}, f32[1024,256]{1,0:T(8,128)}, f32[1024,256]{1,0:T(8,128)}, bf16[1024,256]{1,0:T(8,128)(2,1)}, bf16[256,256]{1,0:T(...) custom-call(s32[1]{0:T(128)} %bitcast.refs_0_, s32[1,16]{1,0:T(1,128)} %refs_1_.5, ...), custom_call_target="tpu_custom_call" | custom-call | flops 24999999488 | bytes 1048576 | tf_op jit(solution)/shard_map/middle_part/pallas_call | solution.py:313
  61.9 1.9 %collective-permute-done.14 = bf16[4,288,256]{2,1,0:T(8,128)(2,1)S(1)} collective-permute-done((bf16[4,288,256]{2,1,0:T(8,128)(2,1)}, bf16[4,288,256]{2,1,0:T(8,128)(2,1)S(1)}, u32[]{:S(2)}, u32[]{:S(2)}) %collective-permute-start.14) | collective-permute-done | bytes 589856 | tf_op jit(solution)/shard_map/ppermute | solution.py:577
  63.8 1.2 %add_convert_fusion = bf16[4,288,256]{2,1,0:T(8,128)(2,1)S(1)} fusion(bf16[4,288,256]{2,1,0:T(8,128)(2,1)S(1)} %collective-permute-done.14, bf16[4,288,256]{2,1,0:T(8,128)(2,1)} %get-tuple-element.57), kind=kLoop, calls=%fused_computation | loop fusion | flops 1179648 | bytes 1769472 | tf_op jit(solution)/shard_map/convert.8
  65.7 2.8 %collective-permute-start.18 = (bf16[288,256]{1,0:T(8,128)(2,1)S(1)}, bf16[288,256]{1,0:T(8,128)(2,1)S(1)}, u32[]{:S(2)}, u32[]{:S(2)}) collective-permute-start(bf16[288,256]{1,0:T(8,128)(2,1)S(1)} %get-tuple-element.67.refs_18_), channel_id=1, source_target_pairs={{0,6},{1,7},{2,4},{3,5},{4,2},{5,3},{6,0},{7,1},{8,14},{9,15},{10,... | collective-permute-start | bytes 442376 | tf_op jit(solution)/shard_map/ppermute | solution.py:577
  68.6 1.6 %collective-permute-start.17 = (bf16[288,256]{1,0:T(8,128)(2,1)S(1)}, bf16[288,256]{1,0:T(8,128)(2,1)S(1)}, u32[]{:S(2)}, u32[]{:S(2)}) collective-permute-start(bf16[288,256]{1,0:T(8,128)(2,1)S(1)} %get-tuple-element.68.refs_17_), channel_id=1, source_target_pairs={{0,4},{1,5},{2,6},{3,7},{4,0},{5,1},{6,2},{7,3},{8,12},{9,13},{10,... | collective-permute-start | bytes 442376 | tf_op jit(solution)/shard_map/ppermute | solution.py:577
  70.6 11.2 %last_part.1 = (bf16[4,32,768]{2,1,0:T(8,128)(2,1)}, bf16[4,32,768]{2,1,0:T(8,128)(2,1)}, f32[1024,256]{1,0:T(8,128)}, f32[1024,256]{1,0:T(8,128)}) custom-call(s32[1]{0:T(128)} %bitcast.refs_0_, bf16[1024,256]{1,0:T(8,128)(2,1)} %get-tuple-element.45.refs_1_, bf16[256,256]{1,0:T(8,128)(2,1)} %get-tuple-element.46.refs_2_, ...), custom_call_target="tpu_custom_call" | custom-call | flops 10000000000 | bytes 1048576 | tf_op jit(solution)/shard_map/last_part/pallas_call | solution.py:313
  81.9 1.1 %slice.42 = bf16[1,1,1]{2,1,0:T(2,128)(2,1)} slice(bf16[4,32,768]{2,1,0:T(8,128)(2,1)} %get-tuple-element.61), slice={[0:1], [0:1], [0:1]} | slice | bytes 4 | tf_op jit(solution)/shard_map/slice | solution.py:593
  86.1 2.4 %collective-permute-start.21 = (bf16[32,768]{1,0:T(8,128)(2,1)S(1)}, bf16[32,768]{1,0:T(8,128)(2,1)S(1)}, u32[]{:S(2)}, u32[]{:S(2)}) collective-permute-start(bf16[32,768]{1,0:T(8,128)(2,1)S(1)} %get-tuple-element.74), channel_id=1, source_target_pairs={{0,6},{1,7},{2,4},{3,5},{4,2},{5,3},{6,0},{7,1},{8,14},{9,15},{10,... | collective-permute-start | bytes 147464 | tf_op jit(solution)/shard_map/ppermute | solution.py:577
  89.3 1.3 %collective-permute-start.19 = (bf16[32,768]{1,0:T(8,128)(2,1)S(1)}, bf16[32,768]{1,0:T(8,128)(2,1)S(1)}, u32[]{:S(2)}, u32[]{:S(2)}) collective-permute-start(bf16[32,768]{1,0:T(8,128)(2,1)S(1)} %get-tuple-element.73), channel_id=1, source_target_pairs={{0,2},{1,3},{2,0},{3,1},{4,6},{5,7},{6,4},{7,5},{8,10},{9,11},{10,... | collective-permute-start | bytes 147464 | tf_op jit(solution)/shard_map/ppermute | solution.py:577
  90.5 1.5 %collective-permute-start.25 = (bf16[288,256]{1,0:T(8,128)(2,1)S(1)}, bf16[288,256]{1,0:T(8,128)(2,1)S(1)}, u32[]{:S(2)}, u32[]{:S(2)}) collective-permute-start(bf16[288,256]{1,0:T(8,128)(2,1)S(1)} %add_convert_fusion.2.refs_2_), channel_id=1, source_target_pairs={{0,8},{8,0},{16,24},{24,16},{1,9},{9,1},{17,25},{25,17},{2,10},{10... | collective-permute-start | bytes 442376 | tf_op jit(solution)/shard_map/ppermute | solution.py:577
  92.1 1.5 %collective-permute-start.26 = (bf16[288,256]{1,0:T(8,128)(2,1)S(1)}, bf16[288,256]{1,0:T(8,128)(2,1)S(1)}, u32[]{:S(2)}, u32[]{:S(2)}) collective-permute-start(bf16[288,256]{1,0:T(8,128)(2,1)S(1)} %add_convert_fusion.2.refs_2_), channel_id=1, source_target_pairs={{0,16},{8,24},{16,0},{24,8},{1,17},{9,25},{17,1},{25,9},{2,18},{10... | collective-permute-start | bytes 442376 | tf_op jit(solution)/shard_map/ppermute | solution.py:577
  93.6 1.1 %collective-permute-start.27 = (bf16[288,256]{1,0:T(8,128)(2,1)S(1)}, bf16[288,256]{1,0:T(8,128)(2,1)S(1)}, u32[]{:S(2)}, u32[]{:S(2)}) collective-permute-start(bf16[288,256]{1,0:T(8,128)(2,1)S(1)} %add_convert_fusion.2.refs_2_), channel_id=1, source_target_pairs={{0,24},{8,16},{16,8},{24,0},{1,25},{9,17},{17,9},{25,1},{2,26},{10... | collective-permute-start | bytes 442376 | tf_op jit(solution)/shard_map/ppermute | solution.py:577
  94.8 2.4 %collective-permute-start.24 = (bf16[32,768]{1,0:T(8,128)(2,1)S(1)}, bf16[32,768]{1,0:T(8,128)(2,1)S(1)}, u32[]{:S(2)}, u32[]{:S(2)}) collective-permute-start(bf16[32,768]{1,0:T(8,128)(2,1)S(1)} %fusion.2), channel_id=1, source_target_pairs={{0,24},{8,16},{16,8},{24,0},{1,25},{9,17},{17,9},{25,1},{2,26},{10... | collective-permute-start | bytes 147464 | tf_op jit(solution)/shard_map/ppermute | solution.py:577
  98.3 2.7 %collective-permute-done.26.refs_4_ = bf16[288,256]{1,0:T(8,128)(2,1)S(1)} collective-permute-done((bf16[288,256]{1,0:T(8,128)(2,1)S(1)}, bf16[288,256]{1,0:T(8,128)(2,1)S(1)}, u32[]{:S(2)}, u32[]{:S(2)}) %collective-permute-start.26) | collective-permute-done | bytes 147488 | tf_op jit(solution)/shard_map/ppermute | solution.py:577
  102.3 2.1 %finished.1 = (f32[32,1024]{1,0:T(8,128)}, f32[1,32]{1,0:T(1,128)}, f32[32,256]{1,0:T(8,128)}, f32[128,256]{1,0:T(8,128)}) custom-call(bf16[32,1024]{1,0:T(8,128)(2,1)} %refs_0_.5, bf16[1,32]{1,0:T(2,128)(2,1)} %bitcast.28, bf16[288,256]{1,0:T(8,128)(2,1)} %copy-done, bf16[288,256]{1,0:T(8,128)(2,1)} %copy-done.6, bf16[288,256]{1,0:T(8,128)(2,1)} %copy-done.7, ...), custom_call_target="tpu_custom_call" | custom-call | flops 1000000 | bytes 1048576 | tf_op jit(solution)/shard_map/finished/pallas_call | solution.py:313
  104.5 1.3 %broadcast_multiply_fusion = (f32[32,768]{1,0:T(8,128)}, f32[32]{0:T(128)}) fusion(f32[32]{0:T(128)S(1)} %convert_element_type.126, bf16[32,768]{1,0:T(8,128)(2,1)S(1)} %collective-permute-done.24, bf16[32,768]{1,0:T(8,128)(2,1)S(1)} %collective-permute-done.23, bf16[32,768]{1,0:T(8,128)(2,1)S(1)} %collective-permute-done.22, bf16[32,768]{1,0:T(8,128)(2,1)S(1)} %fusion.2, ...), kind=kLoop, calls=%fused_computation.17 | loop fusion | flops 270304 | bytes 344320 | tf_op jit(solution)/shard_map/mul | solution.py:650
  (96 shorter events, 12.0 us)
Async XLA Ops:
  2.2 5.7 %collective-permute-start.1 = (bf16[32,768]{1,0:T(8,128)(2,1)}, bf16[32,768]{1,0:T(8,128)(2,1)S(1)}, u32[]{:S(2)}, u32[]{:S(2)}) collective-permute-start(bf16[32,768]{1,0:T(8,128)(2,1)} %pack_qkv.1.refs_4_), channel_id=1, source_target_pairs={{0,2},{1,3},{2,0},{3,1},{4,6},{5,7},{6,4},{7,5},{8,10},{9,11},{10,... | collective-permute-start | bytes 147464 | tf_op jit(solution)/shard_map/ppermute | solution.py:577
  5.3 6.1 %collective-permute-start = (bf16[32,768]{1,0:T(8,128)(2,1)}, bf16[32,768]{1,0:T(8,128)(2,1)S(1)}, u32[]{:S(2)}, u32[]{:S(2)}) collective-permute-start(bf16[32,768]{1,0:T(8,128)(2,1)} %pack_qkv.1.refs_4_), channel_id=1, source_target_pairs={{0,1},{1,0},{2,3},{3,2},{4,5},{5,4},{6,7},{7,6},{8,9},{9,8},{10,11... | collective-permute-start | bytes 147464 | tf_op jit(solution)/shard_map/ppermute | solution.py:577
  5.3 8.8 %collective-permute-start.3 = (bf16[32,768]{1,0:T(8,128)(2,1)}, bf16[32,768]{1,0:T(8,128)(2,1)S(1)}, u32[]{:S(2)}, u32[]{:S(2)}) collective-permute-start(bf16[32,768]{1,0:T(8,128)(2,1)} %pack_qkv.1.refs_4_), channel_id=1, source_target_pairs={{0,4},{1,5},{2,6},{3,7},{4,0},{5,1},{6,2},{7,3},{8,12},{9,13},{10,... | collective-permute-start | bytes 147464 | tf_op jit(solution)/shard_map/ppermute | solution.py:577
  7.9 7.6 %collective-permute-start.5 = (bf16[32,768]{1,0:T(8,128)(2,1)}, bf16[32,768]{1,0:T(8,128)(2,1)S(1)}, u32[]{:S(2)}, u32[]{:S(2)}) collective-permute-start(bf16[32,768]{1,0:T(8,128)(2,1)} %pack_qkv.1.refs_4_), channel_id=1, source_target_pairs={{0,6},{1,7},{2,4},{3,5},{4,2},{5,3},{6,0},{7,1},{8,14},{9,15},{10,... | collective-permute-start | bytes 147464 | tf_op jit(solution)/shard_map/ppermute | solution.py:577
  7.9 7.6 %collective-permute-start.2 = (bf16[32,768]{1,0:T(8,128)(2,1)S(1)}, bf16[32,768]{1,0:T(8,128)(2,1)S(1)}, u32[]{:S(2)}, u32[]{:S(2)}) collective-permute-start(bf16[32,768]{1,0:T(8,128)(2,1)S(1)} %collective-permute-done.1.refs_6_), channel_id=1, source_target_pairs={{0,1},{1,0},{2,3},{3,2},{4,5},{5,4},{6,7},{7,6},{8,9},{9,8},{10,11... | collective-permute-start | bytes 147464 | tf_op jit(solution)/shard_map/ppermute | solution.py:577
  9.8 15.1 %collective-permute-start.7 = (bf16[288,256]{1,0:T(8,128)(2,1)}, bf16[288,256]{1,0:T(8,128)(2,1)S(1)}, u32[]{:S(2)}, u32[]{:S(2)}) collective-permute-start(bf16[288,256]{1,0:T(8,128)(2,1)} %pack_rest.1.refs_8_), channel_id=1, source_target_pairs={{0,2},{1,3},{2,0},{3,1},{4,6},{5,7},{6,4},{7,5},{8,10},{9,11},{10,... | collective-permute-start | bytes 442376 | tf_op jit(solution)/shard_map/ppermute | solution.py:577
  11.3 14.2 %collective-permute-start.8 = (bf16[288,256]{1,0:T(8,128)(2,1)}, bf16[288,256]{1,0:T(8,128)(2,1)S(1)}, u32[]{:S(2)}, u32[]{:S(2)}) collective-permute-start(bf16[288,256]{1,0:T(8,128)(2,1)} %pack_rest.1.refs_8_), channel_id=1, source_target_pairs={{0,4},{1,5},{2,6},{3,7},{4,0},{5,1},{6,2},{7,3},{8,12},{9,13},{10,... | collective-permute-start | bytes 442376 | tf_op jit(solution)/shard_map/ppermute | solution.py:577
  14.0 11.5 %collective-permute-start.9 = (bf16[288,256]{1,0:T(8,128)(2,1)}, bf16[288,256]{1,0:T(8,128)(2,1)S(1)}, u32[]{:S(2)}, u32[]{:S(2)}) collective-permute-start(bf16[288,256]{1,0:T(8,128)(2,1)} %pack_rest.1.refs_8_), channel_id=1, source_target_pairs={{0,6},{1,7},{2,4},{3,5},{4,2},{5,3},{6,0},{7,1},{8,14},{9,15},{10,... | collective-permute-start | bytes 442376 | tf_op jit(solution)/shard_map/ppermute | solution.py:577
  25.6 1.6 %collective-permute-start.11 = (bf16[288,256]{1,0:T(8,128)(2,1)S(1)}, bf16[288,256]{1,0:T(8,128)(2,1)S(1)}, u32[]{:S(2)}, u32[]{:S(2)}) collective-permute-start(bf16[288,256]{1,0:T(8,128)(2,1)S(1)} %collective-permute-done.7.refs_10_), channel_id=1, source_target_pairs={{0,1},{1,0},{2,3},{3,2},{4,5},{5,4},{6,7},{7,6},{8,9},{9,8},{10,11... | collective-permute-start | bytes 442376 | tf_op jit(solution)/shard_map/ppermute | solution.py:577
  26.2 1.5 %collective-permute-start.13 = (bf16[288,256]{1,0:T(8,128)(2,1)S(1)}, bf16[288,256]{1,0:T(8,128)(2,1)S(1)}, u32[]{:S(2)}, u32[]{:S(2)}) collective-permute-start(bf16[288,256]{1,0:T(8,128)(2,1)S(1)} %collective-permute-done.9.refs_14_), channel_id=1, source_target_pairs={{0,1},{1,0},{2,3},{3,2},{4,5},{5,4},{6,7},{7,6},{8,9},{9,8},{10,11... | collective-permute-start | bytes 442376 | tf_op jit(solution)/shard_map/ppermute | solution.py:577
  61.5 2.3 %collective-permute-start.14 = (bf16[4,288,256]{2,1,0:T(8,128)(2,1)}, bf16[4,288,256]{2,1,0:T(8,128)(2,1)S(1)}, u32[]{:S(2)}, u32[]{:S(2)}) collective-permute-start(bf16[4,288,256]{2,1,0:T(8,128)(2,1)} %get-tuple-element.58), channel_id=1, source_target_pairs={{0,1},{1,0},{2,3},{3,2},{4,5},{5,4},{6,7},{7,6},{8,9},{9,8},{10,11... | collective-permute-start | bytes 1769480 | tf_op jit(solution)/shard_map/ppermute | solution.py:577
  65.7 18.0 %collective-permute-start.18 = (bf16[288,256]{1,0:T(8,128)(2,1)S(1)}, bf16[288,256]{1,0:T(8,128)(2,1)S(1)}, u32[]{:S(2)}, u32[]{:S(2)}) collective-permute-start(bf16[288,256]{1,0:T(8,128)(2,1)S(1)} %get-tuple-element.67.refs_18_), channel_id=1, source_target_pairs={{0,6},{1,7},{2,4},{3,5},{4,2},{5,3},{6,0},{7,1},{8,14},{9,15},{10,... | collective-permute-start | bytes 442376 | tf_op jit(solution)/shard_map/ppermute | solution.py:577
  68.6 15.2 %collective-permute-start.17 = (bf16[288,256]{1,0:T(8,128)(2,1)S(1)}, bf16[288,256]{1,0:T(8,128)(2,1)S(1)}, u32[]{:S(2)}, u32[]{:S(2)}) collective-permute-start(bf16[288,256]{1,0:T(8,128)(2,1)S(1)} %get-tuple-element.68.refs_17_), channel_id=1, source_target_pairs={{0,4},{1,5},{2,6},{3,7},{4,0},{5,1},{6,2},{7,3},{8,12},{9,13},{10,... | collective-permute-start | bytes 442376 | tf_op jit(solution)/shard_map/ppermute | solution.py:577
  70.2 13.5 %collective-permute-start.16 = (bf16[288,256]{1,0:T(8,128)(2,1)S(1)}, bf16[288,256]{1,0:T(8,128)(2,1)S(1)}, u32[]{:S(2)}, u32[]{:S(2)}) collective-permute-start(bf16[288,256]{1,0:T(8,128)(2,1)S(1)} %get-tuple-element.69.refs_16_), channel_id=1, source_target_pairs={{0,2},{1,3},{2,0},{3,1},{4,6},{5,7},{6,4},{7,5},{8,10},{9,11},{10,... | collective-permute-start | bytes 442376 | tf_op jit(solution)/shard_map/ppermute | solution.py:577
  81.8 3.2 %collective-permute-start.15 = (bf16[4,32,768]{2,1,0:T(8,128)(2,1)}, bf16[4,32,768]{2,1,0:T(8,128)(2,1)S(1)}, u32[]{:S(2)}, u32[]{:S(2)}) collective-permute-start(bf16[4,32,768]{2,1,0:T(8,128)(2,1)} %get-tuple-element.62), channel_id=1, source_target_pairs={{0,1},{1,0},{2,3},{3,2},{4,5},{5,4},{6,7},{7,6},{8,9},{9,8},{10,11... | collective-permute-start | bytes 589832 | tf_op jit(solution)/shard_map/ppermute | solution.py:577
  86.1 7.5 %collective-permute-start.21 = (bf16[32,768]{1,0:T(8,128)(2,1)S(1)}, bf16[32,768]{1,0:T(8,128)(2,1)S(1)}, u32[]{:S(2)}, u32[]{:S(2)}) collective-permute-start(bf16[32,768]{1,0:T(8,128)(2,1)S(1)} %get-tuple-element.74), channel_id=1, source_target_pairs={{0,6},{1,7},{2,4},{3,5},{4,2},{5,3},{6,0},{7,1},{8,14},{9,15},{10,... | collective-permute-start | bytes 147464 | tf_op jit(solution)/shard_map/ppermute | solution.py:577
  88.5 6.2 %collective-permute-start.20 = (bf16[32,768]{1,0:T(8,128)(2,1)S(1)}, bf16[32,768]{1,0:T(8,128)(2,1)S(1)}, u32[]{:S(2)}, u32[]{:S(2)}) collective-permute-start(bf16[32,768]{1,0:T(8,128)(2,1)S(1)} %get-tuple-element.75), channel_id=1, source_target_pairs={{0,4},{1,5},{2,6},{3,7},{4,0},{5,1},{6,2},{7,3},{8,12},{9,13},{10,... | collective-permute-start | bytes 147464 | tf_op jit(solution)/shard_map/ppermute | solution.py:577
  89.3 5.5 %collective-permute-start.19 = (bf16[32,768]{1,0:T(8,128)(2,1)S(1)}, bf16[32,768]{1,0:T(8,128)(2,1)S(1)}, u32[]{:S(2)}, u32[]{:S(2)}) collective-permute-start(bf16[32,768]{1,0:T(8,128)(2,1)S(1)} %get-tuple-element.73), channel_id=1, source_target_pairs={{0,2},{1,3},{2,0},{3,1},{4,6},{5,7},{6,4},{7,5},{8,10},{9,11},{10,... | collective-permute-start | bytes 147464 | tf_op jit(solution)/shard_map/ppermute | solution.py:577
  90.5 7.2 %collective-permute-start.25 = (bf16[288,256]{1,0:T(8,128)(2,1)S(1)}, bf16[288,256]{1,0:T(8,128)(2,1)S(1)}, u32[]{:S(2)}, u32[]{:S(2)}) collective-permute-start(bf16[288,256]{1,0:T(8,128)(2,1)S(1)} %add_convert_fusion.2.refs_2_), channel_id=1, source_target_pairs={{0,8},{8,0},{16,24},{24,16},{1,9},{9,1},{17,25},{25,17},{2,10},{10... | collective-permute-start | bytes 442376 | tf_op jit(solution)/shard_map/ppermute | solution.py:577
  92.1 8.9 %collective-permute-start.26 = (bf16[288,256]{1,0:T(8,128)(2,1)S(1)}, bf16[288,256]{1,0:T(8,128)(2,1)S(1)}, u32[]{:S(2)}, u32[]{:S(2)}) collective-permute-start(bf16[288,256]{1,0:T(8,128)(2,1)S(1)} %add_convert_fusion.2.refs_2_), channel_id=1, source_target_pairs={{0,16},{8,24},{16,0},{24,8},{1,17},{9,25},{17,1},{25,9},{2,18},{10... | collective-permute-start | bytes 442376 | tf_op jit(solution)/shard_map/ppermute | solution.py:577
  93.6 7.5 %collective-permute-start.27 = (bf16[288,256]{1,0:T(8,128)(2,1)S(1)}, bf16[288,256]{1,0:T(8,128)(2,1)S(1)}, u32[]{:S(2)}, u32[]{:S(2)}) collective-permute-start(bf16[288,256]{1,0:T(8,128)(2,1)S(1)} %add_convert_fusion.2.refs_2_), channel_id=1, source_target_pairs={{0,24},{8,16},{16,8},{24,0},{1,25},{9,17},{17,9},{25,1},{2,26},{10... | collective-permute-start | bytes 442376 | tf_op jit(solution)/shard_map/ppermute | solution.py:577
  94.8 9.7 %collective-permute-start.24 = (bf16[32,768]{1,0:T(8,128)(2,1)S(1)}, bf16[32,768]{1,0:T(8,128)(2,1)S(1)}, u32[]{:S(2)}, u32[]{:S(2)}) collective-permute-start(bf16[32,768]{1,0:T(8,128)(2,1)S(1)} %fusion.2), channel_id=1, source_target_pairs={{0,24},{8,16},{16,8},{24,0},{1,25},{9,17},{17,9},{25,1},{2,26},{10... | collective-permute-start | bytes 147464 | tf_op jit(solution)/shard_map/ppermute | solution.py:577
  97.2 7.2 %collective-permute-start.23 = (bf16[32,768]{1,0:T(8,128)(2,1)S(1)}, bf16[32,768]{1,0:T(8,128)(2,1)S(1)}, u32[]{:S(2)}, u32[]{:S(2)}) collective-permute-start(bf16[32,768]{1,0:T(8,128)(2,1)S(1)} %fusion.2), channel_id=1, source_target_pairs={{0,16},{8,24},{16,0},{24,8},{1,17},{9,25},{17,1},{25,9},{2,18},{10... | collective-permute-start | bytes 147464 | tf_op jit(solution)/shard_map/ppermute | solution.py:577
  97.7 6.7 %collective-permute-start.22 = (bf16[32,768]{1,0:T(8,128)(2,1)S(1)}, bf16[32,768]{1,0:T(8,128)(2,1)S(1)}, u32[]{:S(2)}, u32[]{:S(2)}) collective-permute-start(bf16[32,768]{1,0:T(8,128)(2,1)S(1)} %fusion.2), channel_id=1, source_target_pairs={{0,8},{8,0},{16,24},{24,16},{1,9},{9,1},{17,25},{25,17},{2,10},{10... | collective-permute-start | bytes 147464 | tf_op jit(solution)/shard_map/ppermute | solution.py:577
  (28 other events, 118.5 us)

commit v3 on v2

v3 whole, which is shorter than its diff:
```python
import functools
import types

import jax
import jax.numpy as jnp
from jax import lax
from jax.experimental import pallas as pl
from jax.experimental.pallas import tpu as pltpu
from jax.sharding import PartitionSpec as P

BF = jnp.bfloat16
F32 = jnp.float32
HEADS = 8
ITERS = 2
BLK = 128
CHUNK = 512
NEG = -1e30
LOG2E = 1.4426950408889634
LN2 = 0.6931471805599453
GELU_A = 0.7978845608028654
GELU_B = GELU_A * 0.044715
FLOPS_FIRST = 10 ** 9
FLOPS_PREPARE = 10 ** 9
FLOPS_LAST = 10 ** 10
LIMIT_MIDDLE = 40
LIMIT_LAST = 16


def dot(a, b):
    return jnp.dot(a, b, preferred_element_type=F32)

def dot_tn(a, b):
    return lax.dot_general(a, b, (((0,), (0,)), ((), ())), preferred_element_type=F32)

def dot_nt(a, b):
    return lax.dot_general(a, b, (((1,), (1,)), ((), ())), preferred_element_type=F32)

def rows(start, size):
    return pl.ds(start, size)

def ln_fwd(x):
    c = x - jnp.mean(x, axis=1, keepdims=True)
    r = lax.rsqrt(jnp.mean(c * c, axis=1, keepdims=True) + 1e-5)
    return c * r, r

def ln_bwd(y, n, r):
    return r * (y - jnp.mean(y, axis=1, keepdims=True) - n * jnp.mean(y * n, axis=1, keepdims=True))

def loop(n, body):
    for i in range(n):
        body(i)

def make_masks(len_ref, mask_ref, nb):
    pos = lax.broadcasted_iota(jnp.int32, (1, BLK), 1)
    ends = []
    total = jnp.int32(0)
    for p in range(len_ref.shape[1]):
        total = total + len_ref[0, p]
        ends.append(total)

    def block(i, _):
        q = pos + i * BLK
        start = jnp.zeros((1, BLK), jnp.int32)
        for e in ends:
            start = jnp.where(q >= e, e, start)
        k = lax.broadcasted_iota(jnp.int32, (2 * BLK, BLK), 0) + (i - 1) * BLK
        mask_ref[i] = jnp.where((k >= start) & (k <= q), 0.0, NEG).astype(F32)
        return 0

    lax.fori_loop(0, nb, block, 0)

def pad_zero(s):
    s.kp[0:BLK, :] = jnp.zeros((BLK, s.kp.shape[1]), BF)
    s.vp[0:BLK, :] = jnp.zeros((BLK, s.vp.shape[1]), BF)
    s.kt[0] = jnp.zeros(s.kt.shape[1:], BF)
    s.vt[0] = jnp.zeros(s.vt.shape[1:], BF)

def project(s, j, ent, wqkv):
    n, r = ln_fwd(ent)
    nb16 = n.astype(BF)
    s.n1[rows(j * CHUNK, CHUNK), :] = nb16
    s.r1[rows(j * CHUNK, CHUNK), :] = jnp.broadcast_to(r, (CHUNK, 128))
    pack_heads(s, j, nb16, wqkv)

def pack_heads(s, j, nb16, wqkv):
    d = nb16.shape[1]
    scale = LOG2E * (d // HEADS) ** -0.5
    q = (dot(nb16, wqkv[:, 0:d]) * scale).astype(BF)
    k = dot(nb16, wqkv[:, d:2 * d]).astype(BF)
    v = dot(nb16, wqkv[:, 2 * d:3 * d]).astype(BF)
    s.qs[rows(j * CHUNK, CHUNK), :] = q
    s.kp[pl.ds(j * CHUNK + BLK, CHUNK), :] = k
    s.vp[pl.ds(j * CHUNK + BLK, CHUNK), :] = v
    qt, kt, vt = q.T, k.T, v.T
    for b in range(CHUNK // BLK):
        i = j * (CHUNK // BLK) + b
        s.qst[i] = qt[:, b * BLK:(b + 1) * BLK]
        s.kt[i + 1] = kt[:, b * BLK:(b + 1) * BLK]
        s.vt[i + 1] = vt[:, b * BLK:(b + 1) * BLK]

def split_heads(tile, a, hd):
    def alone(lo):
        parts = [jnp.zeros((n, tile.shape[1]), tile.dtype) for n in (lo, tile.shape[0] - lo - hd)]
        parts = [parts[0], tile[lo:lo + hd], parts[1]]
        return jnp.concatenate([p for p in parts if p.shape[0]], axis=0)
    return jnp.concatenate([alone(a), alone(a + hd)], axis=1)

def stack_heads(tile, a, hd):
    z = jnp.zeros_like(tile)
    lane = lax.broadcasted_iota(jnp.int32, tile.shape, 1)
    top = jnp.where((lane >= a) & (lane < a + hd), tile, z)
    low = jnp.where((lane >= a + hd) & (lane < a + 2 * hd), tile, z)
    return jnp.concatenate([top, low], axis=0)

def pairs_of(d):
    hd = d // HEADS
    per = 128 // (2 * hd)
    return [(p, slice(p // per * 128, p // per * 128 + 128), p % per * 2 * hd, p * 2 * hd) for p in range(HEADS // 2)]

def window(ref, i, lo, n):
    return jnp.concatenate([ref[i, lo:lo + n, :], ref[i + 1, lo:lo + n, :]], axis=1)

def attend(s, blocks, mask_ref):
    d = s.qs.shape[1]
    hd = d // HEADS
    ones = jnp.ones((16, 2 * BLK), BF)
    def scores(i):
        win = pl.ds(i * BLK, 2 * BLK)
        return [dot(s.kp[win, tile], split_heads(s.qst[i, tile, :], a, hd)) for _, tile, a, _ in pairs_of(d)]
    def soft(i, all_scores):
        mask = mask_ref[i]
        mask = jnp.concatenate([mask, mask], axis=1)
        out = []
        for sc in all_scores:
            sc = sc + mask
            out.append(jnp.exp2(sc - jnp.max(sc, axis=0, keepdims=True)).astype(BF))
        return out
    def values(i, es):
        return [dot(jnp.concatenate([window(s.vt, i, lo, 2 * hd), ones], axis=0), es[p]) for p, _, _, lo in pairs_of(d)]
    es = []
    ready = scores(blocks[0])
    for n, i in enumerate(blocks):
        ahead = scores(blocks[n + 1]) if n + 1 < len(blocks) else None
        es.append(soft(i, ready))
        ready = ahead
    os = [values(i, e) for i, e in zip(blocks, es)]
    for i, e, o in zip(blocks, es, os):
        for p, _, _, lo in pairs_of(d):
            s.e[i, p] = e[p]
            inv = 1.0 / o[p][2 * hd:2 * hd + 1, :]
            s.linv[i, 2 * p:2 * p + 1, :] = inv[:, :BLK]
            s.linv[i, 2 * p + 1:2 * p + 2, :] = inv[:, BLK:]
            s.ht[i, lo:lo + hd, :] = (o[p][0:hd, :BLK] * inv[:, :BLK]).astype(BF)
            s.ht[i, lo + hd:lo + 2 * hd, :] = (o[p][hd:2 * hd, BLK:] * inv[:, BLK:]).astype(BF)

def heads_chunk(s, j):
    return jnp.concatenate([s.ht[j * (CHUNK // BLK) + b] for b in range(CHUNK // BLK)], axis=1)

def mlp(s, j, ent, wout, wup, wdown):
    mid = ent + dot_tn(heads_chunk(s, j), wout[...])
    n, r = ln_fwd(mid)
    nb16 = n.astype(BF)
    at = rows(j * CHUNK, CHUNK)
    s.n2[at, :] = nb16
    s.r2[at, :] = jnp.broadcast_to(r, (CHUNK, 128))
    acc = mid
    for f in range(wup.shape[1] // 256):
        c = slice(f * 256, (f + 1) * 256)
        h = dot(nb16, wup[:, c]).astype(BF)
        h2 = h * h
        sg = 0.5 * jnp.tanh(h * (GELU_B * h2 + GELU_A)) + 0.5
        act = h * sg
        s.act[at, c] = act
        s.gp[at, c] = sg + act * (2.0 - 2.0 * sg) * (3 * GELU_B * h2 + GELU_A)
        acc = acc + dot(act, wdown[c, :])
    return acc

def mlp_back(s, j, g, wdown_t, wup_t):
    at = rows(j * CHUNK, CHUNK)
    gb = g.astype(BF)
    s.g2[at, :] = gb
    acc = None
    for f in range(wdown_t.shape[1] // 256):
        c = slice(f * 256, (f + 1) * 256)
        dh = dot(gb, wdown_t[:, c]).astype(BF) * s.gp[at, c]
        s.gp[at, c] = dh
        part = dot(dh, wup_t[c, :])
        acc = part if acc is None else acc + part
    g = g + ln_bwd(acc, s.n2[at, :].astype(F32), s.r2[at, 0:1])
    s.gm[at, :] = g.astype(BF)
    return g

def attend_back(s, blocks, wout, dk_ref, dv_ref):
    d = s.qs.shape[1]
    hd = d // HEADS
    minus = jnp.full((2 * BLK, 128), -1.0, BF)
    def head_grads(i):
        raw = dot_nt(wout[...], s.gm[rows(i * BLK, BLK), :])
        inv = jnp.concatenate([jnp.broadcast_to(s.linv[i, h:h + 1, :], (hd, BLK)) for h in range(HEADS)], axis=0)
        dost = (raw * inv).astype(BF)
        return dost, (dost.astype(F32) * s.ht[i].astype(F32)).astype(BF), dost.T
    def prob_grads(i, dost, doh):
        win = pl.ds(i * BLK, 2 * BLK)
        return [dot(jnp.concatenate([s.vp[win, tile], minus], axis=1),
                    jnp.concatenate([split_heads(dost[tile, :], a, hd), split_heads(doh[tile, :], a, hd)], axis=0))
                for _, tile, a, _ in pairs_of(d)]
    def by_keys(lhs, tokens):
        return [dot(lhs[p], stack_heads(tokens[:, tile], a, hd)) for p, tile, a, _ in pairs_of(d)]
    def by_queries(i, dss):
        out = []
        for p, _, _, lo in pairs_of(d):
            dq = dot(window(s.kt, i, lo, 2 * hd), dss[p])
            out += [dq[0:hd, :BLK], dq[hd:2 * hd, BLK:]]
        return (jnp.concatenate(out, axis=0) * hd ** -0.5).astype(BF)
    heads = [head_grads(i) for i in blocks]
    dps = [prob_grads(i, h[0], h[1]) for i, h in zip(blocks, heads)]
    es = [[s.e[i, p] for p in range(HEADS // 2)] for i in blocks]
    dvs = [by_keys(e, h[2]) for e, h in zip(es, heads)]
    dss = [[(x.astype(F32) * y).astype(BF) for x, y in zip(e, dp)] for e, dp in zip(es, dps)]
    dks = [by_keys(ds, s.qs[rows(i * BLK, BLK), :]) for i, ds in zip(blocks, dss)]
    dqs = [by_queries(i, ds) for i, ds in zip(blocks, dss)]
    per = HEADS // 2 // (d // 128)
    for n, i in enumerate(blocks):
        top, low = pl.ds(i * BLK, BLK), pl.ds(i * BLK + BLK, BLK)
        for ref, parts in ((dk_ref, dks[n]), (dv_ref, dvs[n])):
            for t in range(d // 128):
                tile = slice(t * 128, (t + 1) * 128)
                total = sum(parts[t * per + 1:(t + 1) * per], parts[t * per])
                ref[top, tile] += total[:BLK]
                ref[low, tile] = total[BLK:]
        s.dpk[rows(i * BLK, BLK), 0:d] = dqs[n].T

def finish_packed(s, j, dk_ref, dv_ref):
    d = s.n1.shape[1]
    at = rows(j * CHUNK, CHUNK)
    pat = pl.ds(j * CHUNK + BLK, CHUNK)
    s.dpk[at, d:2 * d] = (dk_ref[pat, :] * LN2).astype(BF)
    s.dpk[at, 2 * d:3 * d] = dv_ref[pat, :].astype(BF)

def project_back(s, j, g, wqkv_t):
    at = rows(j * CHUNK, CHUNK)
    return g + ln_bwd(dot(s.dpk[at, :], wqkv_t[...]), s.n1[at, :].astype(F32), s.r1[at, 0:1])

def weigh(cnt_ref, len_ref, j, cot):
    pos = lax.broadcasted_iota(jnp.int32, (CHUNK, 128), 0) + j * CHUNK
    w = jnp.zeros((CHUNK, 128), F32)
    begin = jnp.int32(0)
    for p in range(len_ref.shape[1]):
        w = jnp.where(pos >= begin, 12.0 / cnt_ref[0, p].astype(F32), w)
        begin = begin + len_ref[0, p]
    return cot * jnp.concatenate([w] * (cot.shape[1] // 128), axis=1)

def saved_shapes(t, d, ff):
    nb = t // BLK
    return dict(n1=((t, d), BF), r1=((t, 128), F32), qs=((t, d), BF), kp=((t + BLK, d), BF), vp=((t + BLK, d), BF),
                qst=((nb, d, BLK), BF), kt=((nb + 1, d, BLK), BF), vt=((nb + 1, d, BLK), BF), e=((nb, HEADS // 2, 2 * BLK, 2 * BLK), BF),
                ht=((nb, d, BLK), BF), linv=((nb, HEADS, BLK), F32))
def more_shapes(t, d, ff):
    return dict(n2=((t, d), BF), r2=((t, 128), F32), act=((t, ff), BF), gp=((t, ff), BF),
                g2=((t, d), BF), gm=((t, d), BF), dpk=((t, 3 * d), BF))

class Memory:
    def __init__(self, ins, outs, sems, hbm, loads):
        self.ins, self.outs, self.sems, self.hbm, self.loads, self.started = ins, outs, sems, hbm, loads, []

    def wait(self, *which):
        for n in which:
            self.loads[n].wait()

    def put(self, n):
        copy = pltpu.make_async_copy(self.outs[n], self.hbm[n], self.sems.at[len(self.started)])
        copy.start()
        self.started.append(copy)

def call(kernel, outs, args, scratch, name, flops, limit=16):
    spec = dict(vmem=pl.BlockSpec(memory_space=pltpu.VMEM), smem=pl.BlockSpec(memory_space=pltpu.SMEM), any=pl.BlockSpec(memory_space=pl.ANY))
    spec["store"] = spec["load"] = spec["any"]
    n_in, n_out, n_scratch = len(args), len(outs), len(scratch)
    stores = [n for n, o in enumerate(outs) if o[0] == "store"]
    loads = [n for n, a in enumerate(args) if a[0] == "load"]
    buffers = [pltpu.VMEM(outs[n][1], outs[n][2]) for n in stores] + [(pltpu.SMEM if args[n][1].dtype == jnp.int32 else pltpu.VMEM)(args[n][1].shape, args[n][1].dtype) for n in loads]
    buffers += [pltpu.SemaphoreType.DMA((max(len(stores), 1),)), pltpu.SemaphoreType.DMA((max(len(loads), 1),))]
    def run(*refs):
        ins, results, rest = list(refs[:n_in]), list(refs[n_in:n_in + n_out]), refs[n_in + n_out:]
        hbm, coming = list(results), {}
        for n, r in zip(stores, rest[n_scratch:]):
            results[n] = r
        for c, (n, r) in enumerate(zip(loads, rest[n_scratch + len(stores):])):
            coming[n] = pltpu.make_async_copy(ins[n], r, rest[-1].at[c])
            coming[n].start()
            ins[n] = r
        memory = Memory(ins, results, rest[-2], hbm, coming)
        kernel(memory, types.SimpleNamespace(**dict(zip(scratch, rest))))
        for copy in memory.started:
            copy.wait()
    shapes = dict(vmem=pltpu.VMEM, store=jax.ShapeDtypeStruct)
    place = dict(vmem=pltpu.VMEM, load=pltpu.HBM)
    return pl.pallas_call(
        run, out_shape=tuple(shapes[o[0]](o[1], o[2]) for o in outs),
        in_specs=[spec[k] for k, _ in args], out_specs=tuple(spec[o[0]] for o in outs),
        scratch_shapes=[pltpu.VMEM(*v) for v in scratch.values()] + buffers,
        compiler_params=pltpu.CompilerParams(vmem_limit_bytes=limit << 20), name=name,
        cost_estimate=pl.CostEstimate(flops=flops, bytes_accessed=1 << 20, transcendentals=0))(
        *[pltpu.with_memory_space_constraint(v, place[k]) if k in place else v for k, v in args])

def place_qkv(me, parts, wqkv):
    r = wqkv.shape[0] // len(parts)
    for x, p in enumerate(parts):
        wqkv[pl.ds(pl.multiple_of((me ^ x) * r, r), r), :] = p[...]

def place_rest(me, parts, wout, wup, wdown):
    r, rd = wout.shape[0] // len(parts), wdown.shape[0] // len(parts)
    for x, p in enumerate(parts):
        at = pl.ds(pl.multiple_of((me ^ x) * r, r), r)
        wout[at, :] = p[0:r, :]
        for c in range(wup.shape[1] // 256):
            wup[at, c * 256:(c + 1) * 256] = p[(c + 1) * r:(c + 2) * r, :]
        lo = r * (1 + wup.shape[1] // 256)
        wdown[pl.ds(pl.multiple_of((me ^ x) * rd, rd), rd), :] = p[lo:lo + rd, :]

def hand_out(me, parts, mats, keep, send):
    for x in range(parts):
        dst = send if x % 2 else keep
        lo = 0
        for m in mats:
            r = m.shape[0] // parts
            at = pl.ds(pl.multiple_of((me ^ x) * r, r), r)
            for c in range(m.shape[1] // 256):
                dst[x // 2, lo:lo + r, :] = m[at, c * 256:(c + 1) * 256]
                lo += r

SAVED = ("e", "n1", "r1", "qs", "vp", "kt", "ht", "linv")

def prepare(lengths, counts, states, inject, cot):
    t, d = states.shape
    nb, nc = t // BLK, t // CHUNK
    def kernel(m, s):
        len_ref, cnt_ref, st, inj, ct = m.ins
        ent, inj_out, g, n1, r1, mask = m.outs
        m.wait(0, 1)
        make_masks(len_ref, mask, nb)
        m.wait(2, 3)
        for j in range(nc):
            at = slice(j * CHUNK, (j + 1) * CHUNK)
            x = st[at, :] + inj[at, :]
            ent[at, :] = x
            inj_out[at, :] = inj[at, :]
            n, r = ln_fwd(x)
            n1[at, :] = n.astype(BF)
            r1[at, :] = jnp.broadcast_to(r, (CHUNK, 128))
        m.wait(4)
        for j in range(nc):
            at = slice(j * CHUNK, (j + 1) * CHUNK)
            g[at, :] = weigh(cnt_ref, len_ref, j, ct[at, :])
    outs = [("vmem", (t, d), F32)] * 3 + [("vmem", (t, d), BF), ("vmem", (t, 128), F32), ("vmem", (nb, 2 * BLK, BLK), F32)]
    args = [("load", v) for v in (lengths, counts, states, inject, cot)]
    return call(kernel, outs, args, {}, "prepare", FLOPS_PREPARE)

def first_attention(me, n1, mask, qkv_parts, ff):
    t, d = n1.shape
    nb, nc = t // BLK, t // CHUNK
    shapes = saved_shapes(t, d, ff)
    made = [k for k in SAVED if k not in ("n1", "r1")]
    scratch = {k: v for k, v in shapes.items() if k not in SAVED}
    def kernel(m, s):
        me_ref, n1_ref, mask_ref = m.ins[:3]
        vars(s).update(zip(made, m.outs))
        wqkv = m.outs[-1]
        pad_zero(s)
        place_qkv(me_ref[0], m.ins[3:], wqkv)
        for j in range(nc):
            pack_heads(s, j, n1_ref[j * CHUNK:(j + 1) * CHUNK, :], wqkv)
        for i in range(0, nb, 2):
            attend(s, (i, i + 1), mask_ref)
    outs = [("vmem",) + shapes[k] for k in made] + [("vmem", (d, 3 * d), BF)]
    args = [("smem", me), ("vmem", n1), ("vmem", mask)] + [("vmem", p) for p in qkv_parts]
    got = call(kernel, outs, args, scratch, "first_attention", FLOPS_FIRST)
    return dict(zip(made, got)), got[-1]

def middle_part(me, ent, inject, weighed, mask, wqkv, ht, rest_parts, ff):
    t, d = ent.shape
    nb, nc = t // BLK, t // CHUNK
    parts = len(rest_parts)
    sh = {"a_" + k: v for k, v in more_shapes(t, d, ff).items() if k not in ("dpk", "gm")}
    sh.update({"b_" + k: v for k, v in {**saved_shapes(t, d, ff), **more_shapes(t, d, ff)}.items()})
    sh.update(state=((t, d), F32), dk=((t + BLK, d), F32), dv=((t + BLK, d), F32),
              wqkv_t=((3 * d, d), BF), wup_t=((ff, d), BF), wdown_t=((d, ff), BF), tr=((2, d, t), BF),
              wup=((d, ff), BF), wdown=((ff, d), BF), mout=((d, d), BF), mup=((d, ff), BF), mdown_t=((d, ff), BF), mdown=((ff, d), BF))
    def kernel(m, x):
        me_ref, ent_ref, inj, weighed_ref, x.mask, wqkv_ref, ht_ref = m.ins[:7]
        final, g, ginj, gm, wout, mqkv, keep, send = m.outs
        its = [types.SimpleNamespace(**{k[2:]: v for k, v in vars(x).items() if k.startswith(p)}) for p in ("a_", "b_")]
        its[0].ht, its[0].gm = ht_ref, gm
        place_rest(me_ref[0], m.ins[7:], wout, x.wup, x.wdown)
        x.wup_t[...] = x.wup[...].T
        x.wdown_t[...] = x.wdown[...].T
        pad_zero(its[1])
        x.wqkv_t[...] = wqkv_ref[...].T
        def rows_of(j):
            return slice(j * CHUNK, (j + 1) * CHUNK)
        def mlp_of(n, j, src, dst):
            at = rows_of(j)
            entered = src[at, :] + inj[at, :] if n else src[at, :]
            dst[at, :] = mlp(its[n], j, entered, wout, x.wup, x.wdown)
        def project_of(j):
            project(its[1], j, x.state[rows_of(j), :] + inj[rows_of(j), :], wqkv_ref)
        def blocks_of(j):
            n = CHUNK // BLK
            return [tuple(range(j * n + b, min(j * n + b + 2, j * n + n))) for b in range(0, n, 2)]
        def attend_of(j):
            for blocks in blocks_of(j):
                attend(its[1], blocks, x.mask)
        def back_two(j):
            at = rows_of(j)
            g[at, :] = mlp_back(its[1], j, weighed_ref[at, :], x.wdown_t, x.wup_t)
        def attend_back_of(j):
            for blocks in blocks_of(j):
                attend_back(its[1], blocks, wout, x.dk, x.dv)
        def back_one(j):
            at = rows_of(j)
            finish_packed(its[1], j, x.dk, x.dv)
            new = project_back(its[1], j, g[at, :], x.wqkv_t)
            ginj[at, :] = new
            g[at, :] = mlp_back(its[0], j, new, x.wdown_t, x.wup_t)
        x.dk[0:BLK, :] = jnp.zeros((BLK, d), F32)
        x.dv[0:BLK, :] = jnp.zeros((BLK, d), F32)
        for j in range(nc): mlp_of(0, j, ent_ref, x.state)
        for j in range(nc): project_of(j)
        for j in range(nc): attend_of(j)
        for j in range(nc): mlp_of(1, j, x.state, final)
        m.put(0)
        for j in range(nc): back_two(j)
        for j in range(nc): attend_back_of(j)
        for j in range(nc): back_one(j)

        def weight_grad(lefts, rights, dst):
            for n, left in enumerate(lefts):
                x.tr[n] = left[...].T
            def tile(c):
                cc = pl.ds(c * 256, 256)
                total = dot(x.tr[0], rights[0][:, cc])
                for n in range(1, len(rights)):
                    total = total + dot(x.tr[n], rights[n][:, cc])
                dst[:, cc] = total.astype(dst.dtype)
            loop(dst.shape[1] // 256, tile)
        weight_grad([s.g2 for s in its], [s.act for s in its], x.mdown_t)
        x.mdown[...] = x.mdown_t[...].T
        weight_grad([s.n2 for s in its], [s.gp for s in its], x.mup)
        weight_grad([its[1].n1], [its[1].dpk], mqkv)
        total = None
        for s in its:
            for b in range(nb):
                part = dot(s.ht[b], s.gm[b * BLK:(b + 1) * BLK, :])
                total = part if total is None else total + part
        x.mout[...] = total.astype(BF)
        hand_out(me_ref[0], parts, (x.mout, x.mup, x.mdown), keep, send)
    piece = ("vmem", (max(parts // 2, 1), (d + ff) // parts + ff // parts, d), BF)
    outs = [("store", (t, d), F32)] + [("vmem", (t, d), F32)] * 2 + [("vmem", (t, d), BF), ("vmem", (d, d), BF), ("vmem", (d, 3 * d), F32)] + [piece] * 2
    args = [("smem", me)] + [("vmem", v) for v in (ent, inject, weighed, mask, wqkv, ht, *rest_parts)]
    return call(kernel, outs, args, sh, "middle_part", 25 * 10 ** 9, limit=LIMIT_MIDDLE)

def last_part(me, saved, gm, wout, wqkv, mqkv, g, ginj, parts, ff, first):
    t, d = gm.shape
    nb, nc = t // BLK, t // CHUNK
    scratch = dict(dk=((t + BLK, d), F32), dv=((t + BLK, d), F32), tr=((d, t), BF), mat=((d, 3 * d), BF), wt=((3 * d, d), BF), dpk=((t, 3 * d), BF))
    def kernel(m, s):
        me_ref, s.gm, wout_ref, w_ref, m_ref, g_ref, gi_ref = m.ins[:7]
        vars(s).update(zip(SAVED, m.ins[7:]))
        keep, send, grad, grad_inject = m.outs
        s.dk[0:BLK, :] = jnp.zeros((BLK, d), F32)
        s.dv[0:BLK, :] = jnp.zeros((BLK, d), F32)
        for i in range(0, nb, 2):
            attend_back(s, (i, i + 1), wout_ref, s.dk, s.dv)
        s.tr[...] = s.n1[...].T
        s.wt[...] = w_ref[...].T
        loop(nc, lambda j: finish_packed(s, j, s.dk, s.dv))
        def tile(c):
            cc = slice(c * 256, (c + 1) * 256)
            s.mat[:, cc] = (m_ref[:, cc] + dot(s.tr[...], s.dpk[:, cc])).astype(BF)
        loop(3, tile)
        hand_out(me_ref[0], parts, (s.mat,), keep, send)
        def chunk(j):
            at = rows(j * CHUNK, CHUNK)
            new = project_back(s, j, g_ref[at, :], s.wt)
            grad[at, :] = new
            grad_inject[at, :] = new + gi_ref[at, :]
        loop(nc, chunk)
        m.put(2)
        m.put(3)
    outs = [("vmem", (max(parts // 2, 1), 3 * d // parts, d), BF)] * 2 + [("store", (t, d), F32)] * 2
    args = [("smem", me)] + [("vmem", v) for v in (gm, wout, wqkv, mqkv, g, ginj)]
    args += [("vmem", saved[k]) for k in SAVED] + [("any", v) for v in first]
    return call(kernel, outs, args, scratch, "last_part", FLOPS_LAST, limit=LIMIT_LAST)

def to_column(row):
    n = row.shape[1]
    eye = lax.broadcasted_iota(jnp.int32, (n, n), 0) == lax.broadcasted_iota(jnp.int32, (n, n), 1)
    return jnp.sum(jnp.where(eye, jnp.broadcast_to(row, (n, n)), 0.0), axis=1, keepdims=True)

def to_row(column):
    n = column.shape[0]
    eye = lax.broadcasted_iota(jnp.int32, (n, n), 0) == lax.broadcasted_iota(jnp.int32, (n, n), 1)
    return jnp.sum(jnp.where(eye, jnp.broadcast_to(column, (n, n)), 0.0), axis=0, keepdims=True)

def pack_weights(w_qkv, gain_one, w_out, w_up, w_down, gain_two):
    r, d = w_out.shape
    n = w_up.shape[1] // d
    def kernel(m, s):
        qkv, g_one, out, up, down, g_two = m.ins
        m.wait(0, 1)
        m.outs[0][...] = (qkv[...].astype(F32) * to_column(g_one[...].astype(F32))).astype(BF)
        m.wait(2, 3, 4, 5)
        m.outs[1][0:r, :] = out[...]
        col = to_column(g_two[...].astype(F32))
        for c in range(n):
            m.outs[1][(c + 1) * r:(c + 2) * r, :] = (up[:, c * d:(c + 1) * d].astype(F32) * col).astype(BF)
        m.outs[1][(n + 1) * r:, :] = down[...]
    args = [("load", v) for v in (w_qkv, gain_one.reshape(1, -1), w_out, w_up, w_down, gain_two.reshape(1, -1))]
    return call(kernel, [("vmem", w_qkv.shape, BF), ("vmem", ((n + 1) * r + w_down.shape[0], d), BF)], args, {}, "pack_weights", 10 ** 6)

def sum_parts(parts, lo, size):
    acc = parts[0][lo:lo + size, :].astype(F32)
    for p in parts[1:]:
        acc = acc + p[lo:lo + size, :].astype(F32)
    return acc

def finished(shares, weight, gain, lead, tail, name):
    r, cols = weight.shape
    d = shares[0].shape[1]
    n = cols // d
    def kernel(m, s):
        w, g, parts = m.ins[0], to_column(m.ins[1][...].astype(F32)), m.ins[2:]
        along = jnp.zeros((r, 1), F32)
        for c in range(n):
            v = sum_parts(parts, lead + c * r, r)
            m.outs[0][:, c * d:(c + 1) * d] = v * g
            along = along + jnp.sum(v * w[:, c * d:(c + 1) * d].astype(F32), axis=1, keepdims=True)
        m.put(0)
        m.outs[1][...] = to_row(along)
        m.put(1)
        if lead:
            m.outs[2][...] = sum_parts(parts, 0, lead)
            m.outs[3][...] = sum_parts(parts, lead + n * r, tail)
            m.put(2)
            m.put(3)
    outs = [("store", (r, cols), F32), ("store", (1, r), F32)] + ([("store", (lead, d), F32), ("store", (tail, d), F32)] if lead else [])
    got = call(kernel, outs, [("vmem", v) for v in (weight, gain.reshape(1, -1), *shares)], {}, name, 10 ** 6)
    return [got[0], got[1].reshape(r)] + list(got[2:])

def after(values, *others):
    return lax.optimization_barrier((values, others))[0]

def exchange(x, axis, size, step):
    return lax.ppermute(x, axis, [(i, i ^ step) for i in range(size)])

def far_parts(x, size):
    return [x] + [exchange(x, "fsdp", size, 2 * k) for k in range(1, size // 2)]

def with_near(far, size):
    return [v for x in far for v in (x, exchange(x, "fsdp", size, 1))]

def sum_near(keep, near, then=None):
    total = keep.astype(F32) + near.astype(F32)
    if then is not None:
        total = total + jnp.minimum(jnp.abs(then[:keep.shape[1]].astype(F32)), 0.0)
    return [total[k].astype(BF) for k in range(keep.shape[0])]

def send_far(summed, size):
    return [exchange(summed[k], "fsdp", size, 2 * k) for k in range(1, size // 2)]

def along_dp(share, size):
    return [share] + [exchange(share, "dp", size, k) for k in range(1, size)]

def send_near(pieces, size):
    return [exchange(p, "fsdp", size, 1) for p in pieces[1::2]]

def send_far(summed, size):
    return [exchange(summed[k], "fsdp", size, 2 * k) for k in range(1, size // 2)]

def reduce_whole(whole, sizes):
    out, lo = [], 0
    for n in sizes:
        share = lax.psum_scatter(whole[lo:lo + n], "fsdp", scatter_dimension=0, tiled=True)
        out.append(lax.psum(share, "dp").astype(F32))
        lo += n
    return jnp.concatenate(out, axis=0)

def on_device(n_dp, n_fsdp, states, inject, ln1_gain, w_qkv, w_out, ln2_gain, w_up, w_down, prompt_lengths, loop_counts, cotangent):
    d = states.shape[1]
    r, ff = w_up.shape
    direct = r % 16 == 0
    if direct:
        me = lax.axis_index("fsdp").astype(jnp.int32).reshape(1)
        own_qkv, own_rest = pack_weights(w_qkv, ln1_gain, w_out, w_up, w_down, ln2_gain)
        qkv_far = far_parts(own_qkv, n_fsdp)
        rest_far = far_parts(own_rest, n_fsdp)
        qkv_parts = with_near(qkv_far, n_fsdp)
    else:
        me = jnp.zeros((1,), jnp.int32)
        full = lambda v: lax.all_gather(v, "fsdp", axis=0, tiled=True)
        up = full((w_up.astype(F32) * ln2_gain.astype(F32)[:, None]).astype(BF))
        qkv_parts = [full((w_qkv.astype(F32) * ln1_gain.astype(F32)[:, None]).astype(BF))]
        rest_parts = [jnp.concatenate([full(w_out)] + [up[:, c:c + d] for c in range(0, ff, d)] + [full(w_down)], axis=0)]
    parts = len(qkv_parts)
    ent, inject, weighed, n1, r1, mask = prepare(prompt_lengths, loop_counts, states, inject, cotangent)
    saved, wqkv = first_attention(me, n1, mask, qkv_parts, ff)
    saved.update(n1=n1, r1=r1)
    if direct:
        rest_parts = with_near(after(rest_far, wqkv), n_fsdp)
    final, g, ginj, gm, wout, mqkv, keep, send = middle_part(
        me, ent, inject, weighed, mask, wqkv, saved["ht"], rest_parts, ff)
    summed = []
    if direct:
        summed = sum_near(keep, exchange(send, "fsdp", n_fsdp, 1))
        far = send_far(summed, n_fsdp)
    else:
        shares = [reduce_whole(keep[0], [d] * (1 + ff // d) + [ff])]
    keep_qkv, send_qkv, grad_states, grad_inject = last_part(me, saved, gm, wout, wqkv, mqkv, g, ginj, parts, ff, summed)
    if direct:
        near = exchange(send_qkv, "fsdp", n_fsdp, 1)
        share = sum_parts([summed[0], *far], 0, summed[0].shape[0]).astype(BF)
        shares = along_dp(share, n_dp)
        summed = sum_near(keep_qkv, near, share)
        shares_qkv = along_dp(sum_parts([summed[0], *send_far(summed, n_fsdp)], 0, 3 * r).astype(BF), n_dp)
    else:
        shares_qkv = [reduce_whole(keep_qkv[0], [d] * 3)]
    d_up, d_gain_two, d_out, d_down = finished(shares, w_up, ln2_gain, r, w_down.shape[0], "finished_rest")
    d_qkv, d_gain_one = finished(shares_qkv, w_qkv, ln1_gain, 0, 0, "finished_qkv")
    return (final, grad_states, grad_inject, d_gain_one, d_qkv, d_out, d_gain_two, d_up, d_down)

def solution(mesh):
    tok, vec, mat = P(("dp", "fsdp"), None), P("fsdp"), P("fsdp", None)
    return jax.shard_map(
        functools.partial(on_device, mesh.shape["dp"], mesh.shape["fsdp"]), mesh=mesh,
        in_specs=(tok, tok, vec, mat, mat, vec, mat, mat, tok, tok, tok),
        out_specs=(tok, tok, tok, vec, mat, mat, vec, mat, mat), check_vma=False)
```

time: 106 us -> 82.3 us (0.78)
  Pallas kernels: 57.2 us -> 37.3 us
  waiting for transfers between devices: 7.16 us -> 14.8 us
  local copies, waits for them, and re-layouts: 4.95 us -> 0.08 us
  other arithmetic: 3.65 us -> 0.34 us
  starting transfers between devices: 30.7 us -> 28.5 us
  between operations: 2.24 us -> 1.03 us
    pallas_call x6 -> x7, Pallas kernels: 57.2 us -> 37.3 us  [call(): pl.pallas_call(run, out_shape=tuple((shapes[o[0]](o[1], o[2]) for o in ou...]
    ppermute x28, waiting for transfers between devices: 7.16 us -> 14.8 us  [exchange(): return lax.ppermute(x, axis, [(i, i ^ step) for i in range(size)])]
    unnamed x48 -> x8, local copies, waits for them, and re-layouts: 2.54 us -> 0.03 us
    ppermute x28, starting transfers between devices: 30.7 us -> 28.5 us  [exchange(): return lax.ppermute(x, axis, [(i, i ^ step) for i in range(size)])]
    another operation x2, other arithmetic: 2.2 us -> 0.22 us
    slice x2 -> x0, local copies, waits for them, and re-layouts: 1.69 us -> none  [nothing(): return jnp.minimum(jnp.abs(value[(0,) * value.ndim].astype(F32)), 0.0)]
    mul x1 -> x0, other arithmetic: 1.34 us -> none  [on_device(): d_qkv = m_qkv * ln1_gain.astype(F32)[:, None]]
  transfers between devices with their start and end apart: 28 -> 28, of which waited for: 10 -> 13; matrix products, arithmetic and copies ran while one was open for 2% -> 0% of each run, Pallas kernels for 21% -> 18%
where the time goes in v3:
time: 82.3 us; the launch traced here: 82.1 us
  Pallas kernels  37.3 us (45%)
  starting transfers between devices  28.5 us (35%)
  waiting for transfers between devices  14.8 us (18%)
  between operations  1.03 us (1%)
    pallas_call x7, Pallas kernels, call(): pl.pallas_call(run, out_shape=tuple((shapes[o[0]](o[1], o[2]) for o in ou...  37.3 us
    ppermute x28, starting transfers between devices, exchange(): return lax.ppermute(x, axis, [(i, i ^ step) for i in range(size)])  28.5 us
    ppermute x28, waiting for transfers between devices, exchange(): return lax.ppermute(x, axis, [(i, i ^ step) for i in range(size)])  14.8 us
  transfers between devices with their start and end apart: 28, of which 13 were waited for; matrix products, arithmetic and copies ran while one was open for 0% of the time, Pallas kernels for 18%

profile of v3, /device:TPU:0, one launch (start us, length us, event | category | flops | bytes accessed | tf_op | source)
XLA Modules:
  0.0 82.1 jit_solution(10863852458173823598)
XLA Ops:
  0.6 1.1 %pack_weights.1 = (bf16[32,768]{1,0:T(8,128)(2,1)S(1)}, bf16[288,256]{1,0:T(8,128)(2,1)S(1)}) custom-call(bf16[32,768]{1,0:T(8,128)(2,1)} %refs_0_.6, bf16[1,32]{1,0:T(2,128)(2,1)} %bitcast.26, bf16[32,256]{1,0:T(8,128)(2,1)} %refs_2_.3, bf16[32,1024]{1,0:T(8,128)(2,1)} %refs_0_.7, bf16[128,256]{1,0:T(8,128)(2,1)} %refs_4_.3, bf16[1,32]{1,0:T(2,128)(2,1)} %bitcast.28), custom_call_target="tpu_custom_call" | custom-call | flops 1000000 | bytes 1048576 | tf_op jit(solution)/shard_map/pack_weights/pallas_call | solution.py:298
  1.7 5.1 %collective-permute-start.5 = (bf16[32,768]{1,0:T(8,128)(2,1)S(1)}, bf16[32,768]{1,0:T(8,128)(2,1)S(1)}, u32[]{:S(2)}, u32[]{:S(2)}) collective-permute-start(bf16[32,768]{1,0:T(8,128)(2,1)S(1)} %get-tuple-element.51.refs_3_), channel_id=1, source_target_pairs={{0,6},{1,7},{2,4},{3,5},{4,2},{5,3},{6,0},{7,1},{8,14},{9,15},{10,... | collective-permute-start | bytes 147464 | tf_op jit(solution)/shard_map/ppermute | solution.py:554
  6.9 0.6 collective-permute-start.1
  7.5 1.6 %collective-permute-done.5.refs_9_ = bf16[32,768]{1,0:T(8,128)(2,1)S(1)} collective-permute-done((bf16[32,768]{1,0:T(8,128)(2,1)S(1)}, bf16[32,768]{1,0:T(8,128)(2,1)S(1)}, u32[]{:S(2)}, u32[]{:S(2)}) %collective-permute-start.5) | collective-permute-done | bytes 49184 | tf_op jit(solution)/shard_map/ppermute | solution.py:554
  9.1 4.2 %collective-permute-start.9 = (bf16[288,256]{1,0:T(8,128)(2,1)S(1)}, bf16[288,256]{1,0:T(8,128)(2,1)S(1)}, u32[]{:S(2)}, u32[]{:S(2)}) collective-permute-start(bf16[288,256]{1,0:T(8,128)(2,1)S(1)} %get-tuple-element.55.refs_7_), channel_id=1, source_target_pairs={{0,6},{1,7},{2,4},{3,5},{4,2},{5,3},{6,0},{7,1},{8,14},{9,15},{10,... | collective-permute-start | bytes 442376 | tf_op jit(solution)/shard_map/ppermute | solution.py:554
  13.3 1.2 %collective-permute-start.7 = (bf16[288,256]{1,0:T(8,128)(2,1)S(1)}, bf16[288,256]{1,0:T(8,128)(2,1)S(1)}, u32[]{:S(2)}, u32[]{:S(2)}) collective-permute-start(bf16[288,256]{1,0:T(8,128)(2,1)S(1)} %get-tuple-element.55.refs_7_), channel_id=1, source_target_pairs={{0,2},{1,3},{2,0},{3,1},{4,6},{5,7},{6,4},{7,5},{8,10},{9,11},{10,... | collective-permute-start | bytes 442376 | tf_op jit(solution)/shard_map/ppermute | solution.py:554
  15.0 3.2 %prepare.1 = (f32[1024,256]{1,0:T(8,128)S(1)}, f32[1024,256]{1,0:T(8,128)S(1)}, f32[1024,256]{1,0:T(8,128)S(1)}, bf16[1024,256]{1,0:T(8,128)(2,1)S(1)}, f32[1024...) custom-call(s32[1,16]{1,0:T(1,128)} %refs_0_.4, s32[1,16]{1,0:T(1,128)} %refs_1_.1, f32[1024,256]{1,0:T(8,128)} %refs_2_.2, ...), custom_call_target="tpu_custom_call" | custom-call | flops 1000000000 | bytes 1048576 | tf_op jit(solution)/shard_map/prepare/pallas_call | solution.py:298
  18.3 3.6 %first_attention.1 = (bf16[8,4,256,256]{3,2,1,0:T(8,128)(2,1)S(1)}, bf16[1024,256]{1,0:T(8,128)(2,1)S(1)}, bf16[1152,256]{1,0:T(8,128)(2,1)S(1)}, bf16[9,256,128...) custom-call(s32[1]{0:T(128)} %bitcast.refs_0_, ...), custom_call_target="tpu_custom_call" | custom-call | flops 1000000000 | bytes 1048576 | tf_op jit(solution)/shard_map/first_attention/pallas_call | solution.py:298
  21.9 3.7 %collective-permute-done.8.refs_11_ = bf16[288,256]{1,0:T(8,128)(2,1)S(1)} collective-permute-done((bf16[288,256]{1,0:T(8,128)(2,1)S(1)}, bf16[288,256]{1,0:T(8,128)(2,1)S(1)}, u32[]{:S(2)}, u32[]{:S(2)}) %collective-permute-start.8) | collective-permute-done | bytes 147488 | tf_op jit(solution)/shard_map/ppermute | solution.py:554
  27.7 20.3 %middle_part.1 = (f32[1024,256]{1,0:T(8,128)}, f32[1024,256]{1,0:T(8,128)S(1)}, f32[1024,256]{1,0:T(8,128)S(1)}, bf16[1024,256]{1,0:T(8,128)(2,1)S(1)}, bf16[256...) custom-call(s32[1]{0:T(128)} %bitcast.refs_0_, ...), custom_call_target="tpu_custom_call" | custom-call | flops 24999999488 | bytes 1048576 | tf_op jit(solution)/shard_map/middle_part/pallas_call | solution.py:298
  48.4 1.7 %collective-permute-done.14 = bf16[4,288,256]{2,1,0:T(8,128)(2,1)S(1)} collective-permute-done((bf16[4,288,256]{2,1,0:T(8,128)(2,1)S(1)}, bf16[4,288,256]{2,1,0:T(8,128)(2,1)S(1)}, u32[]{:S(2)}, u32[]{:S(2)}) %collective-permute-start.14) | collective-permute-done | bytes 589856 | tf_op jit(solution)/shard_map/ppermute | solution.py:554
  50.3 2.7 %collective-permute-start.18 = (bf16[288,256]{1,0:T(8,128)(2,1)S(1)}, bf16[288,256]{1,0:T(8,128)(2,1)S(1)}, u32[]{:S(2)}, u32[]{:S(2)}) collective-permute-start(bf16[288,256]{1,0:T(8,128)(2,1)S(1)} %get-tuple-element.83.refs_18_), channel_id=1, source_target_pairs={{0,6},{1,7},{2,4},{3,5},{4,2},{5,3},{6,0},{7,1},{8,14},{9,15},{10,... | collective-permute-start | bytes 442376 | tf_op jit(solution)/shard_map/ppermute | solution.py:554
  53.0 1.7 %collective-permute-start.16 = (bf16[288,256]{1,0:T(8,128)(2,1)S(1)}, bf16[288,256]{1,0:T(8,128)(2,1)S(1)}, u32[]{:S(2)}, u32[]{:S(2)}) collective-permute-start(bf16[288,256]{1,0:T(8,128)(2,1)S(1)} %get-tuple-element.85.refs_16_), channel_id=1, source_target_pairs={{0,2},{1,3},{2,0},{3,1},{4,6},{5,7},{6,4},{7,5},{8,10},{9,11},{10,... | collective-permute-start | bytes 442376 | tf_op jit(solution)/shard_map/ppermute | solution.py:554
  54.7 7.5 %last_part.1 = (bf16[4,96,256]{2,1,0:T(8,128)(2,1)S(1)}, bf16[4,96,256]{2,1,0:T(8,128)(2,1)S(1)}, f32[1024,256]{1,0:T(8,128)}, f32[1024,256]{1,0:T(8,128)}) custom-call(s32[1]{0:T(128)} %bitcast.refs_0_, bf16[1024,256]{1,0:T(8,128)(2,1)S(1)} %get-tuple-element.60.refs_1_, bf16[256,256]{1,0:T(8,128)(2,1)S(1)} %get-tuple-element.61.refs_2_, ...), custom_call_target="tpu_custom_call" | custom-call | flops 10000000000 | bytes 1048576 | tf_op jit(solution)/shard_map/last_part/pallas_call | solution.py:298
  62.3 3.4 %collective-permute-done.17 = bf16[288,256]{1,0:T(8,128)(2,1)S(1)} collective-permute-done((bf16[288,256]{1,0:T(8,128)(2,1)S(1)}, bf16[288,256]{1,0:T(8,128)(2,1)S(1)}, u32[]{:S(2)}, u32[]{:S(2)}) %collective-permute-start.17) | collective-permute-done | bytes 147488 | tf_op jit(solution)/shard_map/ppermute | solution.py:554
  66.0 1.6 %collective-permute-start.21 = (bf16[96,256]{1,0:T(8,128)(2,1)S(1)}, bf16[96,256]{1,0:T(8,128)(2,1)S(1)}, u32[]{:S(2)}, u32[]{:S(2)}) collective-permute-start(bf16[96,256]{1,0:T(8,128)(2,1)S(1)} %get-tuple-element.88), channel_id=1, source_target_pairs={{0,6},{1,7},{2,4},{3,5},{4,2},{5,3},{6,0},{7,1},{8,14},{9,15},{10,... | collective-permute-start | bytes 147464 | tf_op jit(solution)/shard_map/ppermute | solution.py:554
  67.6 1.9 %collective-permute-start.20 = (bf16[96,256]{1,0:T(8,128)(2,1)S(1)}, bf16[96,256]{1,0:T(8,128)(2,1)S(1)}, u32[]{:S(2)}, u32[]{:S(2)}) collective-permute-start(bf16[96,256]{1,0:T(8,128)(2,1)S(1)} %get-tuple-element.89), channel_id=1, source_target_pairs={{0,4},{1,5},{2,6},{3,7},{4,0},{5,1},{6,2},{7,3},{8,12},{9,13},{10,... | collective-permute-start | bytes 147464 | tf_op jit(solution)/shard_map/ppermute | solution.py:554
  69.5 2.4 %collective-permute-start.27 = (bf16[288,256]{1,0:T(8,128)(2,1)S(1)}, bf16[288,256]{1,0:T(8,128)(2,1)S(1)}, u32[]{:S(2)}, u32[]{:S(2)}) collective-permute-start(bf16[288,256]{1,0:T(8,128)(2,1)S(1)} %add_convert_fusion.2.refs_2_), channel_id=1, source_target_pairs={{0,24},{8,16},{16,8},{24,0},{1,25},{9,17},{17,9},{25,1},{2,26},{10... | collective-permute-start | bytes 442376 | tf_op jit(solution)/shard_map/ppermute | solution.py:554
  72.9 1.0 %collective-permute-done.20 = bf16[96,256]{1,0:T(8,128)(2,1)S(1)} collective-permute-done((bf16[96,256]{1,0:T(8,128)(2,1)S(1)}, bf16[96,256]{1,0:T(8,128)(2,1)S(1)}, u32[]{:S(2)}, u32[]{:S(2)}) %collective-permute-start.20) | collective-permute-done | bytes 49184 | tf_op jit(solution)/shard_map/ppermute | solution.py:554
  74.0 2.5 %collective-permute-start.24 = (bf16[96,256]{1,0:T(8,128)(2,1)S(1)}, bf16[96,256]{1,0:T(8,128)(2,1)S(1)}, u32[]{:S(2)}, u32[]{:S(2)}) collective-permute-start(bf16[96,256]{1,0:T(8,128)(2,1)S(1)} %fusion.2.refs_2_), channel_id=1, source_target_pairs={{0,24},{8,16},{16,8},{24,0},{1,25},{9,17},{17,9},{25,1},{2,26},{10... | collective-permute-start | bytes 147464 | tf_op jit(solution)/shard_map/ppermute | solution.py:554
  77.0 0.9 %collective-permute-start.22 = (bf16[96,256]{1,0:T(8,128)(2,1)S(1)}, bf16[96,256]{1,0:T(8,128)(2,1)S(1)}, u32[]{:S(2)}, u32[]{:S(2)}) collective-permute-start(bf16[96,256]{1,0:T(8,128)(2,1)S(1)} %fusion.2.refs_2_), channel_id=1, source_target_pairs={{0,8},{8,0},{16,24},{24,16},{1,9},{9,1},{17,25},{25,17},{2,10},{10... | collective-permute-start | bytes 147464 | tf_op jit(solution)/shard_map/ppermute | solution.py:554
  77.9 0.8 collective-permute-done.26.refs_4_
  78.7 0.9 %finished_rest.1 = (f32[32,1024]{1,0:T(8,128)}, f32[1,32]{1,0:T(1,128)}, f32[32,256]{1,0:T(8,128)}, f32[128,256]{1,0:T(8,128)}) custom-call(bf16[32,1024]{1,0:T(8,128)(2,1)S(1)} %copy-done, bf16[1,32]{1,0:T(2,128)(2,1)S(1)} %bitcast.29, bf16[288,256]{1,0:T(8,128)(2,1)S(1)} %add_convert_fusion.2.refs_2_, ...), custom_call_target="tpu_custom_call" | custom-call | flops 1000000 | bytes 1048576 | tf_op jit(solution)/shard_map/finished_rest/pallas_call | solution.py:298
  81.1 0.8 finished_qkv.1
  (54 shorter events, 6.6 us)
Async XLA Ops:
  1.7 7.3 %collective-permute-start.5 = (bf16[32,768]{1,0:T(8,128)(2,1)S(1)}, bf16[32,768]{1,0:T(8,128)(2,1)S(1)}, u32[]{:S(2)}, u32[]{:S(2)}) collective-permute-start(bf16[32,768]{1,0:T(8,128)(2,1)S(1)} %get-tuple-element.51.refs_3_), channel_id=1, source_target_pairs={{0,6},{1,7},{2,4},{3,5},{4,2},{5,3},{6,0},{7,1},{8,14},{9,15},{10,... | collective-permute-start | bytes 147464 | tf_op jit(solution)/shard_map/ppermute | solution.py:554
  6.9 6.4 %collective-permute-start.3 = (bf16[32,768]{1,0:T(8,128)(2,1)S(1)}, bf16[32,768]{1,0:T(8,128)(2,1)S(1)}, u32[]{:S(2)}, u32[]{:S(2)}) collective-permute-start(bf16[32,768]{1,0:T(8,128)(2,1)S(1)} %get-tuple-element.51.refs_3_), channel_id=1, source_target_pairs={{0,4},{1,5},{2,6},{3,7},{4,0},{5,1},{6,2},{7,3},{8,12},{9,13},{10,... | collective-permute-start | bytes 147464 | tf_op jit(solution)/shard_map/ppermute | solution.py:554
  6.9 6.4 %collective-permute-start.1 = (bf16[32,768]{1,0:T(8,128)(2,1)S(1)}, bf16[32,768]{1,0:T(8,128)(2,1)S(1)}, u32[]{:S(2)}, u32[]{:S(2)}) collective-permute-start(bf16[32,768]{1,0:T(8,128)(2,1)S(1)} %get-tuple-element.51.refs_3_), channel_id=1, source_target_pairs={{0,2},{1,3},{2,0},{3,1},{4,6},{5,7},{6,4},{7,5},{8,10},{9,11},{10,... | collective-permute-start | bytes 147464 | tf_op jit(solution)/shard_map/ppermute | solution.py:554
  7.5 7.0 %collective-permute-start = (bf16[32,768]{1,0:T(8,128)(2,1)S(1)}, bf16[32,768]{1,0:T(8,128)(2,1)S(1)}, u32[]{:S(2)}, u32[]{:S(2)}) collective-permute-start(bf16[32,768]{1,0:T(8,128)(2,1)S(1)} %get-tuple-element.51.refs_3_), channel_id=1, source_target_pairs={{0,1},{1,0},{2,3},{3,2},{4,5},{5,4},{6,7},{7,6},{8,9},{9,8},{10,11... | collective-permute-start | bytes 147464 | tf_op jit(solution)/shard_map/ppermute | solution.py:554
  9.1 5.4 %collective-permute-start.6 = (bf16[32,768]{1,0:T(8,128)(2,1)S(1)}, bf16[32,768]{1,0:T(8,128)(2,1)S(1)}, u32[]{:S(2)}, u32[]{:S(2)}) collective-permute-start(bf16[32,768]{1,0:T(8,128)(2,1)S(1)} %collective-permute-done.5.refs_9_), channel_id=1, source_target_pairs={{0,1},{1,0},{2,3},{3,2},{4,5},{5,4},{6,7},{7,6},{8,9},{9,8},{10,11... | collective-permute-start | bytes 147464 | tf_op jit(solution)/shard_map/ppermute | solution.py:554
  9.1 12.8 %collective-permute-start.9 = (bf16[288,256]{1,0:T(8,128)(2,1)S(1)}, bf16[288,256]{1,0:T(8,128)(2,1)S(1)}, u32[]{:S(2)}, u32[]{:S(2)}) collective-permute-start(bf16[288,256]{1,0:T(8,128)(2,1)S(1)} %get-tuple-element.55.refs_7_), channel_id=1, source_target_pairs={{0,6},{1,7},{2,4},{3,5},{4,2},{5,3},{6,0},{7,1},{8,14},{9,15},{10,... | collective-permute-start | bytes 442376 | tf_op jit(solution)/shard_map/ppermute | solution.py:554
  13.3 12.3 %collective-permute-start.8 = (bf16[288,256]{1,0:T(8,128)(2,1)S(1)}, bf16[288,256]{1,0:T(8,128)(2,1)S(1)}, u32[]{:S(2)}, u32[]{:S(2)}) collective-permute-start(bf16[288,256]{1,0:T(8,128)(2,1)S(1)} %get-tuple-element.55.refs_7_), channel_id=1, source_target_pairs={{0,4},{1,5},{2,6},{3,7},{4,0},{5,1},{6,2},{7,3},{8,12},{9,13},{10,... | collective-permute-start | bytes 442376 | tf_op jit(solution)/shard_map/ppermute | solution.py:554
  13.3 12.3 %collective-permute-start.7 = (bf16[288,256]{1,0:T(8,128)(2,1)S(1)}, bf16[288,256]{1,0:T(8,128)(2,1)S(1)}, u32[]{:S(2)}, u32[]{:S(2)}) collective-permute-start(bf16[288,256]{1,0:T(8,128)(2,1)S(1)} %get-tuple-element.55.refs_7_), channel_id=1, source_target_pairs={{0,2},{1,3},{2,0},{3,1},{4,6},{5,7},{6,4},{7,5},{8,10},{9,11},{10,... | collective-permute-start | bytes 442376 | tf_op jit(solution)/shard_map/ppermute | solution.py:554
  14.5 3.7 %collective-permute-start.4 = (bf16[32,768]{1,0:T(8,128)(2,1)S(1)}, bf16[32,768]{1,0:T(8,128)(2,1)S(1)}, u32[]{:S(2)}, u32[]{:S(2)}) collective-permute-start(bf16[32,768]{1,0:T(8,128)(2,1)S(1)} %collective-permute-done.3.refs_7_), channel_id=1, source_target_pairs={{0,1},{1,0},{2,3},{3,2},{4,5},{5,4},{6,7},{7,6},{8,9},{9,8},{10,11... | collective-permute-start | bytes 147464 | tf_op jit(solution)/shard_map/ppermute | solution.py:554
  14.5 3.7 %collective-permute-start.2 = (bf16[32,768]{1,0:T(8,128)(2,1)S(1)}, bf16[32,768]{1,0:T(8,128)(2,1)S(1)}, u32[]{:S(2)}, u32[]{:S(2)}) collective-permute-start(bf16[32,768]{1,0:T(8,128)(2,1)S(1)} %collective-permute-done.1.refs_5_), channel_id=1, source_target_pairs={{0,1},{1,0},{2,3},{3,2},{4,5},{5,4},{6,7},{7,6},{8,9},{9,8},{10,11... | collective-permute-start | bytes 147464 | tf_op jit(solution)/shard_map/ppermute | solution.py:554
  48.0 2.1 %collective-permute-start.14 = (bf16[4,288,256]{2,1,0:T(8,128)(2,1)S(1)}, bf16[4,288,256]{2,1,0:T(8,128)(2,1)S(1)}, u32[]{:S(2)}, u32[]{:S(2)}) collective-permute-start(bf16[4,288,256]{2,1,0:T(8,128)(2,1)S(1)} %get-tuple-element.72), channel_id=1, source_target_pairs={{0,1},{1,0},{2,3},{3,2},{4,5},{5,4},{6,7},{7,6},{8,9},{9,8},{10,11... | collective-permute-start | bytes 1769480 | tf_op jit(solution)/shard_map/ppermute | solution.py:554
  50.3 12.0 %collective-permute-start.18 = (bf16[288,256]{1,0:T(8,128)(2,1)S(1)}, bf16[288,256]{1,0:T(8,128)(2,1)S(1)}, u32[]{:S(2)}, u32[]{:S(2)}) collective-permute-start(bf16[288,256]{1,0:T(8,128)(2,1)S(1)} %get-tuple-element.83.refs_18_), channel_id=1, source_target_pairs={{0,6},{1,7},{2,4},{3,5},{4,2},{5,3},{6,0},{7,1},{8,14},{9,15},{10,... | collective-permute-start | bytes 442376 | tf_op jit(solution)/shard_map/ppermute | solution.py:554
  53.0 12.7 %collective-permute-start.17 = (bf16[288,256]{1,0:T(8,128)(2,1)S(1)}, bf16[288,256]{1,0:T(8,128)(2,1)S(1)}, u32[]{:S(2)}, u32[]{:S(2)}) collective-permute-start(bf16[288,256]{1,0:T(8,128)(2,1)S(1)} %get-tuple-element.84.refs_17_), channel_id=1, source_target_pairs={{0,4},{1,5},{2,6},{3,7},{4,0},{5,1},{6,2},{7,3},{8,12},{9,13},{10,... | collective-permute-start | bytes 442376 | tf_op jit(solution)/shard_map/ppermute | solution.py:554
  53.0 12.7 %collective-permute-start.16 = (bf16[288,256]{1,0:T(8,128)(2,1)S(1)}, bf16[288,256]{1,0:T(8,128)(2,1)S(1)}, u32[]{:S(2)}, u32[]{:S(2)}) collective-permute-start(bf16[288,256]{1,0:T(8,128)(2,1)S(1)} %get-tuple-element.85.refs_16_), channel_id=1, source_target_pairs={{0,2},{1,3},{2,0},{3,1},{4,6},{5,7},{6,4},{7,5},{8,10},{9,11},{10,... | collective-permute-start | bytes 442376 | tf_op jit(solution)/shard_map/ppermute | solution.py:554
  62.2 3.6 %collective-permute-start.15 = (bf16[4,96,256]{2,1,0:T(8,128)(2,1)S(1)}, bf16[4,96,256]{2,1,0:T(8,128)(2,1)S(1)}, u32[]{:S(2)}, u32[]{:S(2)}) collective-permute-start(bf16[4,96,256]{2,1,0:T(8,128)(2,1)S(1)} %get-tuple-element.76), channel_id=1, source_target_pairs={{0,1},{1,0},{2,3},{3,2},{4,5},{5,4},{6,7},{7,6},{8,9},{9,8},{10,11... | collective-permute-start | bytes 589832 | tf_op jit(solution)/shard_map/ppermute | solution.py:554
  65.9 6.5 %collective-permute-start.19 = (bf16[96,256]{1,0:T(8,128)(2,1)S(1)}, bf16[96,256]{1,0:T(8,128)(2,1)S(1)}, u32[]{:S(2)}, u32[]{:S(2)}) collective-permute-start(bf16[96,256]{1,0:T(8,128)(2,1)S(1)} %get-tuple-element.87), channel_id=1, source_target_pairs={{0,2},{1,3},{2,0},{3,1},{4,6},{5,7},{6,4},{7,5},{8,10},{9,11},{10,... | collective-permute-start | bytes 147464 | tf_op jit(solution)/shard_map/ppermute | solution.py:554
  66.0 7.0 %collective-permute-start.21 = (bf16[96,256]{1,0:T(8,128)(2,1)S(1)}, bf16[96,256]{1,0:T(8,128)(2,1)S(1)}, u32[]{:S(2)}, u32[]{:S(2)}) collective-permute-start(bf16[96,256]{1,0:T(8,128)(2,1)S(1)} %get-tuple-element.88), channel_id=1, source_target_pairs={{0,6},{1,7},{2,4},{3,5},{4,2},{5,3},{6,0},{7,1},{8,14},{9,15},{10,... | collective-permute-start | bytes 147464 | tf_op jit(solution)/shard_map/ppermute | solution.py:554
  67.6 6.4 %collective-permute-start.20 = (bf16[96,256]{1,0:T(8,128)(2,1)S(1)}, bf16[96,256]{1,0:T(8,128)(2,1)S(1)}, u32[]{:S(2)}, u32[]{:S(2)}) collective-permute-start(bf16[96,256]{1,0:T(8,128)(2,1)S(1)} %get-tuple-element.89), channel_id=1, source_target_pairs={{0,4},{1,5},{2,6},{3,7},{4,0},{5,1},{6,2},{7,3},{8,12},{9,13},{10,... | collective-permute-start | bytes 147464 | tf_op jit(solution)/shard_map/ppermute | solution.py:554
  69.5 7.6 %collective-permute-start.27 = (bf16[288,256]{1,0:T(8,128)(2,1)S(1)}, bf16[288,256]{1,0:T(8,128)(2,1)S(1)}, u32[]{:S(2)}, u32[]{:S(2)}) collective-permute-start(bf16[288,256]{1,0:T(8,128)(2,1)S(1)} %add_convert_fusion.2.refs_2_), channel_id=1, source_target_pairs={{0,24},{8,16},{16,8},{24,0},{1,25},{9,17},{17,9},{25,1},{2,26},{10... | collective-permute-start | bytes 442376 | tf_op jit(solution)/shard_map/ppermute | solution.py:554
  71.9 6.8 %collective-permute-start.26 = (bf16[288,256]{1,0:T(8,128)(2,1)S(1)}, bf16[288,256]{1,0:T(8,128)(2,1)S(1)}, u32[]{:S(2)}, u32[]{:S(2)}) collective-permute-start(bf16[288,256]{1,0:T(8,128)(2,1)S(1)} %add_convert_fusion.2.refs_2_), channel_id=1, source_target_pairs={{0,16},{8,24},{16,0},{24,8},{1,17},{9,25},{17,1},{25,9},{2,18},{10... | collective-permute-start | bytes 442376 | tf_op jit(solution)/shard_map/ppermute | solution.py:554
  72.4 6.3 %collective-permute-start.25 = (bf16[288,256]{1,0:T(8,128)(2,1)S(1)}, bf16[288,256]{1,0:T(8,128)(2,1)S(1)}, u32[]{:S(2)}, u32[]{:S(2)}) collective-permute-start(bf16[288,256]{1,0:T(8,128)(2,1)S(1)} %add_convert_fusion.2.refs_2_), channel_id=1, source_target_pairs={{0,8},{8,0},{16,24},{24,16},{1,9},{9,1},{17,25},{25,17},{2,10},{10... | collective-permute-start | bytes 442376 | tf_op jit(solution)/shard_map/ppermute | solution.py:554
  74.0 6.2 %collective-permute-start.24 = (bf16[96,256]{1,0:T(8,128)(2,1)S(1)}, bf16[96,256]{1,0:T(8,128)(2,1)S(1)}, u32[]{:S(2)}, u32[]{:S(2)}) collective-permute-start(bf16[96,256]{1,0:T(8,128)(2,1)S(1)} %fusion.2.refs_2_), channel_id=1, source_target_pairs={{0,24},{8,16},{16,8},{24,0},{1,25},{9,17},{17,9},{25,1},{2,26},{10... | collective-permute-start | bytes 147464 | tf_op jit(solution)/shard_map/ppermute | solution.py:554
  76.5 4.2 %collective-permute-start.23 = (bf16[96,256]{1,0:T(8,128)(2,1)S(1)}, bf16[96,256]{1,0:T(8,128)(2,1)S(1)}, u32[]{:S(2)}, u32[]{:S(2)}) collective-permute-start(bf16[96,256]{1,0:T(8,128)(2,1)S(1)} %fusion.2.refs_2_), channel_id=1, source_target_pairs={{0,16},{8,24},{16,0},{24,8},{1,17},{9,25},{17,1},{25,9},{2,18},{10... | collective-permute-start | bytes 147464 | tf_op jit(solution)/shard_map/ppermute | solution.py:554
  77.0 4.1 %collective-permute-start.22 = (bf16[96,256]{1,0:T(8,128)(2,1)S(1)}, bf16[96,256]{1,0:T(8,128)(2,1)S(1)}, u32[]{:S(2)}, u32[]{:S(2)}) collective-permute-start(bf16[96,256]{1,0:T(8,128)(2,1)S(1)} %fusion.2.refs_2_), channel_id=1, source_target_pairs={{0,8},{8,0},{16,24},{24,16},{1,9},{9,1},{17,25},{25,17},{2,10},{10... | collective-permute-start | bytes 147464 | tf_op jit(solution)/shard_map/ppermute | solution.py:554
  (8 other events, 69.7 us)

commit v4 on v3

--- a/solution.py
+++ b/solution.py
@@ -19,8 +19,8 @@
 LN2 = 0.6931471805599453
 GELU_A = 0.7978845608028654
 GELU_B = GELU_A * 0.044715
-FLOPS_FIRST = 10 ** 9
-FLOPS_PREPARE = 10 ** 9
+FLOPS_FIRST = 10 ** 6
+FLOPS_PREPARE = 10 ** 6
 FLOPS_LAST = 10 ** 10
 LIMIT_MIDDLE = 40
 LIMIT_LAST = 16
@@ -331,66 +331,66 @@
 
 SAVED = ("e", "n1", "r1", "qs", "vp", "kt", "ht", "linv")
 
-def prepare(lengths, counts, states, inject, cot):
+def prepare(lengths, states, inject):
     t, d = states.shape
     nb, nc = t // BLK, t // CHUNK
     def kernel(m, s):
-        len_ref, cnt_ref, st, inj, ct = m.ins
-        ent, inj_out, g, n1, r1, mask = m.outs
-        m.wait(0, 1)
+        len_ref, st, inj = m.ins
+        n1, r1, mask = m.outs
+        m.wait(0)
         make_masks(len_ref, mask, nb)
-        m.wait(2, 3)
+        m.wait(1, 2)
         for j in range(nc):
             at = slice(j * CHUNK, (j + 1) * CHUNK)
-            x = st[at, :] + inj[at, :]
-            ent[at, :] = x
-            inj_out[at, :] = inj[at, :]
-            n, r = ln_fwd(x)
+            n, r = ln_fwd(st[at, :] + inj[at, :])
             n1[at, :] = n.astype(BF)
             r1[at, :] = jnp.broadcast_to(r, (CHUNK, 128))
-        m.wait(4)
-        for j in range(nc):
-            at = slice(j * CHUNK, (j + 1) * CHUNK)
-            g[at, :] = weigh(cnt_ref, len_ref, j, ct[at, :])
-    outs = [("vmem", (t, d), F32)] * 3 + [("vmem", (t, d), BF), ("vmem", (t, 128), F32), ("vmem", (nb, 2 * BLK, BLK), F32)]
-    args = [("load", v) for v in (lengths, counts, states, inject, cot)]
+    outs = [("vmem", (t, d), BF), ("vmem", (t, 128), F32), ("vmem", (nb, 2 * BLK, BLK), F32)]
+    args = [("load", v) for v in (lengths, states, inject)]
     return call(kernel, outs, args, {}, "prepare", FLOPS_PREPARE)
 
-def first_attention(me, n1, mask, qkv_parts, ff):
+def first_attention(me, lengths, counts, states, inject, cot, n1, mask, qkv_parts, ff):
     t, d = n1.shape
     nb, nc = t // BLK, t // CHUNK
     shapes = saved_shapes(t, d, ff)
     made = [k for k in SAVED if k not in ("n1", "r1")]
     scratch = {k: v for k, v in shapes.items() if k not in SAVED}
     def kernel(m, s):
-        me_ref, n1_ref, mask_ref = m.ins[:3]
+        me_ref, len_ref, cnt_ref, st, inj, ct, n1_ref, mask_ref = m.ins[:8]
         vars(s).update(zip(made, m.outs))
-        wqkv = m.outs[-1]
+        wqkv, ent, inj_out, weighed = m.outs[-4:]
         pad_zero(s)
-        place_qkv(me_ref[0], m.ins[3:], wqkv)
+        place_qkv(me_ref[0], m.ins[8:], wqkv)
         for j in range(nc):
             pack_heads(s, j, n1_ref[j * CHUNK:(j + 1) * CHUNK, :], wqkv)
-        for i in range(0, nb, 2):
-            attend(s, (i, i + 1), mask_ref)
-    outs = [("vmem",) + shapes[k] for k in made] + [("vmem", (d, 3 * d), BF)]
-    args = [("smem", me), ("vmem", n1), ("vmem", mask)] + [("vmem", p) for p in qkv_parts]
+        for i in range(0, nb, 4):
+            attend(s, (i, i + 1, i + 2, i + 3), mask_ref)
+        m.wait(1, 2, 3, 4, 5)
+        for j in range(nc):
+            at = slice(j * CHUNK, (j + 1) * CHUNK)
+            ent[at, :] = st[at, :] + inj[at, :]
+            inj_out[at, :] = inj[at, :]
+            weighed[at, :] = weigh(cnt_ref, len_ref, j, ct[at, :])
+    outs = [("vmem",) + shapes[k] for k in made] + [("vmem", (d, 3 * d), BF)] + [("vmem", (t, d), F32)] * 3
+    args = [("smem", me)] + [("load", v) for v in (lengths, counts, states, inject, cot)] + [("vmem", v) for v in (n1, mask, *qkv_parts)]
     got = call(kernel, outs, args, scratch, "first_attention", FLOPS_FIRST)
-    return dict(zip(made, got)), got[-1]
+    return dict(zip(made, got)), got[-4], got[-3:]
 
 def middle_part(me, ent, inject, weighed, mask, wqkv, ht, rest_parts, ff):
     t, d = ent.shape
     nb, nc = t // BLK, t // CHUNK
     parts = len(rest_parts)
     sh = {"a_" + k: v for k, v in more_shapes(t, d, ff).items() if k not in ("dpk", "gm")}
-    sh.update({"b_" + k: v for k, v in {**saved_shapes(t, d, ff), **more_shapes(t, d, ff)}.items()})
+    sh.update({"b_" + k: v for k, v in {**saved_shapes(t, d, ff), **more_shapes(t, d, ff)}.items() if k not in ("n1", "dpk", "ht", "gm")})
     sh.update(state=((t, d), F32), dk=((t + BLK, d), F32), dv=((t + BLK, d), F32),
               wqkv_t=((3 * d, d), BF), wup_t=((ff, d), BF), wdown_t=((d, ff), BF), tr=((2, d, t), BF),
-              wup=((d, ff), BF), wdown=((ff, d), BF), mout=((d, d), BF), mup=((d, ff), BF), mdown_t=((d, ff), BF), mdown=((ff, d), BF))
+              wup=((d, ff), BF), wdown=((ff, d), BF), mup=((d, ff), BF), mdown_t=((d, ff), BF), mdown=((ff, d), BF))
     def kernel(m, x):
         me_ref, ent_ref, inj, weighed_ref, x.mask, wqkv_ref, ht_ref = m.ins[:7]
-        final, g, ginj, gm, wout, mqkv, keep, send = m.outs
+        final, g, ginj, gm, wout, n1, dpk, ht, gm_two, keep, send = m.outs
         its = [types.SimpleNamespace(**{k[2:]: v for k, v in vars(x).items() if k.startswith(p)}) for p in ("a_", "b_")]
         its[0].ht, its[0].gm = ht_ref, gm
+        its[1].n1, its[1].dpk, its[1].ht, its[1].gm = n1, dpk, ht, gm_two
         place_rest(me_ref[0], m.ins[7:], wout, x.wup, x.wdown)
         x.wup_t[...] = x.wup[...].T
         x.wdown_t[...] = x.wdown[...].T
@@ -406,7 +406,7 @@
             project(its[1], j, x.state[rows_of(j), :] + inj[rows_of(j), :], wqkv_ref)
         def blocks_of(j):
             n = CHUNK // BLK
-            return [tuple(range(j * n + b, min(j * n + b + 2, j * n + n))) for b in range(0, n, 2)]
+            return [tuple(range(j * n, j * n + n))]
         def attend_of(j):
             for blocks in blocks_of(j):
                 attend(its[1], blocks, x.mask)
@@ -446,39 +446,39 @@
         weight_grad([s.g2 for s in its], [s.act for s in its], x.mdown_t)
         x.mdown[...] = x.mdown_t[...].T
         weight_grad([s.n2 for s in its], [s.gp for s in its], x.mup)
-        weight_grad([its[1].n1], [its[1].dpk], mqkv)
-        total = None
-        for s in its:
-            for b in range(nb):
-                part = dot(s.ht[b], s.gm[b * BLK:(b + 1) * BLK, :])
-                total = part if total is None else total + part
-        x.mout[...] = total.astype(BF)
-        hand_out(me_ref[0], parts, (x.mout, x.mup, x.mdown), keep, send)
-    piece = ("vmem", (max(parts // 2, 1), (d + ff) // parts + ff // parts, d), BF)
-    outs = [("store", (t, d), F32)] + [("vmem", (t, d), F32)] * 2 + [("vmem", (t, d), BF), ("vmem", (d, d), BF), ("vmem", (d, 3 * d), F32)] + [piece] * 2
+        hand_out(me_ref[0], parts, (x.mup, x.mdown), keep, send)
+    piece = ("vmem", (max(parts // 2, 1), 2 * ff // parts, d), BF)
+    outs = [("store", (t, d), F32)] + [("vmem", (t, d), F32)] * 2 + [("vmem", (t, d), BF), ("vmem", (d, d), BF), ("vmem", (t, d), BF), ("vmem", (t, 3 * d), BF)] + [("vmem", (nb, d, BLK), BF), ("vmem", (t, d), BF)] + [piece] * 2
     args = [("smem", me)] + [("vmem", v) for v in (ent, inject, weighed, mask, wqkv, ht, *rest_parts)]
     return call(kernel, outs, args, sh, "middle_part", 25 * 10 ** 9, limit=LIMIT_MIDDLE)
 
-def last_part(me, saved, gm, wout, wqkv, mqkv, g, ginj, parts, ff, first):
+def last_part(me, saved, gm, wout, wqkv, n1, dpk, ht, gm_two, g, ginj, parts, ff, first):
     t, d = gm.shape
     nb, nc = t // BLK, t // CHUNK
-    scratch = dict(dk=((t + BLK, d), F32), dv=((t + BLK, d), F32), tr=((d, t), BF), mat=((d, 3 * d), BF), wt=((3 * d, d), BF), dpk=((t, 3 * d), BF))
+    scratch = dict(dk=((t + BLK, d), F32), dv=((t + BLK, d), F32), tr=((2, d, t), BF), mat=((d, 3 * d), BF), mout=((d, d), BF), wt=((3 * d, d), BF), dpk=((t, 3 * d), BF))
     def kernel(m, s):
-        me_ref, s.gm, wout_ref, w_ref, m_ref, g_ref, gi_ref = m.ins[:7]
-        vars(s).update(zip(SAVED, m.ins[7:]))
+        me_ref, s.gm, wout_ref, w_ref, n1_ref, dpk_ref, ht_ref, gm_ref, g_ref, gi_ref = m.ins[:10]
+        vars(s).update(zip(SAVED, m.ins[10:]))
         keep, send, grad, grad_inject = m.outs
         s.dk[0:BLK, :] = jnp.zeros((BLK, d), F32)
         s.dv[0:BLK, :] = jnp.zeros((BLK, d), F32)
-        for i in range(0, nb, 2):
-            attend_back(s, (i, i + 1), wout_ref, s.dk, s.dv)
-        s.tr[...] = s.n1[...].T
+        for i in range(0, nb, 4):
+            attend_back(s, (i, i + 1, i + 2, i + 3), wout_ref, s.dk, s.dv)
+        s.tr[0] = s.n1[...].T
+        s.tr[1] = n1_ref[...].T
         s.wt[...] = w_ref[...].T
         loop(nc, lambda j: finish_packed(s, j, s.dk, s.dv))
         def tile(c):
             cc = slice(c * 256, (c + 1) * 256)
-            s.mat[:, cc] = (m_ref[:, cc] + dot(s.tr[...], s.dpk[:, cc])).astype(BF)
+            s.mat[:, cc] = (dot(s.tr[0], s.dpk[:, cc]) + dot(s.tr[1], dpk_ref[:, cc])).astype(BF)
         loop(3, tile)
-        hand_out(me_ref[0], parts, (s.mat,), keep, send)
+        total = None
+        for left, right in ((s.ht, s.gm), (ht_ref, gm_ref)):
+            for b in range(nb):
+                part = dot(left[b], right[b * BLK:(b + 1) * BLK, :])
+                total = part if total is None else total + part
+        s.mout[...] = total.astype(BF)
+        hand_out(me_ref[0], parts, (s.mout, s.mat), keep, send)
         def chunk(j):
             at = rows(j * CHUNK, CHUNK)
             new = project_back(s, j, g_ref[at, :], s.wt)
@@ -487,8 +487,8 @@
         loop(nc, chunk)
         m.put(2)
         m.put(3)
-    outs = [("vmem", (max(parts // 2, 1), 3 * d // parts, d), BF)] * 2 + [("store", (t, d), F32)] * 2
-    args = [("smem", me)] + [("vmem", v) for v in (gm, wout, wqkv, mqkv, g, ginj)]
+    outs = [("vmem", (max(parts // 2, 1), 4 * d // parts, d), BF)] * 2 + [("store", (t, d), F32)] * 2
+    args = [("smem", me)] + [("vmem", v) for v in (gm, wout, wqkv, n1, dpk, ht, gm_two, g, ginj)]
     args += [("vmem", saved[k]) for k in SAVED] + [("any", v) for v in first]
     return call(kernel, outs, args, scratch, "last_part", FLOPS_LAST, limit=LIMIT_LAST)
 
@@ -528,6 +528,7 @@
     r, cols = weight.shape
     d = shares[0].shape[1]
     n = cols // d
+    others = [(lo, size) for lo, size in ((0, lead), (lead + n * r, tail)) if size]
     def kernel(m, s):
         w, g, parts = m.ins[0], to_column(m.ins[1][...].astype(F32)), m.ins[2:]
         along = jnp.zeros((r, 1), F32)
@@ -538,12 +539,10 @@
         m.put(0)
         m.outs[1][...] = to_row(along)
         m.put(1)
-        if lead:
-            m.outs[2][...] = sum_parts(parts, 0, lead)
-            m.outs[3][...] = sum_parts(parts, lead + n * r, tail)
-            m.put(2)
-            m.put(3)
-    outs = [("store", (r, cols), F32), ("store", (1, r), F32)] + ([("store", (lead, d), F32), ("store", (tail, d), F32)] if lead else [])
+        for at, (lo, size) in enumerate(others):
+            m.outs[2 + at][...] = sum_parts(parts, lo, size)
+            m.put(2 + at)
+    outs = [("store", (r, cols), F32), ("store", (1, r), F32)] + [("store", (size, d), F32) for _, size in others]
     got = call(kernel, outs, [("vmem", v) for v in (weight, gain.reshape(1, -1), *shares)], {}, name, 10 ** 6)
     return [got[0], got[1].reshape(r)] + list(got[2:])
 
@@ -566,7 +565,7 @@
     return [total[k].astype(BF) for k in range(keep.shape[0])]
 
 def send_far(summed, size):
-    return [exchange(summed[k], "fsdp", size, 2 * k) for k in range(1, size // 2)]
+    return [exchange(summed[k], "fsdp", size, 2 * k) for k in range(size // 2 - 1, 0, -1)]
 
 def along_dp(share, size):
     return [share] + [exchange(share, "dp", size, k) for k in range(1, size)]
@@ -575,7 +574,7 @@
     return [exchange(p, "fsdp", size, 1) for p in pieces[1::2]]
 
 def send_far(summed, size):
-    return [exchange(summed[k], "fsdp", size, 2 * k) for k in range(1, size // 2)]
+    return [exchange(summed[k], "fsdp", size, 2 * k) for k in range(size // 2 - 1, 0, -1)]
 
 def reduce_whole(whole, sizes):
     out, lo = [], 0
@@ -594,38 +593,40 @@
         own_qkv, own_rest = pack_weights(w_qkv, ln1_gain, w_out, w_up, w_down, ln2_gain)
         qkv_far = far_parts(own_qkv, n_fsdp)
         rest_far = far_parts(own_rest, n_fsdp)
-        qkv_parts = with_near(qkv_far, n_fsdp)
     else:
         me = jnp.zeros((1,), jnp.int32)
         full = lambda v: lax.all_gather(v, "fsdp", axis=0, tiled=True)
         up = full((w_up.astype(F32) * ln2_gain.astype(F32)[:, None]).astype(BF))
         qkv_parts = [full((w_qkv.astype(F32) * ln1_gain.astype(F32)[:, None]).astype(BF))]
         rest_parts = [jnp.concatenate([full(w_out)] + [up[:, c:c + d] for c in range(0, ff, d)] + [full(w_down)], axis=0)]
+    n1, r1, mask = prepare(prompt_lengths, states, inject)
+    if direct:
+        qkv_parts = with_near(qkv_far[:1], n_fsdp) + with_near(after(qkv_far[1:], n1), n_fsdp)
     parts = len(qkv_parts)
-    ent, inject, weighed, n1, r1, mask = prepare(prompt_lengths, loop_counts, states, inject, cotangent)
-    saved, wqkv = first_attention(me, n1, mask, qkv_parts, ff)
+    saved, wqkv, entering = first_attention(me, prompt_lengths, loop_counts, states, inject, cotangent, n1, mask, qkv_parts, ff)
     saved.update(n1=n1, r1=r1)
     if direct:
         rest_parts = with_near(after(rest_far, wqkv), n_fsdp)
-    final, g, ginj, gm, wout, mqkv, keep, send = middle_part(
-        me, ent, inject, weighed, mask, wqkv, saved["ht"], rest_parts, ff)
+    final, g, ginj, gm, wout, n1, dpk, ht, gm_two, keep, send = middle_part(
+        me, *entering, mask, wqkv, saved["ht"], rest_parts, ff)
     summed = []
     if direct:
         summed = sum_near(keep, exchange(send, "fsdp", n_fsdp, 1))
         far = send_far(summed, n_fsdp)
     else:
-        shares = [reduce_whole(keep[0], [d] * (1 + ff // d) + [ff])]
-    keep_qkv, send_qkv, grad_states, grad_inject = last_part(me, saved, gm, wout, wqkv, mqkv, g, ginj, parts, ff, summed)
+        shares = [reduce_whole(keep[0], [d] * (ff // d) + [ff])]
+    keep_qkv, send_qkv, grad_states, grad_inject = last_part(
+        me, saved, gm, wout, wqkv, n1, dpk, ht, gm_two, g, ginj, parts, ff, summed)
     if direct:
         near = exchange(send_qkv, "fsdp", n_fsdp, 1)
         share = sum_parts([summed[0], *far], 0, summed[0].shape[0]).astype(BF)
         shares = along_dp(share, n_dp)
         summed = sum_near(keep_qkv, near, share)
-        shares_qkv = along_dp(sum_parts([summed[0], *send_far(summed, n_fsdp)], 0, 3 * r).astype(BF), n_dp)
+        shares_qkv = along_dp(sum_parts([summed[0], *send_far(summed, n_fsdp)], 0, 4 * r).astype(BF), n_dp)
     else:
-        shares_qkv = [reduce_whole(keep_qkv[0], [d] * 3)]
-    d_up, d_gain_two, d_out, d_down = finished(shares, w_up, ln2_gain, r, w_down.shape[0], "finished_rest")
-    d_qkv, d_gain_one = finished(shares_qkv, w_qkv, ln1_gain, 0, 0, "finished_qkv")
+        shares_qkv = [reduce_whole(keep_qkv[0], [d] * 4)]
+    d_up, d_gain_two, d_down = finished(shares, w_up, ln2_gain, 0, w_down.shape[0], "finished_mlp")
+    d_qkv, d_gain_one, d_out = finished(shares_qkv, w_qkv, ln1_gain, r, 0, "finished_attention")
     return (final, grad_states, grad_inject, d_gain_one, d_qkv, d_out, d_gain_two, d_up, d_down)
 
 def solution(mesh):

time: 82.3 us -> 79.3 us (0.964)
  waiting for transfers between devices: 14.8 us -> 12 us
  Pallas kernels: 37.3 us -> 36 us
  starting transfers between devices: 28.5 us -> 29.7 us
    ppermute x28, waiting for transfers between devices: 14.8 us -> 12 us  [exchange(): return lax.ppermute(x, axis, [(i, i ^ step) for i in range(size)])]
    pallas_call x7, Pallas kernels: 37.3 us -> 36 us  [call(): pl.pallas_call(run, out_shape=tuple((shapes[o[0]](o[1], o[2]) for o in ou...]
    ppermute x28, starting transfers between devices: 28.5 us -> 29.7 us  [exchange(): return lax.ppermute(x, axis, [(i, i ^ step) for i in range(size)])]
  transfers between devices with their start and end apart: 28 -> 28, of which waited for: 13 -> 15; matrix products, arithmetic and copies ran while one was open for 0% -> 0% of each run, Pallas kernels for 18% -> 20%
where the time goes in v4:
time: 79.3 us; the launch traced here: 79.1 us
  Pallas kernels  36 us (45%)
  starting transfers between devices  29.7 us (37%)
  waiting for transfers between devices  12 us (15%)
  between operations  0.99 us (1%)
    pallas_call x7, Pallas kernels, call(): pl.pallas_call(run, out_shape=tuple((shapes[o[0]](o[1], o[2]) for o in ou...  36 us
    ppermute x28, starting transfers between devices, exchange(): return lax.ppermute(x, axis, [(i, i ^ step) for i in range(size)])  29.7 us
    ppermute x28, waiting for transfers between devices, exchange(): return lax.ppermute(x, axis, [(i, i ^ step) for i in range(size)])  12 us
  transfers between devices with their start and end apart: 28, of which 15 were waited for; matrix products, arithmetic and copies ran while one was open for 0% of the time, Pallas kernels for 20%

profile of v4, /device:TPU:0, one launch (start us, length us, event | category | flops | bytes accessed | tf_op | source)
XLA Modules:
  0.0 79.1 jit_solution(4479052932632060433)
XLA Ops:
  0.6 1.1 %pack_weights.1 = (bf16[32,768]{1,0:T(8,128)(2,1)S(1)}, bf16[288,256]{1,0:T(8,128)(2,1)S(1)}) custom-call(bf16[32,768]{1,0:T(8,128)(2,1)} %refs_0_.6, bf16[1,32]{1,0:T(2,128)(2,1)} %bitcast.26, bf16[32,256]{1,0:T(8,128)(2,1)} %refs_2_.4, bf16[32,1024]{1,0:T(8,128)(2,1)} %refs_0_.7, bf16[128,256]{1,0:T(8,128)(2,1)} %refs_4_.2, bf16[1,32]{1,0:T(2,128)(2,1)} %bitcast.28), custom_call_target="tpu_custom_call" | custom-call | flops 1000000 | bytes 1048576 | tf_op jit(solution)/shard_map/pack_weights/pallas_call | solution.py:298
  1.7 5.1 %collective-permute-start.3 = (bf16[32,768]{1,0:T(8,128)(2,1)S(1)}, bf16[32,768]{1,0:T(8,128)(2,1)S(1)}, u32[]{:S(2)}, u32[]{:S(2)}) collective-permute-start(bf16[32,768]{1,0:T(8,128)(2,1)S(1)} %get-tuple-element.54.refs_8_), channel_id=1, source_target_pairs={{0,6},{1,7},{2,4},{3,5},{4,2},{5,3},{6,0},{7,1},{8,14},{9,15},{10,... | collective-permute-start | bytes 147464 | tf_op jit(solution)/shard_map/ppermute | solution.py:553
  7.5 3.7 %collective-permute-start.9 = (bf16[288,256]{1,0:T(8,128)(2,1)S(1)}, bf16[288,256]{1,0:T(8,128)(2,1)S(1)}, u32[]{:S(2)}, u32[]{:S(2)}) collective-permute-start(bf16[288,256]{1,0:T(8,128)(2,1)S(1)} %get-tuple-element.64.refs_7_), channel_id=1, source_target_pairs={{0,6},{1,7},{2,4},{3,5},{4,2},{5,3},{6,0},{7,1},{8,14},{9,15},{10,... | collective-permute-start | bytes 442376 | tf_op jit(solution)/shard_map/ppermute | solution.py:553
  11.3 0.6 collective-permute-start.7
  11.9 2.0 %prepare.1 = (bf16[1024,256]{1,0:T(8,128)(2,1)S(1)}, f32[1024,128]{1,0:T(8,128)S(1)}, f32[8,256,128]{2,1,0:T(8,128)S(1)}) custom-call(s32[1,16]{1,0:T(1,128)} %refs_1_.3, f32[1024,256]{1,0:T(8,128)} %refs_3_.3, f32[1024,256]{1,0:T(8,128)} %refs_4_.3), custom_call_target="tpu_custom_call" | custom-call | flops 1000000 | bytes 1048576 | tf_op jit(solution)/shard_map/prepare/pallas_call | solution.py:298
  13.9 3.4 %collective-permute-done.2.refs_12_ = bf16[32,768]{1,0:T(8,128)(2,1)S(1)} collective-permute-done((bf16[32,768]{1,0:T(8,128)(2,1)S(1)}, bf16[32,768]{1,0:T(8,128)(2,1)S(1)}, u32[]{:S(2)}, u32[]{:S(2)}) %collective-permute-start.2) | collective-permute-done | bytes 49184 | tf_op jit(solution)/shard_map/ppermute | solution.py:553
  17.8 0.7 collective-permute-done.refs_9_
  19.0 0.7 collective-permute-done.5.refs_13_
  19.9 4.8 %first_attention.1 = (bf16[8,4,256,256]{3,2,1,0:T(8,128)(2,1)S(1)}, bf16[1024,256]{1,0:T(8,128)(2,1)S(1)}, bf16[1152,256]{1,0:T(8,128)(2,1)S(1)}, bf16[9,256,128...) custom-call(s32[1]{0:T(128)} %bitcast.refs_0_, ...), custom_call_target="tpu_custom_call" | custom-call | flops 1000000 | bytes 1048576 | tf_op jit(solution)/shard_map/first_attention/pallas_call | solution.py:298
  27.1 18.3 %middle_part.1 = (f32[1024,256]{1,0:T(8,128)}, f32[1024,256]{1,0:T(8,128)S(1)}, f32[1024,256]{1,0:T(8,128)S(1)}, bf16[1024,256]{1,0:T(8,128)(2,1)S(1)}, bf16[256...) custom-call(s32[1]{0:T(128)} %bitcast.refs_0_, ...), custom_call_target="tpu_custom_call" | custom-call | flops 24999999488 | bytes 1048576 | tf_op jit(solution)/shard_map/middle_part/pallas_call | solution.py:298
  45.7 1.7 %collective-permute-done.14 = bf16[4,256,256]{2,1,0:T(8,128)(2,1)S(1)} collective-permute-done((bf16[4,256,256]{2,1,0:T(8,128)(2,1)S(1)}, bf16[4,256,256]{2,1,0:T(8,128)(2,1)S(1)}, u32[]{:S(2)}, u32[]{:S(2)}) %collective-permute-start.14) | collective-permute-done | bytes 524320 | tf_op jit(solution)/shard_map/ppermute | solution.py:553
  47.6 1.7 %collective-permute-start.16 = (bf16[256,256]{1,0:T(8,128)(2,1)S(1)}, bf16[256,256]{1,0:T(8,128)(2,1)S(1)}, u32[]{:S(2)}, u32[]{:S(2)}) collective-permute-start(bf16[256,256]{1,0:T(8,128)(2,1)S(1)} %get-tuple-element.95.refs_21_), channel_id=1, source_target_pairs={{0,6},{1,7},{2,4},{3,5},{4,2},{5,3},{6,0},{7,1},{8,14},{9,15},{10,... | collective-permute-start | bytes 393224 | tf_op jit(solution)/shard_map/ppermute | solution.py:553
  49.2 2.8 %collective-permute-start.18 = (bf16[256,256]{1,0:T(8,128)(2,1)S(1)}, bf16[256,256]{1,0:T(8,128)(2,1)S(1)}, u32[]{:S(2)}, u32[]{:S(2)}) collective-permute-start(bf16[256,256]{1,0:T(8,128)(2,1)S(1)} %get-tuple-element.97.refs_19_), channel_id=1, source_target_pairs={{0,2},{1,3},{2,0},{3,1},{4,6},{5,7},{6,4},{7,5},{8,10},{9,11},{10,... | collective-permute-start | bytes 393224 | tf_op jit(solution)/shard_map/ppermute | solution.py:553
  52.0 8.1 %last_part.1 = (bf16[4,128,256]{2,1,0:T(8,128)(2,1)S(1)}, bf16[4,128,256]{2,1,0:T(8,128)(2,1)S(1)}, f32[1024,256]{1,0:T(8,128)}, f32[1024,256]{1,0:T(8,128)}) custom-call(s32[1]{0:T(128)} %bitcast.refs_0_, bf16[1024,256]{1,0:T(8,128)(2,1)S(1)} %get-tuple-element.69.refs_1_, bf16[256,256]{1,0:T(8,128)(2,1)S(1)} %get-tuple-element.70.refs_2_, ...), custom_call_target="tpu_custom_call" | custom-call | flops 10000000000 | bytes 1048576 | tf_op jit(solution)/shard_map/last_part/pallas_call | solution.py:298
  60.8 1.0 %collective-permute-done.15 = bf16[4,128,256]{2,1,0:T(8,128)(2,1)S(1)} collective-permute-done((bf16[4,128,256]{2,1,0:T(8,128)(2,1)S(1)}, bf16[4,128,256]{2,1,0:T(8,128)(2,1)S(1)}, u32[]{:S(2)}, u32[]{:S(2)}) %collective-permute-start.15) | collective-permute-done | bytes 262176 | tf_op jit(solution)/shard_map/ppermute | solution.py:553
  61.9 1.7 %collective-permute-start.19 = (bf16[128,256]{1,0:T(8,128)(2,1)S(1)}, bf16[128,256]{1,0:T(8,128)(2,1)S(1)}, u32[]{:S(2)}, u32[]{:S(2)}) collective-permute-start(bf16[128,256]{1,0:T(8,128)(2,1)S(1)} %get-tuple-element.99), channel_id=1, source_target_pairs={{0,6},{1,7},{2,4},{3,5},{4,2},{5,3},{6,0},{7,1},{8,14},{9,15},{10,... | collective-permute-start | bytes 196616 | tf_op jit(solution)/shard_map/ppermute | solution.py:553
  63.6 2.8 %collective-permute-start.20 = (bf16[128,256]{1,0:T(8,128)(2,1)S(1)}, bf16[128,256]{1,0:T(8,128)(2,1)S(1)}, u32[]{:S(2)}, u32[]{:S(2)}) collective-permute-start(bf16[128,256]{1,0:T(8,128)(2,1)S(1)} %get-tuple-element.101), channel_id=1, source_target_pairs={{0,4},{1,5},{2,6},{3,7},{4,0},{5,1},{6,2},{7,3},{8,12},{9,13},{10,... | collective-permute-start | bytes 196616 | tf_op jit(solution)/shard_map/ppermute | solution.py:553
  66.3 2.5 %collective-permute-start.27 = (bf16[256,256]{1,0:T(8,128)(2,1)S(1)}, bf16[256,256]{1,0:T(8,128)(2,1)S(1)}, u32[]{:S(2)}, u32[]{:S(2)}) collective-permute-start(bf16[256,256]{1,0:T(8,128)(2,1)S(1)} %add_convert_fusion.2.refs_2_), channel_id=1, source_target_pairs={{0,24},{8,16},{16,8},{24,0},{1,25},{9,17},{17,9},{25,1},{2,26},{10... | collective-permute-start | bytes 393224 | tf_op jit(solution)/shard_map/ppermute | solution.py:553
  69.3 0.9 %collective-permute-start.25 = (bf16[256,256]{1,0:T(8,128)(2,1)S(1)}, bf16[256,256]{1,0:T(8,128)(2,1)S(1)}, u32[]{:S(2)}, u32[]{:S(2)}) collective-permute-start(bf16[256,256]{1,0:T(8,128)(2,1)S(1)} %add_convert_fusion.2.refs_2_), channel_id=1, source_target_pairs={{0,8},{8,0},{16,24},{24,16},{1,9},{9,1},{17,25},{25,17},{2,10},{10... | collective-permute-start | bytes 393224 | tf_op jit(solution)/shard_map/ppermute | solution.py:553
  70.8 2.5 %collective-permute-start.24 = (bf16[128,256]{1,0:T(8,128)(2,1)S(1)}, bf16[128,256]{1,0:T(8,128)(2,1)S(1)}, u32[]{:S(2)}, u32[]{:S(2)}) collective-permute-start(bf16[128,256]{1,0:T(8,128)(2,1)S(1)} %fusion.2.refs_2_), channel_id=1, source_target_pairs={{0,24},{8,16},{16,8},{24,0},{1,25},{9,17},{17,9},{25,1},{2,26},{10... | collective-permute-start | bytes 196616 | tf_op jit(solution)/shard_map/ppermute | solution.py:553
  73.8 1.3 %collective-permute-start.22 = (bf16[128,256]{1,0:T(8,128)(2,1)S(1)}, bf16[128,256]{1,0:T(8,128)(2,1)S(1)}, u32[]{:S(2)}, u32[]{:S(2)}) collective-permute-start(bf16[128,256]{1,0:T(8,128)(2,1)S(1)} %fusion.2.refs_2_), channel_id=1, source_target_pairs={{0,8},{8,0},{16,24},{24,16},{1,9},{9,1},{17,25},{25,17},{2,10},{10... | collective-permute-start | bytes 196616 | tf_op jit(solution)/shard_map/ppermute | solution.py:553
  75.1 1.3 %collective-permute-done.26.refs_4_ = bf16[256,256]{1,0:T(8,128)(2,1)S(1)} collective-permute-done((bf16[256,256]{1,0:T(8,128)(2,1)S(1)}, bf16[256,256]{1,0:T(8,128)(2,1)S(1)}, u32[]{:S(2)}, u32[]{:S(2)}) %collective-permute-start.26) | collective-permute-done | bytes 131104 | tf_op jit(solution)/shard_map/ppermute | solution.py:553
  76.4 0.9 %finished_mlp.1 = (f32[32,1024]{1,0:T(8,128)}, f32[1,32]{1,0:T(1,128)}, f32[128,256]{1,0:T(8,128)}) custom-call(bf16[32,1024]{1,0:T(8,128)(2,1)S(1)} %copy-done, bf16[1,32]{1,0:T(2,128)(2,1)S(1)} %bitcast.29, bf16[256,256]{1,0:T(8,128)(2,1)S(1)} %add_convert_fusion.2.refs_2_, bf16[256,256]{1,0:T(8,128)(2,1)S(1)} %collective-permute-done.25.refs_3_, ...), custom_call_target="tpu_custom_call" | custom-call | flops 1000000 | bytes 1048576 | tf_op jit(solution)/shard_map/finished_mlp/pallas_call | solution.py:298
  78.1 0.8 %finished_attention.1 = (f32[32,768]{1,0:T(8,128)}, f32[1,32]{1,0:T(1,128)}, f32[32,256]{1,0:T(8,128)}) custom-call(bf16[32,768]{1,0:T(8,128)(2,1)S(1)} %copy-done.1, bf16[1,32]{1,0:T(2,128)(2,1)S(1)} %bitcast.27, bf16[128,256]{1,0:T(8,128)(2,1)S(1)} %fusion.2.refs_2_, bf16[128,256]{1,0:T(8,128)(2,1)S(1)} %collective-permute-done.22.refs_3_, ...), custom_call_target="tpu_custom_call" | custom-call | flops 1000000 | bytes 1048576 | tf_op jit(solution)/shard_map/finished_attention/pallas_call | solution.py:298
  (54 shorter events, 7.7 us)
Async XLA Ops:
  1.7 9.5 %collective-permute-start.3 = (bf16[32,768]{1,0:T(8,128)(2,1)S(1)}, bf16[32,768]{1,0:T(8,128)(2,1)S(1)}, u32[]{:S(2)}, u32[]{:S(2)}) collective-permute-start(bf16[32,768]{1,0:T(8,128)(2,1)S(1)} %get-tuple-element.54.refs_8_), channel_id=1, source_target_pairs={{0,6},{1,7},{2,4},{3,5},{4,2},{5,3},{6,0},{7,1},{8,14},{9,15},{10,... | collective-permute-start | bytes 147464 | tf_op jit(solution)/shard_map/ppermute | solution.py:553
  6.9 10.4 %collective-permute-start.2 = (bf16[32,768]{1,0:T(8,128)(2,1)S(1)}, bf16[32,768]{1,0:T(8,128)(2,1)S(1)}, u32[]{:S(2)}, u32[]{:S(2)}) collective-permute-start(bf16[32,768]{1,0:T(8,128)(2,1)S(1)} %get-tuple-element.54.refs_8_), channel_id=1, source_target_pairs={{0,4},{1,5},{2,6},{3,7},{4,0},{5,1},{6,2},{7,3},{8,12},{9,13},{10,... | collective-permute-start | bytes 147464 | tf_op jit(solution)/shard_map/ppermute | solution.py:553
  6.9 10.4 %collective-permute-start.1 = (bf16[32,768]{1,0:T(8,128)(2,1)S(1)}, bf16[32,768]{1,0:T(8,128)(2,1)S(1)}, u32[]{:S(2)}, u32[]{:S(2)}) collective-permute-start(bf16[32,768]{1,0:T(8,128)(2,1)S(1)} %get-tuple-element.54.refs_8_), channel_id=1, source_target_pairs={{0,2},{1,3},{2,0},{3,1},{4,6},{5,7},{6,4},{7,5},{8,10},{9,11},{10,... | collective-permute-start | bytes 147464 | tf_op jit(solution)/shard_map/ppermute | solution.py:553
  7.5 17.2 %collective-permute-start.9 = (bf16[288,256]{1,0:T(8,128)(2,1)S(1)}, bf16[288,256]{1,0:T(8,128)(2,1)S(1)}, u32[]{:S(2)}, u32[]{:S(2)}) collective-permute-start(bf16[288,256]{1,0:T(8,128)(2,1)S(1)} %get-tuple-element.64.refs_7_), channel_id=1, source_target_pairs={{0,6},{1,7},{2,4},{3,5},{4,2},{5,3},{6,0},{7,1},{8,14},{9,15},{10,... | collective-permute-start | bytes 442376 | tf_op jit(solution)/shard_map/ppermute | solution.py:553
  11.2 13.5 %collective-permute-start.8 = (bf16[288,256]{1,0:T(8,128)(2,1)S(1)}, bf16[288,256]{1,0:T(8,128)(2,1)S(1)}, u32[]{:S(2)}, u32[]{:S(2)}) collective-permute-start(bf16[288,256]{1,0:T(8,128)(2,1)S(1)} %get-tuple-element.64.refs_7_), channel_id=1, source_target_pairs={{0,4},{1,5},{2,6},{3,7},{4,0},{5,1},{6,2},{7,3},{8,12},{9,13},{10,... | collective-permute-start | bytes 442376 | tf_op jit(solution)/shard_map/ppermute | solution.py:553
  11.3 13.5 %collective-permute-start.7 = (bf16[288,256]{1,0:T(8,128)(2,1)S(1)}, bf16[288,256]{1,0:T(8,128)(2,1)S(1)}, u32[]{:S(2)}, u32[]{:S(2)}) collective-permute-start(bf16[288,256]{1,0:T(8,128)(2,1)S(1)} %get-tuple-element.64.refs_7_), channel_id=1, source_target_pairs={{0,2},{1,3},{2,0},{3,1},{4,6},{5,7},{6,4},{7,5},{8,10},{9,11},{10,... | collective-permute-start | bytes 442376 | tf_op jit(solution)/shard_map/ppermute | solution.py:553
  17.3 1.4 %collective-permute-start.4 = (bf16[32,768]{1,0:T(8,128)(2,1)S(1)}, bf16[32,768]{1,0:T(8,128)(2,1)S(1)}, u32[]{:S(2)}, u32[]{:S(2)}) collective-permute-start(bf16[32,768]{1,0:T(8,128)(2,1)S(1)} %collective-permute-done.1.refs_10_), channel_id=1, source_target_pairs={{0,1},{1,0},{2,3},{3,2},{4,5},{5,4},{6,7},{7,6},{8,9},{9,8},{10,11... | collective-permute-start | bytes 147464 | tf_op jit(solution)/shard_map/ppermute | solution.py:553
  24.8 1.4 %collective-permute-start.10 = (bf16[288,256]{1,0:T(8,128)(2,1)S(1)}, bf16[288,256]{1,0:T(8,128)(2,1)S(1)}, u32[]{:S(2)}, u32[]{:S(2)}) collective-permute-start(bf16[288,256]{1,0:T(8,128)(2,1)S(1)} %get-tuple-element.64.refs_7_), channel_id=1, source_target_pairs={{0,1},{1,0},{2,3},{3,2},{4,5},{5,4},{6,7},{7,6},{8,9},{9,8},{10,11... | collective-permute-start | bytes 442376 | tf_op jit(solution)/shard_map/ppermute | solution.py:553
  25.2 1.4 %collective-permute-start.11 = (bf16[288,256]{1,0:T(8,128)(2,1)S(1)}, bf16[288,256]{1,0:T(8,128)(2,1)S(1)}, u32[]{:S(2)}, u32[]{:S(2)}) collective-permute-start(bf16[288,256]{1,0:T(8,128)(2,1)S(1)} %collective-permute-done.7.refs_9_), channel_id=1, source_target_pairs={{0,1},{1,0},{2,3},{3,2},{4,5},{5,4},{6,7},{7,6},{8,9},{9,8},{10,11... | collective-permute-start | bytes 442376 | tf_op jit(solution)/shard_map/ppermute | solution.py:553
  25.4 1.4 %collective-permute-start.12 = (bf16[288,256]{1,0:T(8,128)(2,1)S(1)}, bf16[288,256]{1,0:T(8,128)(2,1)S(1)}, u32[]{:S(2)}, u32[]{:S(2)}) collective-permute-start(bf16[288,256]{1,0:T(8,128)(2,1)S(1)} %collective-permute-done.8.refs_11_), channel_id=1, source_target_pairs={{0,1},{1,0},{2,3},{3,2},{4,5},{5,4},{6,7},{7,6},{8,9},{9,8},{10,11... | collective-permute-start | bytes 442376 | tf_op jit(solution)/shard_map/ppermute | solution.py:553
  45.4 2.0 %collective-permute-start.14 = (bf16[4,256,256]{2,1,0:T(8,128)(2,1)S(1)}, bf16[4,256,256]{2,1,0:T(8,128)(2,1)S(1)}, u32[]{:S(2)}, u32[]{:S(2)}) collective-permute-start(bf16[4,256,256]{2,1,0:T(8,128)(2,1)S(1)} %get-tuple-element.84), channel_id=1, source_target_pairs={{0,1},{1,0},{2,3},{3,2},{4,5},{5,4},{6,7},{7,6},{8,9},{9,8},{10,11... | collective-permute-start | bytes 1572872 | tf_op jit(solution)/shard_map/ppermute | solution.py:553
  47.6 12.7 %collective-permute-start.16 = (bf16[256,256]{1,0:T(8,128)(2,1)S(1)}, bf16[256,256]{1,0:T(8,128)(2,1)S(1)}, u32[]{:S(2)}, u32[]{:S(2)}) collective-permute-start(bf16[256,256]{1,0:T(8,128)(2,1)S(1)} %get-tuple-element.95.refs_21_), channel_id=1, source_target_pairs={{0,6},{1,7},{2,4},{3,5},{4,2},{5,3},{6,0},{7,1},{8,14},{9,15},{10,... | collective-permute-start | bytes 393224 | tf_op jit(solution)/shard_map/ppermute | solution.py:553
  49.2 11.5 %collective-permute-start.17 = (bf16[256,256]{1,0:T(8,128)(2,1)S(1)}, bf16[256,256]{1,0:T(8,128)(2,1)S(1)}, u32[]{:S(2)}, u32[]{:S(2)}) collective-permute-start(bf16[256,256]{1,0:T(8,128)(2,1)S(1)} %get-tuple-element.96.refs_20_), channel_id=1, source_target_pairs={{0,4},{1,5},{2,6},{3,7},{4,0},{5,1},{6,2},{7,3},{8,12},{9,13},{10,... | collective-permute-start | bytes 393224 | tf_op jit(solution)/shard_map/ppermute | solution.py:553
  49.2 11.5 %collective-permute-start.18 = (bf16[256,256]{1,0:T(8,128)(2,1)S(1)}, bf16[256,256]{1,0:T(8,128)(2,1)S(1)}, u32[]{:S(2)}, u32[]{:S(2)}) collective-permute-start(bf16[256,256]{1,0:T(8,128)(2,1)S(1)} %get-tuple-element.97.refs_19_), channel_id=1, source_target_pairs={{0,2},{1,3},{2,0},{3,1},{4,6},{5,7},{6,4},{7,5},{8,10},{9,11},{10,... | collective-permute-start | bytes 393224 | tf_op jit(solution)/shard_map/ppermute | solution.py:553
  60.2 1.6 %collective-permute-start.15 = (bf16[4,128,256]{2,1,0:T(8,128)(2,1)S(1)}, bf16[4,128,256]{2,1,0:T(8,128)(2,1)S(1)}, u32[]{:S(2)}, u32[]{:S(2)}) collective-permute-start(bf16[4,128,256]{2,1,0:T(8,128)(2,1)S(1)} %get-tuple-element.88), channel_id=1, source_target_pairs={{0,1},{1,0},{2,3},{3,2},{4,5},{5,4},{6,7},{7,6},{8,9},{9,8},{10,11... | collective-permute-start | bytes 786440 | tf_op jit(solution)/shard_map/ppermute | solution.py:553
  61.9 7.4 %collective-permute-start.19 = (bf16[128,256]{1,0:T(8,128)(2,1)S(1)}, bf16[128,256]{1,0:T(8,128)(2,1)S(1)}, u32[]{:S(2)}, u32[]{:S(2)}) collective-permute-start(bf16[128,256]{1,0:T(8,128)(2,1)S(1)} %get-tuple-element.99), channel_id=1, source_target_pairs={{0,6},{1,7},{2,4},{3,5},{4,2},{5,3},{6,0},{7,1},{8,14},{9,15},{10,... | collective-permute-start | bytes 196616 | tf_op jit(solution)/shard_map/ppermute | solution.py:553
  63.6 6.6 %collective-permute-start.21 = (bf16[128,256]{1,0:T(8,128)(2,1)S(1)}, bf16[128,256]{1,0:T(8,128)(2,1)S(1)}, u32[]{:S(2)}, u32[]{:S(2)}) collective-permute-start(bf16[128,256]{1,0:T(8,128)(2,1)S(1)} %get-tuple-element.100), channel_id=1, source_target_pairs={{0,2},{1,3},{2,0},{3,1},{4,6},{5,7},{6,4},{7,5},{8,10},{9,11},{10,... | collective-permute-start | bytes 196616 | tf_op jit(solution)/shard_map/ppermute | solution.py:553
  63.6 7.2 %collective-permute-start.20 = (bf16[128,256]{1,0:T(8,128)(2,1)S(1)}, bf16[128,256]{1,0:T(8,128)(2,1)S(1)}, u32[]{:S(2)}, u32[]{:S(2)}) collective-permute-start(bf16[128,256]{1,0:T(8,128)(2,1)S(1)} %get-tuple-element.101), channel_id=1, source_target_pairs={{0,4},{1,5},{2,6},{3,7},{4,0},{5,1},{6,2},{7,3},{8,12},{9,13},{10,... | collective-permute-start | bytes 196616 | tf_op jit(solution)/shard_map/ppermute | solution.py:553
  66.3 7.5 %collective-permute-start.27 = (bf16[256,256]{1,0:T(8,128)(2,1)S(1)}, bf16[256,256]{1,0:T(8,128)(2,1)S(1)}, u32[]{:S(2)}, u32[]{:S(2)}) collective-permute-start(bf16[256,256]{1,0:T(8,128)(2,1)S(1)} %add_convert_fusion.2.refs_2_), channel_id=1, source_target_pairs={{0,24},{8,16},{16,8},{24,0},{1,25},{9,17},{17,9},{25,1},{2,26},{10... | collective-permute-start | bytes 393224 | tf_op jit(solution)/shard_map/ppermute | solution.py:553
  68.8 7.6 %collective-permute-start.26 = (bf16[256,256]{1,0:T(8,128)(2,1)S(1)}, bf16[256,256]{1,0:T(8,128)(2,1)S(1)}, u32[]{:S(2)}, u32[]{:S(2)}) collective-permute-start(bf16[256,256]{1,0:T(8,128)(2,1)S(1)} %add_convert_fusion.2.refs_2_), channel_id=1, source_target_pairs={{0,16},{8,24},{16,0},{24,8},{1,17},{9,25},{17,1},{25,9},{2,18},{10... | collective-permute-start | bytes 393224 | tf_op jit(solution)/shard_map/ppermute | solution.py:553
  69.3 7.1 %collective-permute-start.25 = (bf16[256,256]{1,0:T(8,128)(2,1)S(1)}, bf16[256,256]{1,0:T(8,128)(2,1)S(1)}, u32[]{:S(2)}, u32[]{:S(2)}) collective-permute-start(bf16[256,256]{1,0:T(8,128)(2,1)S(1)} %add_convert_fusion.2.refs_2_), channel_id=1, source_target_pairs={{0,8},{8,0},{16,24},{24,16},{1,9},{9,1},{17,25},{25,17},{2,10},{10... | collective-permute-start | bytes 393224 | tf_op jit(solution)/shard_map/ppermute | solution.py:553
  70.8 6.5 %collective-permute-start.24 = (bf16[128,256]{1,0:T(8,128)(2,1)S(1)}, bf16[128,256]{1,0:T(8,128)(2,1)S(1)}, u32[]{:S(2)}, u32[]{:S(2)}) collective-permute-start(bf16[128,256]{1,0:T(8,128)(2,1)S(1)} %fusion.2.refs_2_), channel_id=1, source_target_pairs={{0,24},{8,16},{16,8},{24,0},{1,25},{9,17},{17,9},{25,1},{2,26},{10... | collective-permute-start | bytes 196616 | tf_op jit(solution)/shard_map/ppermute | solution.py:553
  73.3 4.5 %collective-permute-start.23 = (bf16[128,256]{1,0:T(8,128)(2,1)S(1)}, bf16[128,256]{1,0:T(8,128)(2,1)S(1)}, u32[]{:S(2)}, u32[]{:S(2)}) collective-permute-start(bf16[128,256]{1,0:T(8,128)(2,1)S(1)} %fusion.2.refs_2_), channel_id=1, source_target_pairs={{0,16},{8,24},{16,0},{24,8},{1,17},{9,25},{17,1},{25,9},{2,18},{10... | collective-permute-start | bytes 196616 | tf_op jit(solution)/shard_map/ppermute | solution.py:553
  73.8 4.3 %collective-permute-start.22 = (bf16[128,256]{1,0:T(8,128)(2,1)S(1)}, bf16[128,256]{1,0:T(8,128)(2,1)S(1)}, u32[]{:S(2)}, u32[]{:S(2)}) collective-permute-start(bf16[128,256]{1,0:T(8,128)(2,1)S(1)} %fusion.2.refs_2_), channel_id=1, source_target_pairs={{0,8},{8,0},{16,24},{24,16},{1,9},{9,1},{17,25},{25,17},{2,10},{10... | collective-permute-start | bytes 196616 | tf_op jit(solution)/shard_map/ppermute | solution.py:553
  (8 other events, 106.0 us)

commit v5 on v4

--- a/solution.py
+++ b/solution.py
@@ -22,7 +22,7 @@
 FLOPS_FIRST = 10 ** 6
 FLOPS_PREPARE = 10 ** 6
 FLOPS_LAST = 10 ** 10
-LIMIT_MIDDLE = 40
+LIMIT_MIDDLE = 42
 LIMIT_LAST = 16
 
 
@@ -172,8 +172,7 @@
         act = h * sg
         s.act[at, c] = act
         s.gp[at, c] = sg + act * (2.0 - 2.0 * sg) * (3 * GELU_B * h2 + GELU_A)
-        acc = acc + dot(act, wdown[c, :])
-    return acc
+    return mid + dot(s.act[at, :], wdown[...])
 
 def mlp_back(s, j, g, wdown_t, wup_t):
     at = rows(j * CHUNK, CHUNK)
@@ -184,8 +183,7 @@
         c = slice(f * 256, (f + 1) * 256)
         dh = dot(gb, wdown_t[:, c]).astype(BF) * s.gp[at, c]
         s.gp[at, c] = dh
-        part = dot(dh, wup_t[c, :])
-        acc = part if acc is None else acc + part
+    acc = dot(s.gp[at, :], wup_t[...])
     g = g + ln_bwd(acc, s.n2[at, :].astype(F32), s.r2[at, 0:1])
     s.gm[at, :] = g.astype(BF)
     return g
@@ -392,10 +390,7 @@
         its[0].ht, its[0].gm = ht_ref, gm
         its[1].n1, its[1].dpk, its[1].ht, its[1].gm = n1, dpk, ht, gm_two
         place_rest(me_ref[0], m.ins[7:], wout, x.wup, x.wdown)
-        x.wup_t[...] = x.wup[...].T
-        x.wdown_t[...] = x.wdown[...].T
         pad_zero(its[1])
-        x.wqkv_t[...] = wqkv_ref[...].T
         def rows_of(j):
             return slice(j * CHUNK, (j + 1) * CHUNK)
         def mlp_of(n, j, src, dst):
@@ -427,7 +422,12 @@
         for j in range(nc): mlp_of(0, j, ent_ref, x.state)
         for j in range(nc): project_of(j)
         for j in range(nc): attend_of(j)
-        for j in range(nc): mlp_of(1, j, x.state, final)
+        for j in range(nc):
+            mlp_of(1, j, x.state, final)
+            if j == 0:
+                x.wup_t[...] = x.wup[...].T
+                x.wdown_t[...] = x.wdown[...].T
+                x.wqkv_t[...] = wqkv_ref[...].T
         m.put(0)
         for j in range(nc): back_two(j)
         for j in range(nc): attend_back_of(j)
@@ -606,7 +606,7 @@
     saved, wqkv, entering = first_attention(me, prompt_lengths, loop_counts, states, inject, cotangent, n1, mask, qkv_parts, ff)
     saved.update(n1=n1, r1=r1)
     if direct:
-        rest_parts = with_near(after(rest_far, wqkv), n_fsdp)
+        rest_parts = with_near(rest_far[:1], n_fsdp) + with_near(after(rest_far[1:], wqkv), n_fsdp)
     final, g, ginj, gm, wout, n1, dpk, ht, gm_two, keep, send = middle_part(
         me, *entering, mask, wqkv, saved["ht"], rest_parts, ff)
     summed = []

time: 79.3 us -> 78.6 us (level)
  transfers between devices with their start and end apart: 28 -> 28, of which waited for: 15 -> 14; matrix products, arithmetic and copies ran while one was open for 0% -> 0% of each run, Pallas kernels for 20% -> 20%
where the time goes in v5:
time: 78.6 us; the launch traced here: 78.4 us
  Pallas kernels  35.6 us (45%)
  starting transfers between devices  29.8 us (38%)
  waiting for transfers between devices  11.5 us (15%)
  between operations  0.99 us (1%)
    pallas_call x7, Pallas kernels, call(): pl.pallas_call(run, out_shape=tuple((shapes[o[0]](o[1], o[2]) for o in ou...  35.6 us
    ppermute x28, starting transfers between devices, exchange(): return lax.ppermute(x, axis, [(i, i ^ step) for i in range(size)])  29.8 us
    ppermute x28, waiting for transfers between devices, exchange(): return lax.ppermute(x, axis, [(i, i ^ step) for i in range(size)])  11.5 us
  transfers between devices with their start and end apart: 28, of which 14 were waited for; matrix products, arithmetic and copies ran while one was open for 0% of the time, Pallas kernels for 20%

profile of v5, /device:TPU:0, one launch (start us, length us, event | category | flops | bytes accessed | tf_op | source)
XLA Modules:
  0.0 78.4 jit_solution(5144800813833351143)
XLA Ops:
  0.6 1.1 %pack_weights.1 = (bf16[32,768]{1,0:T(8,128)(2,1)S(1)}, bf16[288,256]{1,0:T(8,128)(2,1)S(1)}) custom-call(bf16[32,768]{1,0:T(8,128)(2,1)} %refs_0_.6, bf16[1,32]{1,0:T(2,128)(2,1)} %bitcast.26, bf16[32,256]{1,0:T(8,128)(2,1)} %refs_2_.4, bf16[32,1024]{1,0:T(8,128)(2,1)} %refs_0_.7, bf16[128,256]{1,0:T(8,128)(2,1)} %refs_4_.2, bf16[1,32]{1,0:T(2,128)(2,1)} %bitcast.28), custom_call_target="tpu_custom_call" | custom-call | flops 1000000 | bytes 1048576 | tf_op jit(solution)/shard_map/pack_weights/pallas_call | solution.py:296
  1.7 5.1 %collective-permute-start.3 = (bf16[32,768]{1,0:T(8,128)(2,1)S(1)}, bf16[32,768]{1,0:T(8,128)(2,1)S(1)}, u32[]{:S(2)}, u32[]{:S(2)}) collective-permute-start(bf16[32,768]{1,0:T(8,128)(2,1)S(1)} %get-tuple-element.53.refs_8_), channel_id=1, source_target_pairs={{0,6},{1,7},{2,4},{3,5},{4,2},{5,3},{6,0},{7,1},{8,14},{9,15},{10,... | collective-permute-start | bytes 147464 | tf_op jit(solution)/shard_map/ppermute | solution.py:553
  7.5 3.7 %collective-permute-start.10 = (bf16[288,256]{1,0:T(8,128)(2,1)S(1)}, bf16[288,256]{1,0:T(8,128)(2,1)S(1)}, u32[]{:S(2)}, u32[]{:S(2)}) collective-permute-start(bf16[288,256]{1,0:T(8,128)(2,1)S(1)} %get-tuple-element.62.refs_7_), channel_id=1, source_target_pairs={{0,6},{1,7},{2,4},{3,5},{4,2},{5,3},{6,0},{7,1},{8,14},{9,15},{10,... | collective-permute-start | bytes 442376 | tf_op jit(solution)/shard_map/ppermute | solution.py:553
  11.9 2.0 %prepare.1 = (bf16[1024,256]{1,0:T(8,128)(2,1)S(1)}, f32[1024,128]{1,0:T(8,128)S(1)}, f32[8,256,128]{2,1,0:T(8,128)S(1)}) custom-call(s32[1,16]{1,0:T(1,128)} %refs_1_.3, f32[1024,256]{1,0:T(8,128)} %refs_3_.3, f32[1024,256]{1,0:T(8,128)} %refs_4_.3), custom_call_target="tpu_custom_call" | custom-call | flops 1000000 | bytes 1048576 | tf_op jit(solution)/shard_map/prepare/pallas_call | solution.py:296
  13.9 3.4 %collective-permute-done.2.refs_12_ = bf16[32,768]{1,0:T(8,128)(2,1)S(1)} collective-permute-done((bf16[32,768]{1,0:T(8,128)(2,1)S(1)}, bf16[32,768]{1,0:T(8,128)(2,1)S(1)}, u32[]{:S(2)}, u32[]{:S(2)}) %collective-permute-start.2) | collective-permute-done | bytes 49184 | tf_op jit(solution)/shard_map/ppermute | solution.py:553
  17.8 0.7 collective-permute-done.refs_9_
  19.0 0.7 collective-permute-done.5.refs_13_
  19.9 4.8 %first_attention.1 = (bf16[8,4,256,256]{3,2,1,0:T(8,128)(2,1)S(1)}, bf16[1024,256]{1,0:T(8,128)(2,1)S(1)}, bf16[1152,256]{1,0:T(8,128)(2,1)S(1)}, bf16[9,256,128...) custom-call(s32[1]{0:T(128)} %bitcast.refs_0_, ...), custom_call_target="tpu_custom_call" | custom-call | flops 1000000 | bytes 1048576 | tf_op jit(solution)/shard_map/first_attention/pallas_call | solution.py:296
  26.8 18.1 %middle_part.1 = (f32[1024,256]{1,0:T(8,128)}, f32[1024,256]{1,0:T(8,128)S(1)}, f32[1024,256]{1,0:T(8,128)S(1)}, bf16[1024,256]{1,0:T(8,128)(2,1)S(1)}, bf16[256...) custom-call(s32[1]{0:T(128)} %bitcast.refs_0_, ...), custom_call_target="tpu_custom_call" | custom-call | flops 24999999488 | bytes 1048576 | tf_op jit(solution)/shard_map/middle_part/pallas_call | solution.py:296
  45.2 1.6 %collective-permute-done.14 = bf16[4,256,256]{2,1,0:T(8,128)(2,1)S(1)} collective-permute-done((bf16[4,256,256]{2,1,0:T(8,128)(2,1)S(1)}, bf16[4,256,256]{2,1,0:T(8,128)(2,1)S(1)}, u32[]{:S(2)}, u32[]{:S(2)}) %collective-permute-start.14) | collective-permute-done | bytes 524320 | tf_op jit(solution)/shard_map/ppermute | solution.py:553
  47.0 1.8 %collective-permute-start.16 = (bf16[256,256]{1,0:T(8,128)(2,1)S(1)}, bf16[256,256]{1,0:T(8,128)(2,1)S(1)}, u32[]{:S(2)}, u32[]{:S(2)}) collective-permute-start(bf16[256,256]{1,0:T(8,128)(2,1)S(1)} %get-tuple-element.93.refs_21_), channel_id=1, source_target_pairs={{0,6},{1,7},{2,4},{3,5},{4,2},{5,3},{6,0},{7,1},{8,14},{9,15},{10,... | collective-permute-start | bytes 393224 | tf_op jit(solution)/shard_map/ppermute | solution.py:553
  48.8 2.6 %collective-permute-start.18 = (bf16[256,256]{1,0:T(8,128)(2,1)S(1)}, bf16[256,256]{1,0:T(8,128)(2,1)S(1)}, u32[]{:S(2)}, u32[]{:S(2)}) collective-permute-start(bf16[256,256]{1,0:T(8,128)(2,1)S(1)} %get-tuple-element.95.refs_19_), channel_id=1, source_target_pairs={{0,2},{1,3},{2,0},{3,1},{4,6},{5,7},{6,4},{7,5},{8,10},{9,11},{10,... | collective-permute-start | bytes 393224 | tf_op jit(solution)/shard_map/ppermute | solution.py:553
  51.5 8.0 %last_part.1 = (bf16[4,128,256]{2,1,0:T(8,128)(2,1)S(1)}, bf16[4,128,256]{2,1,0:T(8,128)(2,1)S(1)}, f32[1024,256]{1,0:T(8,128)}, f32[1024,256]{1,0:T(8,128)}) custom-call(s32[1]{0:T(128)} %bitcast.refs_0_, bf16[1024,256]{1,0:T(8,128)(2,1)S(1)} %get-tuple-element.67.refs_1_, bf16[256,256]{1,0:T(8,128)(2,1)S(1)} %get-tuple-element.68.refs_2_, ...), custom_call_target="tpu_custom_call" | custom-call | flops 10000000000 | bytes 1048576 | tf_op jit(solution)/shard_map/last_part/pallas_call | solution.py:296
  59.5 0.7 collective-permute-done.17
  60.3 0.7 collective-permute-done.15
  61.2 1.8 %collective-permute-start.19 = (bf16[128,256]{1,0:T(8,128)(2,1)S(1)}, bf16[128,256]{1,0:T(8,128)(2,1)S(1)}, u32[]{:S(2)}, u32[]{:S(2)}) collective-permute-start(bf16[128,256]{1,0:T(8,128)(2,1)S(1)} %get-tuple-element.97), channel_id=1, source_target_pairs={{0,6},{1,7},{2,4},{3,5},{4,2},{5,3},{6,0},{7,1},{8,14},{9,15},{10,... | collective-permute-start | bytes 196616 | tf_op jit(solution)/shard_map/ppermute | solution.py:553
  63.0 2.6 %collective-permute-start.20 = (bf16[128,256]{1,0:T(8,128)(2,1)S(1)}, bf16[128,256]{1,0:T(8,128)(2,1)S(1)}, u32[]{:S(2)}, u32[]{:S(2)}) collective-permute-start(bf16[128,256]{1,0:T(8,128)(2,1)S(1)} %get-tuple-element.99), channel_id=1, source_target_pairs={{0,4},{1,5},{2,6},{3,7},{4,0},{5,1},{6,2},{7,3},{8,12},{9,13},{10,... | collective-permute-start | bytes 196616 | tf_op jit(solution)/shard_map/ppermute | solution.py:553
  65.6 2.5 %collective-permute-start.27 = (bf16[256,256]{1,0:T(8,128)(2,1)S(1)}, bf16[256,256]{1,0:T(8,128)(2,1)S(1)}, u32[]{:S(2)}, u32[]{:S(2)}) collective-permute-start(bf16[256,256]{1,0:T(8,128)(2,1)S(1)} %add_convert_fusion.2.refs_2_), channel_id=1, source_target_pairs={{0,24},{8,16},{16,8},{24,0},{1,25},{9,17},{17,9},{25,1},{2,26},{10... | collective-permute-start | bytes 393224 | tf_op jit(solution)/shard_map/ppermute | solution.py:553
  68.6 0.9 %collective-permute-start.25 = (bf16[256,256]{1,0:T(8,128)(2,1)S(1)}, bf16[256,256]{1,0:T(8,128)(2,1)S(1)}, u32[]{:S(2)}, u32[]{:S(2)}) collective-permute-start(bf16[256,256]{1,0:T(8,128)(2,1)S(1)} %add_convert_fusion.2.refs_2_), channel_id=1, source_target_pairs={{0,8},{8,0},{16,24},{24,16},{1,9},{9,1},{17,25},{25,17},{2,10},{10... | collective-permute-start | bytes 393224 | tf_op jit(solution)/shard_map/ppermute | solution.py:553
  70.0 2.6 %collective-permute-start.24 = (bf16[128,256]{1,0:T(8,128)(2,1)S(1)}, bf16[128,256]{1,0:T(8,128)(2,1)S(1)}, u32[]{:S(2)}, u32[]{:S(2)}) collective-permute-start(bf16[128,256]{1,0:T(8,128)(2,1)S(1)} %fusion.2.refs_2_), channel_id=1, source_target_pairs={{0,24},{8,16},{16,8},{24,0},{1,25},{9,17},{17,9},{25,1},{2,26},{10... | collective-permute-start | bytes 196616 | tf_op jit(solution)/shard_map/ppermute | solution.py:553
  73.1 1.3 %collective-permute-start.22 = (bf16[128,256]{1,0:T(8,128)(2,1)S(1)}, bf16[128,256]{1,0:T(8,128)(2,1)S(1)}, u32[]{:S(2)}, u32[]{:S(2)}) collective-permute-start(bf16[128,256]{1,0:T(8,128)(2,1)S(1)} %fusion.2.refs_2_), channel_id=1, source_target_pairs={{0,8},{8,0},{16,24},{24,16},{1,9},{9,1},{17,25},{25,17},{2,10},{10... | collective-permute-start | bytes 196616 | tf_op jit(solution)/shard_map/ppermute | solution.py:553
  74.4 1.4 %collective-permute-done.26.refs_4_ = bf16[256,256]{1,0:T(8,128)(2,1)S(1)} collective-permute-done((bf16[256,256]{1,0:T(8,128)(2,1)S(1)}, bf16[256,256]{1,0:T(8,128)(2,1)S(1)}, u32[]{:S(2)}, u32[]{:S(2)}) %collective-permute-start.26) | collective-permute-done | bytes 131104 | tf_op jit(solution)/shard_map/ppermute | solution.py:553
  75.9 0.9 %finished_mlp.1 = (f32[32,1024]{1,0:T(8,128)}, f32[1,32]{1,0:T(1,128)}, f32[128,256]{1,0:T(8,128)}) custom-call(bf16[32,1024]{1,0:T(8,128)(2,1)S(1)} %copy-done, bf16[1,32]{1,0:T(2,128)(2,1)S(1)} %bitcast.29, bf16[256,256]{1,0:T(8,128)(2,1)S(1)} %add_convert_fusion.2.refs_2_, bf16[256,256]{1,0:T(8,128)(2,1)S(1)} %collective-permute-done.25.refs_3_, ...), custom_call_target="tpu_custom_call" | custom-call | flops 1000000 | bytes 1048576 | tf_op jit(solution)/shard_map/finished_mlp/pallas_call | solution.py:296
  77.4 0.8 %finished_attention.1 = (f32[32,768]{1,0:T(8,128)}, f32[1,32]{1,0:T(1,128)}, f32[32,256]{1,0:T(8,128)}) custom-call(bf16[32,768]{1,0:T(8,128)(2,1)S(1)} %copy-done.1, bf16[1,32]{1,0:T(2,128)(2,1)S(1)} %bitcast.27, bf16[128,256]{1,0:T(8,128)(2,1)S(1)} %fusion.2.refs_2_, bf16[128,256]{1,0:T(8,128)(2,1)S(1)} %collective-permute-done.22.refs_3_, ...), custom_call_target="tpu_custom_call" | custom-call | flops 1000000 | bytes 1048576 | tf_op jit(solution)/shard_map/finished_attention/pallas_call | solution.py:296
  (54 shorter events, 7.5 us)
Async XLA Ops:
  1.7 9.5 %collective-permute-start.3 = (bf16[32,768]{1,0:T(8,128)(2,1)S(1)}, bf16[32,768]{1,0:T(8,128)(2,1)S(1)}, u32[]{:S(2)}, u32[]{:S(2)}) collective-permute-start(bf16[32,768]{1,0:T(8,128)(2,1)S(1)} %get-tuple-element.53.refs_8_), channel_id=1, source_target_pairs={{0,6},{1,7},{2,4},{3,5},{4,2},{5,3},{6,0},{7,1},{8,14},{9,15},{10,... | collective-permute-start | bytes 147464 | tf_op jit(solution)/shard_map/ppermute | solution.py:553
  6.9 10.4 %collective-permute-start.2 = (bf16[32,768]{1,0:T(8,128)(2,1)S(1)}, bf16[32,768]{1,0:T(8,128)(2,1)S(1)}, u32[]{:S(2)}, u32[]{:S(2)}) collective-permute-start(bf16[32,768]{1,0:T(8,128)(2,1)S(1)} %get-tuple-element.53.refs_8_), channel_id=1, source_target_pairs={{0,4},{1,5},{2,6},{3,7},{4,0},{5,1},{6,2},{7,3},{8,12},{9,13},{10,... | collective-permute-start | bytes 147464 | tf_op jit(solution)/shard_map/ppermute | solution.py:553
  6.9 10.4 %collective-permute-start.1 = (bf16[32,768]{1,0:T(8,128)(2,1)S(1)}, bf16[32,768]{1,0:T(8,128)(2,1)S(1)}, u32[]{:S(2)}, u32[]{:S(2)}) collective-permute-start(bf16[32,768]{1,0:T(8,128)(2,1)S(1)} %get-tuple-element.53.refs_8_), channel_id=1, source_target_pairs={{0,2},{1,3},{2,0},{3,1},{4,6},{5,7},{6,4},{7,5},{8,10},{9,11},{10,... | collective-permute-start | bytes 147464 | tf_op jit(solution)/shard_map/ppermute | solution.py:553
  7.5 17.2 %collective-permute-start.10 = (bf16[288,256]{1,0:T(8,128)(2,1)S(1)}, bf16[288,256]{1,0:T(8,128)(2,1)S(1)}, u32[]{:S(2)}, u32[]{:S(2)}) collective-permute-start(bf16[288,256]{1,0:T(8,128)(2,1)S(1)} %get-tuple-element.62.refs_7_), channel_id=1, source_target_pairs={{0,6},{1,7},{2,4},{3,5},{4,2},{5,3},{6,0},{7,1},{8,14},{9,15},{10,... | collective-permute-start | bytes 442376 | tf_op jit(solution)/shard_map/ppermute | solution.py:553
  11.2 13.5 %collective-permute-start.9 = (bf16[288,256]{1,0:T(8,128)(2,1)S(1)}, bf16[288,256]{1,0:T(8,128)(2,1)S(1)}, u32[]{:S(2)}, u32[]{:S(2)}) collective-permute-start(bf16[288,256]{1,0:T(8,128)(2,1)S(1)} %get-tuple-element.62.refs_7_), channel_id=1, source_target_pairs={{0,4},{1,5},{2,6},{3,7},{4,0},{5,1},{6,2},{7,3},{8,12},{9,13},{10,... | collective-permute-start | bytes 442376 | tf_op jit(solution)/shard_map/ppermute | solution.py:553
  11.3 13.5 %collective-permute-start.8 = (bf16[288,256]{1,0:T(8,128)(2,1)S(1)}, bf16[288,256]{1,0:T(8,128)(2,1)S(1)}, u32[]{:S(2)}, u32[]{:S(2)}) collective-permute-start(bf16[288,256]{1,0:T(8,128)(2,1)S(1)} %get-tuple-element.62.refs_7_), channel_id=1, source_target_pairs={{0,2},{1,3},{2,0},{3,1},{4,6},{5,7},{6,4},{7,5},{8,10},{9,11},{10,... | collective-permute-start | bytes 442376 | tf_op jit(solution)/shard_map/ppermute | solution.py:553
  17.3 1.4 %collective-permute-start.4 = (bf16[32,768]{1,0:T(8,128)(2,1)S(1)}, bf16[32,768]{1,0:T(8,128)(2,1)S(1)}, u32[]{:S(2)}, u32[]{:S(2)}) collective-permute-start(bf16[32,768]{1,0:T(8,128)(2,1)S(1)} %collective-permute-done.1.refs_10_), channel_id=1, source_target_pairs={{0,1},{1,0},{2,3},{3,2},{4,5},{5,4},{6,7},{7,6},{8,9},{9,8},{10,11... | collective-permute-start | bytes 147464 | tf_op jit(solution)/shard_map/ppermute | solution.py:553
  19.7 6.0 %collective-permute-start.7 = (bf16[288,256]{1,0:T(8,128)(2,1)S(1)}, bf16[288,256]{1,0:T(8,128)(2,1)S(1)}, u32[]{:S(2)}, u32[]{:S(2)}) collective-permute-start(bf16[288,256]{1,0:T(8,128)(2,1)S(1)} %get-tuple-element.62.refs_7_), channel_id=1, source_target_pairs={{0,1},{1,0},{2,3},{3,2},{4,5},{5,4},{6,7},{7,6},{8,9},{9,8},{10,11... | collective-permute-start | bytes 442376 | tf_op jit(solution)/shard_map/ppermute | solution.py:553
  24.8 1.4 %collective-permute-start.11 = (bf16[288,256]{1,0:T(8,128)(2,1)S(1)}, bf16[288,256]{1,0:T(8,128)(2,1)S(1)}, u32[]{:S(2)}, u32[]{:S(2)}) collective-permute-start(bf16[288,256]{1,0:T(8,128)(2,1)S(1)} %collective-permute-done.8.refs_9_), channel_id=1, source_target_pairs={{0,1},{1,0},{2,3},{3,2},{4,5},{5,4},{6,7},{7,6},{8,9},{9,8},{10,11... | collective-permute-start | bytes 442376 | tf_op jit(solution)/shard_map/ppermute | solution.py:553
  25.3 1.4 %collective-permute-start.13 = (bf16[288,256]{1,0:T(8,128)(2,1)S(1)}, bf16[288,256]{1,0:T(8,128)(2,1)S(1)}, u32[]{:S(2)}, u32[]{:S(2)}) collective-permute-start(bf16[288,256]{1,0:T(8,128)(2,1)S(1)} %collective-permute-done.10.refs_13_), channel_id=1, source_target_pairs={{0,1},{1,0},{2,3},{3,2},{4,5},{5,4},{6,7},{7,6},{8,9},{9,8},{10,11... | collective-permute-start | bytes 442376 | tf_op jit(solution)/shard_map/ppermute | solution.py:553
  44.9 2.0 %collective-permute-start.14 = (bf16[4,256,256]{2,1,0:T(8,128)(2,1)S(1)}, bf16[4,256,256]{2,1,0:T(8,128)(2,1)S(1)}, u32[]{:S(2)}, u32[]{:S(2)}) collective-permute-start(bf16[4,256,256]{2,1,0:T(8,128)(2,1)S(1)} %get-tuple-element.82), channel_id=1, source_target_pairs={{0,1},{1,0},{2,3},{3,2},{4,5},{5,4},{6,7},{7,6},{8,9},{9,8},{10,11... | collective-permute-start | bytes 1572872 | tf_op jit(solution)/shard_map/ppermute | solution.py:553
  47.0 12.5 %collective-permute-start.16 = (bf16[256,256]{1,0:T(8,128)(2,1)S(1)}, bf16[256,256]{1,0:T(8,128)(2,1)S(1)}, u32[]{:S(2)}, u32[]{:S(2)}) collective-permute-start(bf16[256,256]{1,0:T(8,128)(2,1)S(1)} %get-tuple-element.93.refs_21_), channel_id=1, source_target_pairs={{0,6},{1,7},{2,4},{3,5},{4,2},{5,3},{6,0},{7,1},{8,14},{9,15},{10,... | collective-permute-start | bytes 393224 | tf_op jit(solution)/shard_map/ppermute | solution.py:553
  48.8 11.4 %collective-permute-start.17 = (bf16[256,256]{1,0:T(8,128)(2,1)S(1)}, bf16[256,256]{1,0:T(8,128)(2,1)S(1)}, u32[]{:S(2)}, u32[]{:S(2)}) collective-permute-start(bf16[256,256]{1,0:T(8,128)(2,1)S(1)} %get-tuple-element.94.refs_20_), channel_id=1, source_target_pairs={{0,4},{1,5},{2,6},{3,7},{4,0},{5,1},{6,2},{7,3},{8,12},{9,13},{10,... | collective-permute-start | bytes 393224 | tf_op jit(solution)/shard_map/ppermute | solution.py:553
  48.8 11.4 %collective-permute-start.18 = (bf16[256,256]{1,0:T(8,128)(2,1)S(1)}, bf16[256,256]{1,0:T(8,128)(2,1)S(1)}, u32[]{:S(2)}, u32[]{:S(2)}) collective-permute-start(bf16[256,256]{1,0:T(8,128)(2,1)S(1)} %get-tuple-element.95.refs_19_), channel_id=1, source_target_pairs={{0,2},{1,3},{2,0},{3,1},{4,6},{5,7},{6,4},{7,5},{8,10},{9,11},{10,... | collective-permute-start | bytes 393224 | tf_op jit(solution)/shard_map/ppermute | solution.py:553
  59.4 1.6 %collective-permute-start.15 = (bf16[4,128,256]{2,1,0:T(8,128)(2,1)S(1)}, bf16[4,128,256]{2,1,0:T(8,128)(2,1)S(1)}, u32[]{:S(2)}, u32[]{:S(2)}) collective-permute-start(bf16[4,128,256]{2,1,0:T(8,128)(2,1)S(1)} %get-tuple-element.86), channel_id=1, source_target_pairs={{0,1},{1,0},{2,3},{3,2},{4,5},{5,4},{6,7},{7,6},{8,9},{9,8},{10,11... | collective-permute-start | bytes 786440 | tf_op jit(solution)/shard_map/ppermute | solution.py:553
  61.2 7.4 %collective-permute-start.19 = (bf16[128,256]{1,0:T(8,128)(2,1)S(1)}, bf16[128,256]{1,0:T(8,128)(2,1)S(1)}, u32[]{:S(2)}, u32[]{:S(2)}) collective-permute-start(bf16[128,256]{1,0:T(8,128)(2,1)S(1)} %get-tuple-element.97), channel_id=1, source_target_pairs={{0,6},{1,7},{2,4},{3,5},{4,2},{5,3},{6,0},{7,1},{8,14},{9,15},{10,... | collective-permute-start | bytes 196616 | tf_op jit(solution)/shard_map/ppermute | solution.py:553
  63.0 6.6 %collective-permute-start.21 = (bf16[128,256]{1,0:T(8,128)(2,1)S(1)}, bf16[128,256]{1,0:T(8,128)(2,1)S(1)}, u32[]{:S(2)}, u32[]{:S(2)}) collective-permute-start(bf16[128,256]{1,0:T(8,128)(2,1)S(1)} %get-tuple-element.98), channel_id=1, source_target_pairs={{0,2},{1,3},{2,0},{3,1},{4,6},{5,7},{6,4},{7,5},{8,10},{9,11},{10,... | collective-permute-start | bytes 196616 | tf_op jit(solution)/shard_map/ppermute | solution.py:553
  63.0 7.0 %collective-permute-start.20 = (bf16[128,256]{1,0:T(8,128)(2,1)S(1)}, bf16[128,256]{1,0:T(8,128)(2,1)S(1)}, u32[]{:S(2)}, u32[]{:S(2)}) collective-permute-start(bf16[128,256]{1,0:T(8,128)(2,1)S(1)} %get-tuple-element.99), channel_id=1, source_target_pairs={{0,4},{1,5},{2,6},{3,7},{4,0},{5,1},{6,2},{7,3},{8,12},{9,13},{10,... | collective-permute-start | bytes 196616 | tf_op jit(solution)/shard_map/ppermute | solution.py:553
  65.6 7.5 %collective-permute-start.27 = (bf16[256,256]{1,0:T(8,128)(2,1)S(1)}, bf16[256,256]{1,0:T(8,128)(2,1)S(1)}, u32[]{:S(2)}, u32[]{:S(2)}) collective-permute-start(bf16[256,256]{1,0:T(8,128)(2,1)S(1)} %add_convert_fusion.2.refs_2_), channel_id=1, source_target_pairs={{0,24},{8,16},{16,8},{24,0},{1,25},{9,17},{17,9},{25,1},{2,26},{10... | collective-permute-start | bytes 393224 | tf_op jit(solution)/shard_map/ppermute | solution.py:553
  68.1 7.7 %collective-permute-start.26 = (bf16[256,256]{1,0:T(8,128)(2,1)S(1)}, bf16[256,256]{1,0:T(8,128)(2,1)S(1)}, u32[]{:S(2)}, u32[]{:S(2)}) collective-permute-start(bf16[256,256]{1,0:T(8,128)(2,1)S(1)} %add_convert_fusion.2.refs_2_), channel_id=1, source_target_pairs={{0,16},{8,24},{16,0},{24,8},{1,17},{9,25},{17,1},{25,9},{2,18},{10... | collective-permute-start | bytes 393224 | tf_op jit(solution)/shard_map/ppermute | solution.py:553
  68.6 7.2 %collective-permute-start.25 = (bf16[256,256]{1,0:T(8,128)(2,1)S(1)}, bf16[256,256]{1,0:T(8,128)(2,1)S(1)}, u32[]{:S(2)}, u32[]{:S(2)}) collective-permute-start(bf16[256,256]{1,0:T(8,128)(2,1)S(1)} %add_convert_fusion.2.refs_2_), channel_id=1, source_target_pairs={{0,8},{8,0},{16,24},{24,16},{1,9},{9,1},{17,25},{25,17},{2,10},{10... | collective-permute-start | bytes 393224 | tf_op jit(solution)/shard_map/ppermute | solution.py:553
  70.0 6.7 %collective-permute-start.24 = (bf16[128,256]{1,0:T(8,128)(2,1)S(1)}, bf16[128,256]{1,0:T(8,128)(2,1)S(1)}, u32[]{:S(2)}, u32[]{:S(2)}) collective-permute-start(bf16[128,256]{1,0:T(8,128)(2,1)S(1)} %fusion.2.refs_2_), channel_id=1, source_target_pairs={{0,24},{8,16},{16,8},{24,0},{1,25},{9,17},{17,9},{25,1},{2,26},{10... | collective-permute-start | bytes 196616 | tf_op jit(solution)/shard_map/ppermute | solution.py:553
  72.6 4.4 %collective-permute-start.23 = (bf16[128,256]{1,0:T(8,128)(2,1)S(1)}, bf16[128,256]{1,0:T(8,128)(2,1)S(1)}, u32[]{:S(2)}, u32[]{:S(2)}) collective-permute-start(bf16[128,256]{1,0:T(8,128)(2,1)S(1)} %fusion.2.refs_2_), channel_id=1, source_target_pairs={{0,16},{8,24},{16,0},{24,8},{1,17},{9,25},{17,1},{25,9},{2,18},{10... | collective-permute-start | bytes 196616 | tf_op jit(solution)/shard_map/ppermute | solution.py:553
  73.1 4.3 %collective-permute-start.22 = (bf16[128,256]{1,0:T(8,128)(2,1)S(1)}, bf16[128,256]{1,0:T(8,128)(2,1)S(1)}, u32[]{:S(2)}, u32[]{:S(2)}) collective-permute-start(bf16[128,256]{1,0:T(8,128)(2,1)S(1)} %fusion.2.refs_2_), channel_id=1, source_target_pairs={{0,8},{8,0},{16,24},{24,16},{1,9},{9,1},{17,25},{25,17},{2,10},{10... | collective-permute-start | bytes 196616 | tf_op jit(solution)/shard_map/ppermute | solution.py:553
  (8 other events, 105.7 us)

commit v6 on v5

--- a/solution.py
+++ b/solution.py
@@ -606,7 +606,8 @@
     saved, wqkv, entering = first_attention(me, prompt_lengths, loop_counts, states, inject, cotangent, n1, mask, qkv_parts, ff)
     saved.update(n1=n1, r1=r1)
     if direct:
-        rest_parts = with_near(rest_far[:1], n_fsdp) + with_near(after(rest_far[1:], wqkv), n_fsdp)
+        late = with_near(after(rest_far[:0:-1], wqkv), n_fsdp)
+        rest_parts = with_near(rest_far[:1], n_fsdp) + [v for x in range(len(late) - 2, -1, -2) for v in late[x:x + 2]]
     final, g, ginj, gm, wout, n1, dpk, ht, gm_two, keep, send = middle_part(
         me, *entering, mask, wqkv, saved["ht"], rest_parts, ff)
     summed = []

time: 78.6 us -> 77.9 us (level)
  waiting for transfers between devices: 11.5 us -> 9.78 us
  starting transfers between devices: 29.8 us -> 30.9 us
    ppermute x28, waiting for transfers between devices: 11.5 us -> 9.78 us  [exchange(): return lax.ppermute(x, axis, [(i, i ^ step) for i in range(size)])]
    ppermute x28, starting transfers between devices: 29.8 us -> 30.9 us  [exchange(): return lax.ppermute(x, axis, [(i, i ^ step) for i in range(size)])]
  transfers between devices with their start and end apart: 28 -> 28, of which waited for: 14 -> 13; matrix products, arithmetic and copies ran while one was open for 0% -> 0% of each run, Pallas kernels for 20% -> 20%
where the time goes in v6:
time: 77.9 us; the launch traced here: 77.7 us
  Pallas kernels  35.6 us (46%)
  starting transfers between devices  30.9 us (40%)
  waiting for transfers between devices  9.78 us (13%)
  between operations  1 us (1%)
    pallas_call x7, Pallas kernels, call(): pl.pallas_call(run, out_shape=tuple((shapes[o[0]](o[1], o[2]) for o in ou...  35.6 us
    ppermute x28, starting transfers between devices, exchange(): return lax.ppermute(x, axis, [(i, i ^ step) for i in range(size)])  30.9 us
    ppermute x28, waiting for transfers between devices, exchange(): return lax.ppermute(x, axis, [(i, i ^ step) for i in range(size)])  9.78 us
  transfers between devices with their start and end apart: 28, of which 13 were waited for; matrix products, arithmetic and copies ran while one was open for 0% of the time, Pallas kernels for 20%

profile of v6, /device:TPU:0, one launch (start us, length us, event | category | flops | bytes accessed | tf_op | source)
XLA Modules:
  0.0 77.7 jit_solution(6007903161900300444)
XLA Ops:
  0.6 1.1 %pack_weights.1 = (bf16[32,768]{1,0:T(8,128)(2,1)S(1)}, bf16[288,256]{1,0:T(8,128)(2,1)S(1)}) custom-call(bf16[32,768]{1,0:T(8,128)(2,1)} %refs_0_.6, bf16[1,32]{1,0:T(2,128)(2,1)} %bitcast.26, bf16[32,256]{1,0:T(8,128)(2,1)} %refs_2_.4, bf16[32,1024]{1,0:T(8,128)(2,1)} %refs_0_.7, bf16[128,256]{1,0:T(8,128)(2,1)} %refs_4_.2, bf16[1,32]{1,0:T(2,128)(2,1)} %bitcast.28), custom_call_target="tpu_custom_call" | custom-call | flops 1000000 | bytes 1048576 | tf_op jit(solution)/shard_map/pack_weights/pallas_call | solution.py:296
  1.7 5.1 %collective-permute-start.3 = (bf16[32,768]{1,0:T(8,128)(2,1)S(1)}, bf16[32,768]{1,0:T(8,128)(2,1)S(1)}, u32[]{:S(2)}, u32[]{:S(2)}) collective-permute-start(bf16[32,768]{1,0:T(8,128)(2,1)S(1)} %get-tuple-element.53.refs_8_), channel_id=1, source_target_pairs={{0,6},{1,7},{2,4},{3,5},{4,2},{5,3},{6,0},{7,1},{8,14},{9,15},{10,... | collective-permute-start | bytes 147464 | tf_op jit(solution)/shard_map/ppermute | solution.py:553
  7.5 1.4 %collective-permute-start.10 = (bf16[288,256]{1,0:T(8,128)(2,1)S(1)}, bf16[288,256]{1,0:T(8,128)(2,1)S(1)}, u32[]{:S(2)}, u32[]{:S(2)}) collective-permute-start(bf16[288,256]{1,0:T(8,128)(2,1)S(1)} %get-tuple-element.62.refs_7_), channel_id=1, source_target_pairs={{0,2},{1,3},{2,0},{3,1},{4,6},{5,7},{6,4},{7,5},{8,10},{9,11},{10,... | collective-permute-start | bytes 442376 | tf_op jit(solution)/shard_map/ppermute | solution.py:553
  8.9 2.9 %collective-permute-start.9 = (bf16[288,256]{1,0:T(8,128)(2,1)S(1)}, bf16[288,256]{1,0:T(8,128)(2,1)S(1)}, u32[]{:S(2)}, u32[]{:S(2)}) collective-permute-start(bf16[288,256]{1,0:T(8,128)(2,1)S(1)} %get-tuple-element.62.refs_7_), channel_id=1, source_target_pairs={{0,4},{1,5},{2,6},{3,7},{4,0},{5,1},{6,2},{7,3},{8,12},{9,13},{10,... | collective-permute-start | bytes 442376 | tf_op jit(solution)/shard_map/ppermute | solution.py:553
  11.8 1.5 %collective-permute-start.8 = (bf16[288,256]{1,0:T(8,128)(2,1)S(1)}, bf16[288,256]{1,0:T(8,128)(2,1)S(1)}, u32[]{:S(2)}, u32[]{:S(2)}) collective-permute-start(bf16[288,256]{1,0:T(8,128)(2,1)S(1)} %get-tuple-element.62.refs_7_), channel_id=1, source_target_pairs={{0,6},{1,7},{2,4},{3,5},{4,2},{5,3},{6,0},{7,1},{8,14},{9,15},{10,... | collective-permute-start | bytes 442376 | tf_op jit(solution)/shard_map/ppermute | solution.py:553
  13.3 2.0 %prepare.1 = (bf16[1024,256]{1,0:T(8,128)(2,1)S(1)}, f32[1024,128]{1,0:T(8,128)S(1)}, f32[8,256,128]{2,1,0:T(8,128)S(1)}) custom-call(s32[1,16]{1,0:T(1,128)} %refs_1_.3, f32[1024,256]{1,0:T(8,128)} %refs_3_.3, f32[1024,256]{1,0:T(8,128)} %refs_4_.3), custom_call_target="tpu_custom_call" | custom-call | flops 1000000 | bytes 1048576 | tf_op jit(solution)/shard_map/prepare/pallas_call | solution.py:296
  15.9 0.7 collective-permute-done.refs_9_
  17.1 0.7 collective-permute-done.5.refs_13_
  18.0 4.8 %first_attention.1 = (bf16[8,4,256,256]{3,2,1,0:T(8,128)(2,1)S(1)}, bf16[1024,256]{1,0:T(8,128)(2,1)S(1)}, bf16[1152,256]{1,0:T(8,128)(2,1)S(1)}, bf16[9,256,128...) custom-call(s32[1]{0:T(128)} %bitcast.refs_0_, ...), custom_call_target="tpu_custom_call" | custom-call | flops 1000000 | bytes 1048576 | tf_op jit(solution)/shard_map/first_attention/pallas_call | solution.py:296
  24.9 18.1 %middle_part.1 = (f32[1024,256]{1,0:T(8,128)}, f32[1024,256]{1,0:T(8,128)S(1)}, f32[1024,256]{1,0:T(8,128)S(1)}, bf16[1024,256]{1,0:T(8,128)(2,1)S(1)}, bf16[256...) custom-call(s32[1]{0:T(128)} %bitcast.refs_0_, ...), custom_call_target="tpu_custom_call" | custom-call | flops 24999999488 | bytes 1048576 | tf_op jit(solution)/shard_map/middle_part/pallas_call | solution.py:296
  43.3 1.6 %collective-permute-done.14 = bf16[4,256,256]{2,1,0:T(8,128)(2,1)S(1)} collective-permute-done((bf16[4,256,256]{2,1,0:T(8,128)(2,1)S(1)}, bf16[4,256,256]{2,1,0:T(8,128)(2,1)S(1)}, u32[]{:S(2)}, u32[]{:S(2)}) %collective-permute-start.14) | collective-permute-done | bytes 524320 | tf_op jit(solution)/shard_map/ppermute | solution.py:553
  45.1 2.4 %collective-permute-start.16 = (bf16[256,256]{1,0:T(8,128)(2,1)S(1)}, bf16[256,256]{1,0:T(8,128)(2,1)S(1)}, u32[]{:S(2)}, u32[]{:S(2)}) collective-permute-start(bf16[256,256]{1,0:T(8,128)(2,1)S(1)} %get-tuple-element.93.refs_21_), channel_id=1, source_target_pairs={{0,6},{1,7},{2,4},{3,5},{4,2},{5,3},{6,0},{7,1},{8,14},{9,15},{10,... | collective-permute-start | bytes 393224 | tf_op jit(solution)/shard_map/ppermute | solution.py:553
  47.5 1.2 %collective-permute-start.17 = (bf16[256,256]{1,0:T(8,128)(2,1)S(1)}, bf16[256,256]{1,0:T(8,128)(2,1)S(1)}, u32[]{:S(2)}, u32[]{:S(2)}) collective-permute-start(bf16[256,256]{1,0:T(8,128)(2,1)S(1)} %get-tuple-element.94.refs_20_), channel_id=1, source_target_pairs={{0,4},{1,5},{2,6},{3,7},{4,0},{5,1},{6,2},{7,3},{8,12},{9,13},{10,... | collective-permute-start | bytes 393224 | tf_op jit(solution)/shard_map/ppermute | solution.py:553
  48.7 0.8 %collective-permute-start.18 = (bf16[256,256]{1,0:T(8,128)(2,1)S(1)}, bf16[256,256]{1,0:T(8,128)(2,1)S(1)}, u32[]{:S(2)}, u32[]{:S(2)}) collective-permute-start(bf16[256,256]{1,0:T(8,128)(2,1)S(1)} %get-tuple-element.95.refs_19_), channel_id=1, source_target_pairs={{0,2},{1,3},{2,0},{3,1},{4,6},{5,7},{6,4},{7,5},{8,10},{9,11},{10,... | collective-permute-start | bytes 393224 | tf_op jit(solution)/shard_map/ppermute | solution.py:553
  49.6 8.0 %last_part.1 = (bf16[4,128,256]{2,1,0:T(8,128)(2,1)S(1)}, bf16[4,128,256]{2,1,0:T(8,128)(2,1)S(1)}, f32[1024,256]{1,0:T(8,128)}, f32[1024,256]{1,0:T(8,128)}) custom-call(s32[1]{0:T(128)} %bitcast.refs_0_, bf16[1024,256]{1,0:T(8,128)(2,1)S(1)} %get-tuple-element.67.refs_1_, bf16[256,256]{1,0:T(8,128)(2,1)S(1)} %get-tuple-element.68.refs_2_, ...), custom_call_target="tpu_custom_call" | custom-call | flops 10000000000 | bytes 1048576 | tf_op jit(solution)/shard_map/last_part/pallas_call | solution.py:296
  57.7 3.0 %collective-permute-done.17 = bf16[256,256]{1,0:T(8,128)(2,1)S(1)} collective-permute-done((bf16[256,256]{1,0:T(8,128)(2,1)S(1)}, bf16[256,256]{1,0:T(8,128)(2,1)S(1)}, u32[]{:S(2)}, u32[]{:S(2)}) %collective-permute-start.17) | collective-permute-done | bytes 131104 | tf_op jit(solution)/shard_map/ppermute | solution.py:553
  60.9 2.3 %collective-permute-start.19 = (bf16[128,256]{1,0:T(8,128)(2,1)S(1)}, bf16[128,256]{1,0:T(8,128)(2,1)S(1)}, u32[]{:S(2)}, u32[]{:S(2)}) collective-permute-start(bf16[128,256]{1,0:T(8,128)(2,1)S(1)} %get-tuple-element.97), channel_id=1, source_target_pairs={{0,6},{1,7},{2,4},{3,5},{4,2},{5,3},{6,0},{7,1},{8,14},{9,15},{10,... | collective-permute-start | bytes 196616 | tf_op jit(solution)/shard_map/ppermute | solution.py:553
  63.2 2.2 %collective-permute-start.20 = (bf16[128,256]{1,0:T(8,128)(2,1)S(1)}, bf16[128,256]{1,0:T(8,128)(2,1)S(1)}, u32[]{:S(2)}, u32[]{:S(2)}) collective-permute-start(bf16[128,256]{1,0:T(8,128)(2,1)S(1)} %get-tuple-element.99), channel_id=1, source_target_pairs={{0,4},{1,5},{2,6},{3,7},{4,0},{5,1},{6,2},{7,3},{8,12},{9,13},{10,... | collective-permute-start | bytes 196616 | tf_op jit(solution)/shard_map/ppermute | solution.py:553
  65.4 2.5 %collective-permute-start.27 = (bf16[256,256]{1,0:T(8,128)(2,1)S(1)}, bf16[256,256]{1,0:T(8,128)(2,1)S(1)}, u32[]{:S(2)}, u32[]{:S(2)}) collective-permute-start(bf16[256,256]{1,0:T(8,128)(2,1)S(1)} %add_convert_fusion.2.refs_2_), channel_id=1, source_target_pairs={{0,24},{8,16},{16,8},{24,0},{1,25},{9,17},{17,9},{25,1},{2,26},{10... | collective-permute-start | bytes 393224 | tf_op jit(solution)/shard_map/ppermute | solution.py:553
  69.3 2.6 %collective-permute-start.24 = (bf16[128,256]{1,0:T(8,128)(2,1)S(1)}, bf16[128,256]{1,0:T(8,128)(2,1)S(1)}, u32[]{:S(2)}, u32[]{:S(2)}) collective-permute-start(bf16[128,256]{1,0:T(8,128)(2,1)S(1)} %fusion.2.refs_2_), channel_id=1, source_target_pairs={{0,24},{8,16},{16,8},{24,0},{1,25},{9,17},{17,9},{25,1},{2,26},{10... | collective-permute-start | bytes 196616 | tf_op jit(solution)/shard_map/ppermute | solution.py:553
  72.4 1.2 %collective-permute-start.22 = (bf16[128,256]{1,0:T(8,128)(2,1)S(1)}, bf16[128,256]{1,0:T(8,128)(2,1)S(1)}, u32[]{:S(2)}, u32[]{:S(2)}) collective-permute-start(bf16[128,256]{1,0:T(8,128)(2,1)S(1)} %fusion.2.refs_2_), channel_id=1, source_target_pairs={{0,8},{8,0},{16,24},{24,16},{1,9},{9,1},{17,25},{25,17},{2,10},{10... | collective-permute-start | bytes 196616 | tf_op jit(solution)/shard_map/ppermute | solution.py:553
  74.2 0.9 %finished_mlp.1 = (f32[32,1024]{1,0:T(8,128)}, f32[1,32]{1,0:T(1,128)}, f32[128,256]{1,0:T(8,128)}) custom-call(bf16[32,1024]{1,0:T(8,128)(2,1)S(1)} %copy-done, bf16[1,32]{1,0:T(2,128)(2,1)S(1)} %bitcast.29, bf16[256,256]{1,0:T(8,128)(2,1)S(1)} %add_convert_fusion.2.refs_2_, bf16[256,256]{1,0:T(8,128)(2,1)S(1)} %collective-permute-done.25.refs_3_, ...), custom_call_target="tpu_custom_call" | custom-call | flops 1000000 | bytes 1048576 | tf_op jit(solution)/shard_map/finished_mlp/pallas_call | solution.py:296
  75.1 0.7 collective-permute-done.24.refs_5_
  76.7 0.8 %finished_attention.1 = (f32[32,768]{1,0:T(8,128)}, f32[1,32]{1,0:T(1,128)}, f32[32,256]{1,0:T(8,128)}) custom-call(bf16[32,768]{1,0:T(8,128)(2,1)S(1)} %copy-done.1, bf16[1,32]{1,0:T(2,128)(2,1)S(1)} %bitcast.27, bf16[128,256]{1,0:T(8,128)(2,1)S(1)} %fusion.2.refs_2_, bf16[128,256]{1,0:T(8,128)(2,1)S(1)} %collective-permute-done.22.refs_3_, ...), custom_call_target="tpu_custom_call" | custom-call | flops 1000000 | bytes 1048576 | tf_op jit(solution)/shard_map/finished_attention/pallas_call | solution.py:296
  (54 shorter events, 8.2 us)
Async XLA Ops:
  1.7 10.1 %collective-permute-start.3 = (bf16[32,768]{1,0:T(8,128)(2,1)S(1)}, bf16[32,768]{1,0:T(8,128)(2,1)S(1)}, u32[]{:S(2)}, u32[]{:S(2)}) collective-permute-start(bf16[32,768]{1,0:T(8,128)(2,1)S(1)} %get-tuple-element.53.refs_8_), channel_id=1, source_target_pairs={{0,6},{1,7},{2,4},{3,5},{4,2},{5,3},{6,0},{7,1},{8,14},{9,15},{10,... | collective-permute-start | bytes 147464 | tf_op jit(solution)/shard_map/ppermute | solution.py:553
  6.9 8.5 %collective-permute-start.2 = (bf16[32,768]{1,0:T(8,128)(2,1)S(1)}, bf16[32,768]{1,0:T(8,128)(2,1)S(1)}, u32[]{:S(2)}, u32[]{:S(2)}) collective-permute-start(bf16[32,768]{1,0:T(8,128)(2,1)S(1)} %get-tuple-element.53.refs_8_), channel_id=1, source_target_pairs={{0,4},{1,5},{2,6},{3,7},{4,0},{5,1},{6,2},{7,3},{8,12},{9,13},{10,... | collective-permute-start | bytes 147464 | tf_op jit(solution)/shard_map/ppermute | solution.py:553
  6.9 8.5 %collective-permute-start.1 = (bf16[32,768]{1,0:T(8,128)(2,1)S(1)}, bf16[32,768]{1,0:T(8,128)(2,1)S(1)}, u32[]{:S(2)}, u32[]{:S(2)}) collective-permute-start(bf16[32,768]{1,0:T(8,128)(2,1)S(1)} %get-tuple-element.53.refs_8_), channel_id=1, source_target_pairs={{0,2},{1,3},{2,0},{3,1},{4,6},{5,7},{6,4},{7,5},{8,10},{9,11},{10,... | collective-permute-start | bytes 147464 | tf_op jit(solution)/shard_map/ppermute | solution.py:553
  7.5 15.4 %collective-permute-start.10 = (bf16[288,256]{1,0:T(8,128)(2,1)S(1)}, bf16[288,256]{1,0:T(8,128)(2,1)S(1)}, u32[]{:S(2)}, u32[]{:S(2)}) collective-permute-start(bf16[288,256]{1,0:T(8,128)(2,1)S(1)} %get-tuple-element.62.refs_7_), channel_id=1, source_target_pairs={{0,2},{1,3},{2,0},{3,1},{4,6},{5,7},{6,4},{7,5},{8,10},{9,11},{10,... | collective-permute-start | bytes 442376 | tf_op jit(solution)/shard_map/ppermute | solution.py:553
  8.9 14.0 %collective-permute-start.9 = (bf16[288,256]{1,0:T(8,128)(2,1)S(1)}, bf16[288,256]{1,0:T(8,128)(2,1)S(1)}, u32[]{:S(2)}, u32[]{:S(2)}) collective-permute-start(bf16[288,256]{1,0:T(8,128)(2,1)S(1)} %get-tuple-element.62.refs_7_), channel_id=1, source_target_pairs={{0,4},{1,5},{2,6},{3,7},{4,0},{5,1},{6,2},{7,3},{8,12},{9,13},{10,... | collective-permute-start | bytes 442376 | tf_op jit(solution)/shard_map/ppermute | solution.py:553
  11.8 11.1 %collective-permute-start.8 = (bf16[288,256]{1,0:T(8,128)(2,1)S(1)}, bf16[288,256]{1,0:T(8,128)(2,1)S(1)}, u32[]{:S(2)}, u32[]{:S(2)}) collective-permute-start(bf16[288,256]{1,0:T(8,128)(2,1)S(1)} %get-tuple-element.62.refs_7_), channel_id=1, source_target_pairs={{0,6},{1,7},{2,4},{3,5},{4,2},{5,3},{6,0},{7,1},{8,14},{9,15},{10,... | collective-permute-start | bytes 442376 | tf_op jit(solution)/shard_map/ppermute | solution.py:553
  15.4 1.4 %collective-permute-start.4 = (bf16[32,768]{1,0:T(8,128)(2,1)S(1)}, bf16[32,768]{1,0:T(8,128)(2,1)S(1)}, u32[]{:S(2)}, u32[]{:S(2)}) collective-permute-start(bf16[32,768]{1,0:T(8,128)(2,1)S(1)} %collective-permute-done.1.refs_10_), channel_id=1, source_target_pairs={{0,1},{1,0},{2,3},{3,2},{4,5},{5,4},{6,7},{7,6},{8,9},{9,8},{10,11... | collective-permute-start | bytes 147464 | tf_op jit(solution)/shard_map/ppermute | solution.py:553
  17.8 6.0 %collective-permute-start.7 = (bf16[288,256]{1,0:T(8,128)(2,1)S(1)}, bf16[288,256]{1,0:T(8,128)(2,1)S(1)}, u32[]{:S(2)}, u32[]{:S(2)}) collective-permute-start(bf16[288,256]{1,0:T(8,128)(2,1)S(1)} %get-tuple-element.62.refs_7_), channel_id=1, source_target_pairs={{0,1},{1,0},{2,3},{3,2},{4,5},{5,4},{6,7},{7,6},{8,9},{9,8},{10,11... | collective-permute-start | bytes 442376 | tf_op jit(solution)/shard_map/ppermute | solution.py:553
  22.9 1.4 %collective-permute-start.11 = (bf16[288,256]{1,0:T(8,128)(2,1)S(1)}, bf16[288,256]{1,0:T(8,128)(2,1)S(1)}, u32[]{:S(2)}, u32[]{:S(2)}) collective-permute-start(bf16[288,256]{1,0:T(8,128)(2,1)S(1)} %collective-permute-done.10.refs_9_), channel_id=1, source_target_pairs={{0,1},{1,0},{2,3},{3,2},{4,5},{5,4},{6,7},{7,6},{8,9},{9,8},{10,11... | collective-permute-start | bytes 442376 | tf_op jit(solution)/shard_map/ppermute | solution.py:553
  23.5 1.4 %collective-permute-start.13 = (bf16[288,256]{1,0:T(8,128)(2,1)S(1)}, bf16[288,256]{1,0:T(8,128)(2,1)S(1)}, u32[]{:S(2)}, u32[]{:S(2)}) collective-permute-start(bf16[288,256]{1,0:T(8,128)(2,1)S(1)} %collective-permute-done.8.refs_13_), channel_id=1, source_target_pairs={{0,1},{1,0},{2,3},{3,2},{4,5},{5,4},{6,7},{7,6},{8,9},{9,8},{10,11... | collective-permute-start | bytes 442376 | tf_op jit(solution)/shard_map/ppermute | solution.py:553
  43.0 2.0 %collective-permute-start.14 = (bf16[4,256,256]{2,1,0:T(8,128)(2,1)S(1)}, bf16[4,256,256]{2,1,0:T(8,128)(2,1)S(1)}, u32[]{:S(2)}, u32[]{:S(2)}) collective-permute-start(bf16[4,256,256]{2,1,0:T(8,128)(2,1)S(1)} %get-tuple-element.82), channel_id=1, source_target_pairs={{0,1},{1,0},{2,3},{3,2},{4,5},{5,4},{6,7},{7,6},{8,9},{9,8},{10,11... | collective-permute-start | bytes 1572872 | tf_op jit(solution)/shard_map/ppermute | solution.py:553
  45.1 12.5 %collective-permute-start.16 = (bf16[256,256]{1,0:T(8,128)(2,1)S(1)}, bf16[256,256]{1,0:T(8,128)(2,1)S(1)}, u32[]{:S(2)}, u32[]{:S(2)}) collective-permute-start(bf16[256,256]{1,0:T(8,128)(2,1)S(1)} %get-tuple-element.93.refs_21_), channel_id=1, source_target_pairs={{0,6},{1,7},{2,4},{3,5},{4,2},{5,3},{6,0},{7,1},{8,14},{9,15},{10,... | collective-permute-start | bytes 393224 | tf_op jit(solution)/shard_map/ppermute | solution.py:553
  47.5 13.2 %collective-permute-start.17 = (bf16[256,256]{1,0:T(8,128)(2,1)S(1)}, bf16[256,256]{1,0:T(8,128)(2,1)S(1)}, u32[]{:S(2)}, u32[]{:S(2)}) collective-permute-start(bf16[256,256]{1,0:T(8,128)(2,1)S(1)} %get-tuple-element.94.refs_20_), channel_id=1, source_target_pairs={{0,4},{1,5},{2,6},{3,7},{4,0},{5,1},{6,2},{7,3},{8,12},{9,13},{10,... | collective-permute-start | bytes 393224 | tf_op jit(solution)/shard_map/ppermute | solution.py:553
  48.7 12.0 %collective-permute-start.18 = (bf16[256,256]{1,0:T(8,128)(2,1)S(1)}, bf16[256,256]{1,0:T(8,128)(2,1)S(1)}, u32[]{:S(2)}, u32[]{:S(2)}) collective-permute-start(bf16[256,256]{1,0:T(8,128)(2,1)S(1)} %get-tuple-element.95.refs_19_), channel_id=1, source_target_pairs={{0,2},{1,3},{2,0},{3,1},{4,6},{5,7},{6,4},{7,5},{8,10},{9,11},{10,... | collective-permute-start | bytes 393224 | tf_op jit(solution)/shard_map/ppermute | solution.py:553
  57.6 3.2 %collective-permute-start.15 = (bf16[4,128,256]{2,1,0:T(8,128)(2,1)S(1)}, bf16[4,128,256]{2,1,0:T(8,128)(2,1)S(1)}, u32[]{:S(2)}, u32[]{:S(2)}) collective-permute-start(bf16[4,128,256]{2,1,0:T(8,128)(2,1)S(1)} %get-tuple-element.86), channel_id=1, source_target_pairs={{0,1},{1,0},{2,3},{3,2},{4,5},{5,4},{6,7},{7,6},{8,9},{9,8},{10,11... | collective-permute-start | bytes 786440 | tf_op jit(solution)/shard_map/ppermute | solution.py:553
  60.9 7.5 %collective-permute-start.19 = (bf16[128,256]{1,0:T(8,128)(2,1)S(1)}, bf16[128,256]{1,0:T(8,128)(2,1)S(1)}, u32[]{:S(2)}, u32[]{:S(2)}) collective-permute-start(bf16[128,256]{1,0:T(8,128)(2,1)S(1)} %get-tuple-element.97), channel_id=1, source_target_pairs={{0,6},{1,7},{2,4},{3,5},{4,2},{5,3},{6,0},{7,1},{8,14},{9,15},{10,... | collective-permute-start | bytes 196616 | tf_op jit(solution)/shard_map/ppermute | solution.py:553
  63.2 6.0 %collective-permute-start.21 = (bf16[128,256]{1,0:T(8,128)(2,1)S(1)}, bf16[128,256]{1,0:T(8,128)(2,1)S(1)}, u32[]{:S(2)}, u32[]{:S(2)}) collective-permute-start(bf16[128,256]{1,0:T(8,128)(2,1)S(1)} %get-tuple-element.98), channel_id=1, source_target_pairs={{0,2},{1,3},{2,0},{3,1},{4,6},{5,7},{6,4},{7,5},{8,10},{9,11},{10,... | collective-permute-start | bytes 196616 | tf_op jit(solution)/shard_map/ppermute | solution.py:553
  63.2 6.0 %collective-permute-start.20 = (bf16[128,256]{1,0:T(8,128)(2,1)S(1)}, bf16[128,256]{1,0:T(8,128)(2,1)S(1)}, u32[]{:S(2)}, u32[]{:S(2)}) collective-permute-start(bf16[128,256]{1,0:T(8,128)(2,1)S(1)} %get-tuple-element.99), channel_id=1, source_target_pairs={{0,4},{1,5},{2,6},{3,7},{4,0},{5,1},{6,2},{7,3},{8,12},{9,13},{10,... | collective-permute-start | bytes 196616 | tf_op jit(solution)/shard_map/ppermute | solution.py:553
  65.4 7.0 %collective-permute-start.27 = (bf16[256,256]{1,0:T(8,128)(2,1)S(1)}, bf16[256,256]{1,0:T(8,128)(2,1)S(1)}, u32[]{:S(2)}, u32[]{:S(2)}) collective-permute-start(bf16[256,256]{1,0:T(8,128)(2,1)S(1)} %add_convert_fusion.2.refs_2_), channel_id=1, source_target_pairs={{0,24},{8,16},{16,8},{24,0},{1,25},{9,17},{17,9},{25,1},{2,26},{10... | collective-permute-start | bytes 393224 | tf_op jit(solution)/shard_map/ppermute | solution.py:553
  67.9 6.1 %collective-permute-start.26 = (bf16[256,256]{1,0:T(8,128)(2,1)S(1)}, bf16[256,256]{1,0:T(8,128)(2,1)S(1)}, u32[]{:S(2)}, u32[]{:S(2)}) collective-permute-start(bf16[256,256]{1,0:T(8,128)(2,1)S(1)} %add_convert_fusion.2.refs_2_), channel_id=1, source_target_pairs={{0,16},{8,24},{16,0},{24,8},{1,17},{9,25},{17,1},{25,9},{2,18},{10... | collective-permute-start | bytes 393224 | tf_op jit(solution)/shard_map/ppermute | solution.py:553
  68.4 5.8 %collective-permute-start.25 = (bf16[256,256]{1,0:T(8,128)(2,1)S(1)}, bf16[256,256]{1,0:T(8,128)(2,1)S(1)}, u32[]{:S(2)}, u32[]{:S(2)}) collective-permute-start(bf16[256,256]{1,0:T(8,128)(2,1)S(1)} %add_convert_fusion.2.refs_2_), channel_id=1, source_target_pairs={{0,8},{8,0},{16,24},{24,16},{1,9},{9,1},{17,25},{25,17},{2,10},{10... | collective-permute-start | bytes 393224 | tf_op jit(solution)/shard_map/ppermute | solution.py:553
  69.3 6.5 %collective-permute-start.24 = (bf16[128,256]{1,0:T(8,128)(2,1)S(1)}, bf16[128,256]{1,0:T(8,128)(2,1)S(1)}, u32[]{:S(2)}, u32[]{:S(2)}) collective-permute-start(bf16[128,256]{1,0:T(8,128)(2,1)S(1)} %fusion.2.refs_2_), channel_id=1, source_target_pairs={{0,24},{8,16},{16,8},{24,0},{1,25},{9,17},{17,9},{25,1},{2,26},{10... | collective-permute-start | bytes 196616 | tf_op jit(solution)/shard_map/ppermute | solution.py:553
  71.8 4.4 %collective-permute-start.23 = (bf16[128,256]{1,0:T(8,128)(2,1)S(1)}, bf16[128,256]{1,0:T(8,128)(2,1)S(1)}, u32[]{:S(2)}, u32[]{:S(2)}) collective-permute-start(bf16[128,256]{1,0:T(8,128)(2,1)S(1)} %fusion.2.refs_2_), channel_id=1, source_target_pairs={{0,16},{8,24},{16,0},{24,8},{1,17},{9,25},{17,1},{25,9},{2,18},{10... | collective-permute-start | bytes 196616 | tf_op jit(solution)/shard_map/ppermute | solution.py:553
  72.4 4.3 %collective-permute-start.22 = (bf16[128,256]{1,0:T(8,128)(2,1)S(1)}, bf16[128,256]{1,0:T(8,128)(2,1)S(1)}, u32[]{:S(2)}, u32[]{:S(2)}) collective-permute-start(bf16[128,256]{1,0:T(8,128)(2,1)S(1)} %fusion.2.refs_2_), channel_id=1, source_target_pairs={{0,8},{8,0},{16,24},{24,16},{1,9},{9,1},{17,25},{25,17},{2,10},{10... | collective-permute-start | bytes 196616 | tf_op jit(solution)/shard_map/ppermute | solution.py:553
  (8 other events, 108.5 us)

commit v7 on v6

--- a/solution.py
+++ b/solution.py
@@ -613,7 +613,7 @@
     summed = []
     if direct:
         summed = sum_near(keep, exchange(send, "fsdp", n_fsdp, 1))
-        far = send_far(summed, n_fsdp)
+        far = send_far(summed, n_fsdp)[::-1]
     else:
         shares = [reduce_whole(keep[0], [d] * (ff // d) + [ff])]
     keep_qkv, send_qkv, grad_states, grad_inject = last_part(

time: 77.9 us -> 77.9 us (level)
  no operation moved by 1% of the time
where the time goes in v7:
time: 77.9 us; the launch traced here: 77.7 us
  Pallas kernels  35.6 us (46%)
  starting transfers between devices  30.9 us (40%)
  waiting for transfers between devices  9.78 us (13%)
  between operations  1 us (1%)
    pallas_call x7, Pallas kernels, call(): pl.pallas_call(run, out_shape=tuple((shapes[o[0]](o[1], o[2]) for o in ou...  35.6 us
    ppermute x28, starting transfers between devices, exchange(): return lax.ppermute(x, axis, [(i, i ^ step) for i in range(size)])  30.9 us
    ppermute x28, waiting for transfers between devices, exchange(): return lax.ppermute(x, axis, [(i, i ^ step) for i in range(size)])  9.78 us
  transfers between devices with their start and end apart: 28, of which 13 were waited for; matrix products, arithmetic and copies ran while one was open for 0% of the time, Pallas kernels for 20%

profile of v7, /device:TPU:0, one launch (start us, length us, event | category | flops | bytes accessed | tf_op | source)
XLA Modules:
  0.0 77.7 jit_solution(4670526780871166540)
XLA Ops:
  0.6 1.1 %pack_weights.1 = (bf16[32,768]{1,0:T(8,128)(2,1)S(1)}, bf16[288,256]{1,0:T(8,128)(2,1)S(1)}) custom-call(bf16[32,768]{1,0:T(8,128)(2,1)} %refs_0_.6, bf16[1,32]{1,0:T(2,128)(2,1)} %bitcast.26, bf16[32,256]{1,0:T(8,128)(2,1)} %refs_2_.4, bf16[32,1024]{1,0:T(8,128)(2,1)} %refs_0_.7, bf16[128,256]{1,0:T(8,128)(2,1)} %refs_4_.2, bf16[1,32]{1,0:T(2,128)(2,1)} %bitcast.28), custom_call_target="tpu_custom_call" | custom-call | flops 1000000 | bytes 1048576 | tf_op jit(solution)/shard_map/pack_weights/pallas_call | solution.py:296
  1.7 5.1 %collective-permute-start.3 = (bf16[32,768]{1,0:T(8,128)(2,1)S(1)}, bf16[32,768]{1,0:T(8,128)(2,1)S(1)}, u32[]{:S(2)}, u32[]{:S(2)}) collective-permute-start(bf16[32,768]{1,0:T(8,128)(2,1)S(1)} %get-tuple-element.53.refs_8_), channel_id=1, source_target_pairs={{0,6},{1,7},{2,4},{3,5},{4,2},{5,3},{6,0},{7,1},{8,14},{9,15},{10,... | collective-permute-start | bytes 147464 | tf_op jit(solution)/shard_map/ppermute | solution.py:553
  7.5 1.4 %collective-permute-start.10 = (bf16[288,256]{1,0:T(8,128)(2,1)S(1)}, bf16[288,256]{1,0:T(8,128)(2,1)S(1)}, u32[]{:S(2)}, u32[]{:S(2)}) collective-permute-start(bf16[288,256]{1,0:T(8,128)(2,1)S(1)} %get-tuple-element.62.refs_7_), channel_id=1, source_target_pairs={{0,2},{1,3},{2,0},{3,1},{4,6},{5,7},{6,4},{7,5},{8,10},{9,11},{10,... | collective-permute-start | bytes 442376 | tf_op jit(solution)/shard_map/ppermute | solution.py:553
  8.9 2.9 %collective-permute-start.9 = (bf16[288,256]{1,0:T(8,128)(2,1)S(1)}, bf16[288,256]{1,0:T(8,128)(2,1)S(1)}, u32[]{:S(2)}, u32[]{:S(2)}) collective-permute-start(bf16[288,256]{1,0:T(8,128)(2,1)S(1)} %get-tuple-element.62.refs_7_), channel_id=1, source_target_pairs={{0,4},{1,5},{2,6},{3,7},{4,0},{5,1},{6,2},{7,3},{8,12},{9,13},{10,... | collective-permute-start | bytes 442376 | tf_op jit(solution)/shard_map/ppermute | solution.py:553
  11.8 1.5 %collective-permute-start.8 = (bf16[288,256]{1,0:T(8,128)(2,1)S(1)}, bf16[288,256]{1,0:T(8,128)(2,1)S(1)}, u32[]{:S(2)}, u32[]{:S(2)}) collective-permute-start(bf16[288,256]{1,0:T(8,128)(2,1)S(1)} %get-tuple-element.62.refs_7_), channel_id=1, source_target_pairs={{0,6},{1,7},{2,4},{3,5},{4,2},{5,3},{6,0},{7,1},{8,14},{9,15},{10,... | collective-permute-start | bytes 442376 | tf_op jit(solution)/shard_map/ppermute | solution.py:553
  13.3 2.0 %prepare.1 = (bf16[1024,256]{1,0:T(8,128)(2,1)S(1)}, f32[1024,128]{1,0:T(8,128)S(1)}, f32[8,256,128]{2,1,0:T(8,128)S(1)}) custom-call(s32[1,16]{1,0:T(1,128)} %refs_1_.3, f32[1024,256]{1,0:T(8,128)} %refs_3_.3, f32[1024,256]{1,0:T(8,128)} %refs_4_.3), custom_call_target="tpu_custom_call" | custom-call | flops 1000000 | bytes 1048576 | tf_op jit(solution)/shard_map/prepare/pallas_call | solution.py:296
  15.9 0.7 collective-permute-done.refs_9_
  17.1 0.7 collective-permute-done.5.refs_13_
  18.0 4.8 %first_attention.1 = (bf16[8,4,256,256]{3,2,1,0:T(8,128)(2,1)S(1)}, bf16[1024,256]{1,0:T(8,128)(2,1)S(1)}, bf16[1152,256]{1,0:T(8,128)(2,1)S(1)}, bf16[9,256,128...) custom-call(s32[1]{0:T(128)} %bitcast.refs_0_, ...), custom_call_target="tpu_custom_call" | custom-call | flops 1000000 | bytes 1048576 | tf_op jit(solution)/shard_map/first_attention/pallas_call | solution.py:296
  24.9 18.1 %middle_part.1 = (f32[1024,256]{1,0:T(8,128)}, f32[1024,256]{1,0:T(8,128)S(1)}, f32[1024,256]{1,0:T(8,128)S(1)}, bf16[1024,256]{1,0:T(8,128)(2,1)S(1)}, bf16[256...) custom-call(s32[1]{0:T(128)} %bitcast.refs_0_, ...), custom_call_target="tpu_custom_call" | custom-call | flops 24999999488 | bytes 1048576 | tf_op jit(solution)/shard_map/middle_part/pallas_call | solution.py:296
  43.3 1.6 %collective-permute-done.14 = bf16[4,256,256]{2,1,0:T(8,128)(2,1)S(1)} collective-permute-done((bf16[4,256,256]{2,1,0:T(8,128)(2,1)S(1)}, bf16[4,256,256]{2,1,0:T(8,128)(2,1)S(1)}, u32[]{:S(2)}, u32[]{:S(2)}) %collective-permute-start.14) | collective-permute-done | bytes 524320 | tf_op jit(solution)/shard_map/ppermute | solution.py:553
  45.1 2.4 %collective-permute-start.18 = (bf16[256,256]{1,0:T(8,128)(2,1)S(1)}, bf16[256,256]{1,0:T(8,128)(2,1)S(1)}, u32[]{:S(2)}, u32[]{:S(2)}) collective-permute-start(bf16[256,256]{1,0:T(8,128)(2,1)S(1)} %get-tuple-element.93.refs_21_), channel_id=1, source_target_pairs={{0,6},{1,7},{2,4},{3,5},{4,2},{5,3},{6,0},{7,1},{8,14},{9,15},{10,... | collective-permute-start | bytes 393224 | tf_op jit(solution)/shard_map/ppermute | solution.py:553
  47.5 1.2 %collective-permute-start.17 = (bf16[256,256]{1,0:T(8,128)(2,1)S(1)}, bf16[256,256]{1,0:T(8,128)(2,1)S(1)}, u32[]{:S(2)}, u32[]{:S(2)}) collective-permute-start(bf16[256,256]{1,0:T(8,128)(2,1)S(1)} %get-tuple-element.94.refs_20_), channel_id=1, source_target_pairs={{0,4},{1,5},{2,6},{3,7},{4,0},{5,1},{6,2},{7,3},{8,12},{9,13},{10,... | collective-permute-start | bytes 393224 | tf_op jit(solution)/shard_map/ppermute | solution.py:553
  48.7 0.8 %collective-permute-start.16 = (bf16[256,256]{1,0:T(8,128)(2,1)S(1)}, bf16[256,256]{1,0:T(8,128)(2,1)S(1)}, u32[]{:S(2)}, u32[]{:S(2)}) collective-permute-start(bf16[256,256]{1,0:T(8,128)(2,1)S(1)} %get-tuple-element.95.refs_19_), channel_id=1, source_target_pairs={{0,2},{1,3},{2,0},{3,1},{4,6},{5,7},{6,4},{7,5},{8,10},{9,11},{10,... | collective-permute-start | bytes 393224 | tf_op jit(solution)/shard_map/ppermute | solution.py:553
  49.6 8.0 %last_part.1 = (bf16[4,128,256]{2,1,0:T(8,128)(2,1)S(1)}, bf16[4,128,256]{2,1,0:T(8,128)(2,1)S(1)}, f32[1024,256]{1,0:T(8,128)}, f32[1024,256]{1,0:T(8,128)}) custom-call(s32[1]{0:T(128)} %bitcast.refs_0_, bf16[1024,256]{1,0:T(8,128)(2,1)S(1)} %get-tuple-element.67.refs_1_, bf16[256,256]{1,0:T(8,128)(2,1)S(1)} %get-tuple-element.68.refs_2_, ...), custom_call_target="tpu_custom_call" | custom-call | flops 10000000000 | bytes 1048576 | tf_op jit(solution)/shard_map/last_part/pallas_call | solution.py:296
  57.7 3.0 %collective-permute-done.17 = bf16[256,256]{1,0:T(8,128)(2,1)S(1)} collective-permute-done((bf16[256,256]{1,0:T(8,128)(2,1)S(1)}, bf16[256,256]{1,0:T(8,128)(2,1)S(1)}, u32[]{:S(2)}, u32[]{:S(2)}) %collective-permute-start.17) | collective-permute-done | bytes 131104 | tf_op jit(solution)/shard_map/ppermute | solution.py:553
  60.9 2.3 %collective-permute-start.19 = (bf16[128,256]{1,0:T(8,128)(2,1)S(1)}, bf16[128,256]{1,0:T(8,128)(2,1)S(1)}, u32[]{:S(2)}, u32[]{:S(2)}) collective-permute-start(bf16[128,256]{1,0:T(8,128)(2,1)S(1)} %get-tuple-element.97), channel_id=1, source_target_pairs={{0,6},{1,7},{2,4},{3,5},{4,2},{5,3},{6,0},{7,1},{8,14},{9,15},{10,... | collective-permute-start | bytes 196616 | tf_op jit(solution)/shard_map/ppermute | solution.py:553
  63.2 2.2 %collective-permute-start.20 = (bf16[128,256]{1,0:T(8,128)(2,1)S(1)}, bf16[128,256]{1,0:T(8,128)(2,1)S(1)}, u32[]{:S(2)}, u32[]{:S(2)}) collective-permute-start(bf16[128,256]{1,0:T(8,128)(2,1)S(1)} %get-tuple-element.99), channel_id=1, source_target_pairs={{0,4},{1,5},{2,6},{3,7},{4,0},{5,1},{6,2},{7,3},{8,12},{9,13},{10,... | collective-permute-start | bytes 196616 | tf_op jit(solution)/shard_map/ppermute | solution.py:553
  65.4 2.5 %collective-permute-start.27 = (bf16[256,256]{1,0:T(8,128)(2,1)S(1)}, bf16[256,256]{1,0:T(8,128)(2,1)S(1)}, u32[]{:S(2)}, u32[]{:S(2)}) collective-permute-start(bf16[256,256]{1,0:T(8,128)(2,1)S(1)} %add_convert_fusion.2.refs_2_), channel_id=1, source_target_pairs={{0,24},{8,16},{16,8},{24,0},{1,25},{9,17},{17,9},{25,1},{2,26},{10... | collective-permute-start | bytes 393224 | tf_op jit(solution)/shard_map/ppermute | solution.py:553
  69.3 2.6 %collective-permute-start.24 = (bf16[128,256]{1,0:T(8,128)(2,1)S(1)}, bf16[128,256]{1,0:T(8,128)(2,1)S(1)}, u32[]{:S(2)}, u32[]{:S(2)}) collective-permute-start(bf16[128,256]{1,0:T(8,128)(2,1)S(1)} %fusion.2.refs_2_), channel_id=1, source_target_pairs={{0,24},{8,16},{16,8},{24,0},{1,25},{9,17},{17,9},{25,1},{2,26},{10... | collective-permute-start | bytes 196616 | tf_op jit(solution)/shard_map/ppermute | solution.py:553
  72.4 1.2 %collective-permute-start.22 = (bf16[128,256]{1,0:T(8,128)(2,1)S(1)}, bf16[128,256]{1,0:T(8,128)(2,1)S(1)}, u32[]{:S(2)}, u32[]{:S(2)}) collective-permute-start(bf16[128,256]{1,0:T(8,128)(2,1)S(1)} %fusion.2.refs_2_), channel_id=1, source_target_pairs={{0,8},{8,0},{16,24},{24,16},{1,9},{9,1},{17,25},{25,17},{2,10},{10... | collective-permute-start | bytes 196616 | tf_op jit(solution)/shard_map/ppermute | solution.py:553
  74.2 0.9 %finished_mlp.1 = (f32[32,1024]{1,0:T(8,128)}, f32[1,32]{1,0:T(1,128)}, f32[128,256]{1,0:T(8,128)}) custom-call(bf16[32,1024]{1,0:T(8,128)(2,1)S(1)} %copy-done, bf16[1,32]{1,0:T(2,128)(2,1)S(1)} %bitcast.29, bf16[256,256]{1,0:T(8,128)(2,1)S(1)} %add_convert_fusion.2.refs_2_, bf16[256,256]{1,0:T(8,128)(2,1)S(1)} %collective-permute-done.25.refs_3_, ...), custom_call_target="tpu_custom_call" | custom-call | flops 1000000 | bytes 1048576 | tf_op jit(solution)/shard_map/finished_mlp/pallas_call | solution.py:296
  75.1 0.7 collective-permute-done.24.refs_5_
  76.7 0.8 %finished_attention.1 = (f32[32,768]{1,0:T(8,128)}, f32[1,32]{1,0:T(1,128)}, f32[32,256]{1,0:T(8,128)}) custom-call(bf16[32,768]{1,0:T(8,128)(2,1)S(1)} %copy-done.1, bf16[1,32]{1,0:T(2,128)(2,1)S(1)} %bitcast.27, bf16[128,256]{1,0:T(8,128)(2,1)S(1)} %fusion.2.refs_2_, bf16[128,256]{1,0:T(8,128)(2,1)S(1)} %collective-permute-done.22.refs_3_, ...), custom_call_target="tpu_custom_call" | custom-call | flops 1000000 | bytes 1048576 | tf_op jit(solution)/shard_map/finished_attention/pallas_call | solution.py:296
  (54 shorter events, 8.2 us)
Async XLA Ops:
  1.7 10.1 %collective-permute-start.3 = (bf16[32,768]{1,0:T(8,128)(2,1)S(1)}, bf16[32,768]{1,0:T(8,128)(2,1)S(1)}, u32[]{:S(2)}, u32[]{:S(2)}) collective-permute-start(bf16[32,768]{1,0:T(8,128)(2,1)S(1)} %get-tuple-element.53.refs_8_), channel_id=1, source_target_pairs={{0,6},{1,7},{2,4},{3,5},{4,2},{5,3},{6,0},{7,1},{8,14},{9,15},{10,... | collective-permute-start | bytes 147464 | tf_op jit(solution)/shard_map/ppermute | solution.py:553
  6.9 8.5 %collective-permute-start.2 = (bf16[32,768]{1,0:T(8,128)(2,1)S(1)}, bf16[32,768]{1,0:T(8,128)(2,1)S(1)}, u32[]{:S(2)}, u32[]{:S(2)}) collective-permute-start(bf16[32,768]{1,0:T(8,128)(2,1)S(1)} %get-tuple-element.53.refs_8_), channel_id=1, source_target_pairs={{0,4},{1,5},{2,6},{3,7},{4,0},{5,1},{6,2},{7,3},{8,12},{9,13},{10,... | collective-permute-start | bytes 147464 | tf_op jit(solution)/shard_map/ppermute | solution.py:553
  6.9 8.5 %collective-permute-start.1 = (bf16[32,768]{1,0:T(8,128)(2,1)S(1)}, bf16[32,768]{1,0:T(8,128)(2,1)S(1)}, u32[]{:S(2)}, u32[]{:S(2)}) collective-permute-start(bf16[32,768]{1,0:T(8,128)(2,1)S(1)} %get-tuple-element.53.refs_8_), channel_id=1, source_target_pairs={{0,2},{1,3},{2,0},{3,1},{4,6},{5,7},{6,4},{7,5},{8,10},{9,11},{10,... | collective-permute-start | bytes 147464 | tf_op jit(solution)/shard_map/ppermute | solution.py:553
  7.5 15.4 %collective-permute-start.10 = (bf16[288,256]{1,0:T(8,128)(2,1)S(1)}, bf16[288,256]{1,0:T(8,128)(2,1)S(1)}, u32[]{:S(2)}, u32[]{:S(2)}) collective-permute-start(bf16[288,256]{1,0:T(8,128)(2,1)S(1)} %get-tuple-element.62.refs_7_), channel_id=1, source_target_pairs={{0,2},{1,3},{2,0},{3,1},{4,6},{5,7},{6,4},{7,5},{8,10},{9,11},{10,... | collective-permute-start | bytes 442376 | tf_op jit(solution)/shard_map/ppermute | solution.py:553
  8.9 14.0 %collective-permute-start.9 = (bf16[288,256]{1,0:T(8,128)(2,1)S(1)}, bf16[288,256]{1,0:T(8,128)(2,1)S(1)}, u32[]{:S(2)}, u32[]{:S(2)}) collective-permute-start(bf16[288,256]{1,0:T(8,128)(2,1)S(1)} %get-tuple-element.62.refs_7_), channel_id=1, source_target_pairs={{0,4},{1,5},{2,6},{3,7},{4,0},{5,1},{6,2},{7,3},{8,12},{9,13},{10,... | collective-permute-start | bytes 442376 | tf_op jit(solution)/shard_map/ppermute | solution.py:553
  11.8 11.1 %collective-permute-start.8 = (bf16[288,256]{1,0:T(8,128)(2,1)S(1)}, bf16[288,256]{1,0:T(8,128)(2,1)S(1)}, u32[]{:S(2)}, u32[]{:S(2)}) collective-permute-start(bf16[288,256]{1,0:T(8,128)(2,1)S(1)} %get-tuple-element.62.refs_7_), channel_id=1, source_target_pairs={{0,6},{1,7},{2,4},{3,5},{4,2},{5,3},{6,0},{7,1},{8,14},{9,15},{10,... | collective-permute-start | bytes 442376 | tf_op jit(solution)/shard_map/ppermute | solution.py:553
  15.4 1.4 %collective-permute-start.4 = (bf16[32,768]{1,0:T(8,128)(2,1)S(1)}, bf16[32,768]{1,0:T(8,128)(2,1)S(1)}, u32[]{:S(2)}, u32[]{:S(2)}) collective-permute-start(bf16[32,768]{1,0:T(8,128)(2,1)S(1)} %collective-permute-done.1.refs_10_), channel_id=1, source_target_pairs={{0,1},{1,0},{2,3},{3,2},{4,5},{5,4},{6,7},{7,6},{8,9},{9,8},{10,11... | collective-permute-start | bytes 147464 | tf_op jit(solution)/shard_map/ppermute | solution.py:553
  17.8 6.0 %collective-permute-start.7 = (bf16[288,256]{1,0:T(8,128)(2,1)S(1)}, bf16[288,256]{1,0:T(8,128)(2,1)S(1)}, u32[]{:S(2)}, u32[]{:S(2)}) collective-permute-start(bf16[288,256]{1,0:T(8,128)(2,1)S(1)} %get-tuple-element.62.refs_7_), channel_id=1, source_target_pairs={{0,1},{1,0},{2,3},{3,2},{4,5},{5,4},{6,7},{7,6},{8,9},{9,8},{10,11... | collective-permute-start | bytes 442376 | tf_op jit(solution)/shard_map/ppermute | solution.py:553
  22.9 1.4 %collective-permute-start.11 = (bf16[288,256]{1,0:T(8,128)(2,1)S(1)}, bf16[288,256]{1,0:T(8,128)(2,1)S(1)}, u32[]{:S(2)}, u32[]{:S(2)}) collective-permute-start(bf16[288,256]{1,0:T(8,128)(2,1)S(1)} %collective-permute-done.10.refs_9_), channel_id=1, source_target_pairs={{0,1},{1,0},{2,3},{3,2},{4,5},{5,4},{6,7},{7,6},{8,9},{9,8},{10,11... | collective-permute-start | bytes 442376 | tf_op jit(solution)/shard_map/ppermute | solution.py:553
  23.5 1.4 %collective-permute-start.13 = (bf16[288,256]{1,0:T(8,128)(2,1)S(1)}, bf16[288,256]{1,0:T(8,128)(2,1)S(1)}, u32[]{:S(2)}, u32[]{:S(2)}) collective-permute-start(bf16[288,256]{1,0:T(8,128)(2,1)S(1)} %collective-permute-done.8.refs_13_), channel_id=1, source_target_pairs={{0,1},{1,0},{2,3},{3,2},{4,5},{5,4},{6,7},{7,6},{8,9},{9,8},{10,11... | collective-permute-start | bytes 442376 | tf_op jit(solution)/shard_map/ppermute | solution.py:553
  43.0 2.0 %collective-permute-start.14 = (bf16[4,256,256]{2,1,0:T(8,128)(2,1)S(1)}, bf16[4,256,256]{2,1,0:T(8,128)(2,1)S(1)}, u32[]{:S(2)}, u32[]{:S(2)}) collective-permute-start(bf16[4,256,256]{2,1,0:T(8,128)(2,1)S(1)} %get-tuple-element.82), channel_id=1, source_target_pairs={{0,1},{1,0},{2,3},{3,2},{4,5},{5,4},{6,7},{7,6},{8,9},{9,8},{10,11... | collective-permute-start | bytes 1572872 | tf_op jit(solution)/shard_map/ppermute | solution.py:553
  45.1 12.5 %collective-permute-start.18 = (bf16[256,256]{1,0:T(8,128)(2,1)S(1)}, bf16[256,256]{1,0:T(8,128)(2,1)S(1)}, u32[]{:S(2)}, u32[]{:S(2)}) collective-permute-start(bf16[256,256]{1,0:T(8,128)(2,1)S(1)} %get-tuple-element.93.refs_21_), channel_id=1, source_target_pairs={{0,6},{1,7},{2,4},{3,5},{4,2},{5,3},{6,0},{7,1},{8,14},{9,15},{10,... | collective-permute-start | bytes 393224 | tf_op jit(solution)/shard_map/ppermute | solution.py:553
  47.5 13.2 %collective-permute-start.17 = (bf16[256,256]{1,0:T(8,128)(2,1)S(1)}, bf16[256,256]{1,0:T(8,128)(2,1)S(1)}, u32[]{:S(2)}, u32[]{:S(2)}) collective-permute-start(bf16[256,256]{1,0:T(8,128)(2,1)S(1)} %get-tuple-element.94.refs_20_), channel_id=1, source_target_pairs={{0,4},{1,5},{2,6},{3,7},{4,0},{5,1},{6,2},{7,3},{8,12},{9,13},{10,... | collective-permute-start | bytes 393224 | tf_op jit(solution)/shard_map/ppermute | solution.py:553
  48.7 12.0 %collective-permute-start.16 = (bf16[256,256]{1,0:T(8,128)(2,1)S(1)}, bf16[256,256]{1,0:T(8,128)(2,1)S(1)}, u32[]{:S(2)}, u32[]{:S(2)}) collective-permute-start(bf16[256,256]{1,0:T(8,128)(2,1)S(1)} %get-tuple-element.95.refs_19_), channel_id=1, source_target_pairs={{0,2},{1,3},{2,0},{3,1},{4,6},{5,7},{6,4},{7,5},{8,10},{9,11},{10,... | collective-permute-start | bytes 393224 | tf_op jit(solution)/shard_map/ppermute | solution.py:553
  57.6 3.2 %collective-permute-start.15 = (bf16[4,128,256]{2,1,0:T(8,128)(2,1)S(1)}, bf16[4,128,256]{2,1,0:T(8,128)(2,1)S(1)}, u32[]{:S(2)}, u32[]{:S(2)}) collective-permute-start(bf16[4,128,256]{2,1,0:T(8,128)(2,1)S(1)} %get-tuple-element.86), channel_id=1, source_target_pairs={{0,1},{1,0},{2,3},{3,2},{4,5},{5,4},{6,7},{7,6},{8,9},{9,8},{10,11... | collective-permute-start | bytes 786440 | tf_op jit(solution)/shard_map/ppermute | solution.py:553
  60.9 7.5 %collective-permute-start.19 = (bf16[128,256]{1,0:T(8,128)(2,1)S(1)}, bf16[128,256]{1,0:T(8,128)(2,1)S(1)}, u32[]{:S(2)}, u32[]{:S(2)}) collective-permute-start(bf16[128,256]{1,0:T(8,128)(2,1)S(1)} %get-tuple-element.97), channel_id=1, source_target_pairs={{0,6},{1,7},{2,4},{3,5},{4,2},{5,3},{6,0},{7,1},{8,14},{9,15},{10,... | collective-permute-start | bytes 196616 | tf_op jit(solution)/shard_map/ppermute | solution.py:553
  63.2 6.0 %collective-permute-start.21 = (bf16[128,256]{1,0:T(8,128)(2,1)S(1)}, bf16[128,256]{1,0:T(8,128)(2,1)S(1)}, u32[]{:S(2)}, u32[]{:S(2)}) collective-permute-start(bf16[128,256]{1,0:T(8,128)(2,1)S(1)} %get-tuple-element.98), channel_id=1, source_target_pairs={{0,2},{1,3},{2,0},{3,1},{4,6},{5,7},{6,4},{7,5},{8,10},{9,11},{10,... | collective-permute-start | bytes 196616 | tf_op jit(solution)/shard_map/ppermute | solution.py:553
  63.2 6.0 %collective-permute-start.20 = (bf16[128,256]{1,0:T(8,128)(2,1)S(1)}, bf16[128,256]{1,0:T(8,128)(2,1)S(1)}, u32[]{:S(2)}, u32[]{:S(2)}) collective-permute-start(bf16[128,256]{1,0:T(8,128)(2,1)S(1)} %get-tuple-element.99), channel_id=1, source_target_pairs={{0,4},{1,5},{2,6},{3,7},{4,0},{5,1},{6,2},{7,3},{8,12},{9,13},{10,... | collective-permute-start | bytes 196616 | tf_op jit(solution)/shard_map/ppermute | solution.py:553
  65.4 7.0 %collective-permute-start.27 = (bf16[256,256]{1,0:T(8,128)(2,1)S(1)}, bf16[256,256]{1,0:T(8,128)(2,1)S(1)}, u32[]{:S(2)}, u32[]{:S(2)}) collective-permute-start(bf16[256,256]{1,0:T(8,128)(2,1)S(1)} %add_convert_fusion.2.refs_2_), channel_id=1, source_target_pairs={{0,24},{8,16},{16,8},{24,0},{1,25},{9,17},{17,9},{25,1},{2,26},{10... | collective-permute-start | bytes 393224 | tf_op jit(solution)/shard_map/ppermute | solution.py:553
  67.9 6.1 %collective-permute-start.26 = (bf16[256,256]{1,0:T(8,128)(2,1)S(1)}, bf16[256,256]{1,0:T(8,128)(2,1)S(1)}, u32[]{:S(2)}, u32[]{:S(2)}) collective-permute-start(bf16[256,256]{1,0:T(8,128)(2,1)S(1)} %add_convert_fusion.2.refs_2_), channel_id=1, source_target_pairs={{0,16},{8,24},{16,0},{24,8},{1,17},{9,25},{17,1},{25,9},{2,18},{10... | collective-permute-start | bytes 393224 | tf_op jit(solution)/shard_map/ppermute | solution.py:553
  68.4 5.8 %collective-permute-start.25 = (bf16[256,256]{1,0:T(8,128)(2,1)S(1)}, bf16[256,256]{1,0:T(8,128)(2,1)S(1)}, u32[]{:S(2)}, u32[]{:S(2)}) collective-permute-start(bf16[256,256]{1,0:T(8,128)(2,1)S(1)} %add_convert_fusion.2.refs_2_), channel_id=1, source_target_pairs={{0,8},{8,0},{16,24},{24,16},{1,9},{9,1},{17,25},{25,17},{2,10},{10... | collective-permute-start | bytes 393224 | tf_op jit(solution)/shard_map/ppermute | solution.py:553
  69.3 6.5 %collective-permute-start.24 = (bf16[128,256]{1,0:T(8,128)(2,1)S(1)}, bf16[128,256]{1,0:T(8,128)(2,1)S(1)}, u32[]{:S(2)}, u32[]{:S(2)}) collective-permute-start(bf16[128,256]{1,0:T(8,128)(2,1)S(1)} %fusion.2.refs_2_), channel_id=1, source_target_pairs={{0,24},{8,16},{16,8},{24,0},{1,25},{9,17},{17,9},{25,1},{2,26},{10... | collective-permute-start | bytes 196616 | tf_op jit(solution)/shard_map/ppermute | solution.py:553
  71.8 4.4 %collective-permute-start.23 = (bf16[128,256]{1,0:T(8,128)(2,1)S(1)}, bf16[128,256]{1,0:T(8,128)(2,1)S(1)}, u32[]{:S(2)}, u32[]{:S(2)}) collective-permute-start(bf16[128,256]{1,0:T(8,128)(2,1)S(1)} %fusion.2.refs_2_), channel_id=1, source_target_pairs={{0,16},{8,24},{16,0},{24,8},{1,17},{9,25},{17,1},{25,9},{2,18},{10... | collective-permute-start | bytes 196616 | tf_op jit(solution)/shard_map/ppermute | solution.py:553
  72.4 4.3 %collective-permute-start.22 = (bf16[128,256]{1,0:T(8,128)(2,1)S(1)}, bf16[128,256]{1,0:T(8,128)(2,1)S(1)}, u32[]{:S(2)}, u32[]{:S(2)}) collective-permute-start(bf16[128,256]{1,0:T(8,128)(2,1)S(1)} %fusion.2.refs_2_), channel_id=1, source_target_pairs={{0,8},{8,0},{16,24},{24,16},{1,9},{9,1},{17,25},{25,17},{2,10},{10... | collective-permute-start | bytes 196616 | tf_op jit(solution)/shard_map/ppermute | solution.py:553
  (8 other events, 108.5 us)
